TPU v7x, 32 devices: a whole 2x2x4 slice. The times are simulated.
32 devices in a mesh: row: 4 (over y, core), col: 8 (over z, x).
Axes of the slice: x: 2, y: 2, z: 4, core: 2. Of those that a mesh axis runs over, the one named last changes fastest.
Arguments:
- queries: bfloat16 [8, 8, 128, 2048], P('row', 'col'), may hold values from -70 to 70
- fine_keys: bfloat16 [8, 8, 128, 2048], P('row', 'col'), may hold values from -4 to 4
- fine_values: bfloat16 [8, 8, 128, 2048], P('row', 'col'), may hold values from -6 to 6
- keep_flags: int32 [8, 8, 9], P('row', 'col'), may hold values 0 or 1
- coarse_keys: bfloat16 [1024, 2048], P('col'), may hold values from -6 to 6
- coarse_values: bfloat16 [1024, 2048], P('col'), may hold values from -6 to 6
Outputs:
- attended: bfloat16 [8, 8, 128, 2048], P('row', 'col')
All inputs are finite; a program needn't handle non-finite values. No bound on the sum of `keep_flags` on one device may be relied on, other than what follows from the above.
Results may differ from a plain program's by a relative error of at most 0.0035.
Values may be sent and summed in bfloat16 or wider, within the bound.
No kernel may reach another device: no remote copies, remote signals or barrier semaphores. Data moves between devices by JAX's collectives and lax.ppermute only.
A program may use at most 128 MiB of HBM per device.

v0:
```python
import jax
import jax.numpy as jnp
from jax import lax
from jax.sharding import PartitionSpec as P

HEADS = 16
HEAD_DIM = 128


def padded_2(cells, sides, width):
    for axis, dim in sides:
        count = lax.axis_size(axis)
        ends = count - 1
        head = lax.slice_in_dim(cells, 0, width, axis=dim)
        tail = lax.slice_in_dim(cells, cells.shape[dim] - width, cells.shape[dim], axis=dim)
        cells = jnp.concatenate(
            [
                lax.ppermute(tail, axis, [(i, (i + 1) % count) for i in range(ends)]),
                cells,
                lax.ppermute(head, axis, [((i + 1) % count, i) for i in range(ends)]),
            ],
            axis=dim,
        )
    return cells


def body(queries, fine_keys, fine_values, keep_flags, coarse_keys, coarse_values):
    rows_tiles, cols_tiles, tile_len, model_width = queries.shape
    tile_count = rows_tiles * cols_tiles
    scale = HEAD_DIM ** (-0.5)
    stacked = jnp.stack((fine_keys, fine_values), 0)
    padded = padded_2(stacked, (("row", 1), ("col", 2)), 1)
    far_keys, far_values = (
        lax.all_gather(coarse_keys, "col", axis=0, tiled=True),
        lax.all_gather(coarse_values, "col", axis=0, tiled=True),
    )
    row_base = lax.axis_index("row") * rows_tiles
    col_base = lax.axis_index("col") * cols_tiles
    rows_total = rows_tiles * lax.axis_size("row")
    cols_total = cols_tiles * lax.axis_size("col")
    windows = []
    usable = []
    for tile_row in range(rows_tiles):
        pieces = []
        kept_list = []
        for row_step in range(3):
            for col_step in range(3):
                pieces.append(padded[:, tile_row + row_step, col_step])
                grid_row = row_base + tile_row + row_step - 1
                grid_col = col_base + 0 + col_step - 1
                inside = (
                    (grid_row >= 0)
                    & (grid_row < rows_total)
                    & (grid_col >= 0)
                    & (grid_col < cols_total)
                )
                kept_here = (keep_flags[tile_row, 0, row_step * 3 + col_step] > 0) | (
                    row_step == 1 and col_step == 1
                )
                kept_list.append(inside & kept_here)
        windows.append(jnp.concatenate(pieces, axis=1))
        usable.append(jnp.stack(kept_list))
    window_kv = jnp.stack(windows, 1)
    window_ok = jnp.repeat(jnp.stack(usable), tile_len, axis=1)
    query_flat = queries.reshape(tile_count, tile_len, model_width)

    def one_head(head):
        begin_at = head * HEAD_DIM
        query_head = lax.dynamic_slice_in_dim(query_flat, begin_at, HEAD_DIM, 2)
        near_keys = lax.dynamic_slice_in_dim(window_kv[0], begin_at, HEAD_DIM, 2)
        near_values = lax.dynamic_slice_in_dim(window_kv[1], begin_at, HEAD_DIM, 2)
        far_key_head = lax.dynamic_slice_in_dim(far_keys, begin_at, HEAD_DIM, 1)
        far_value_head = lax.dynamic_slice_in_dim(far_values, begin_at, HEAD_DIM, 1)
        near_scores = (
            jnp.einsum("tqd,tkd->tqk", query_head, near_keys, preferred_element_type=jnp.float32)
            * scale
        )
        near_scores = jnp.where(window_ok[:, None, :], near_scores, -jnp.inf)
        far_scores = (
            jnp.einsum("tqd,kd->tqk", query_head, far_key_head, preferred_element_type=jnp.float32)
            * scale
        )
        largest = jnp.maximum(jnp.max(near_scores, -1), jnp.max(far_scores, -1))[..., None]
        near_probs = jnp.exp(near_scores - largest)
        far_probs = jnp.exp(far_scores - largest)
        total = jnp.sum(near_probs, -1) + jnp.sum(far_probs, -1)
        mixed = jnp.einsum(
            "tqk,tkd->tqd",
            near_probs.astype(jnp.bfloat16),
            near_values,
            preferred_element_type=jnp.float32,
        )
        mixed = mixed + jnp.einsum(
            "tqk,kd->tqd",
            far_probs.astype(jnp.bfloat16),
            far_value_head,
            preferred_element_type=jnp.float32,
        )
        return mixed / total[..., None]

    result = lax.map(one_head, jnp.arange(HEADS))
    result = jnp.transpose(result, (1, 2, 0, 3)).reshape(
        rows_tiles, cols_tiles, tile_len, model_width
    )
    return result.astype(jnp.bfloat16)


def solution(mesh):
    placed = (
        P("row", "col", None, None),
        P("row", "col", None, None),
        P("row", "col", None, None),
        P("row", "col", None),
        P("col", None),
        P("col", None),
    )
    return jax.shard_map(
        body, mesh=mesh, in_specs=placed, out_specs=P("row", "col", None, None), check_vma=False
    )
```

profile of v0, /device:TPU:8, one launch (start us, length us, event | category | flops | bytes accessed | tf_op | source)
XLA Modules:
  0.0 515.5 jit_solution(2279782534609030921)
XLA Ops:
  7.3 1.7 fusion.29
  9.0 1.8 collective-permute-start
  13.0 3.6 collective-permute-done.1
  16.6 3.5 pad_maximum_fusion.1
  20.1 3.4 collective-permute-start.2
  23.5 3.3 collective-permute-start.3
  38.1 185.5 %collective-permute-done.2 = bf16[2,4,1,128,2048]{4,3,0,2,1:T(8,128)(2,1)} collective-permute-done((bf16[2,4,1,128,2048]{4,3,0,2,1:T(8,128)(2,1)}, bf16[2,4,1,128,2048]{4,3,0,2,1:T(8,128)(2,1)}, u32[]{:S(2)}, u32[]{:S(2)}) %collective-permute-start.2) | collective-permute-done | bytes 4194336 | tf_op jit(solution)/shard_map/ppermute | solution.py:18
  226.1 3.0 collective-permute-done.3
  230.4 1.5 fusion.35
  232.2 1.6 fusion.37
  233.8 1.5 fusion.39
  235.6 1.5 fusion.41
  238.5 1.3 fusion.30
  239.9 7.7 %pad_maximum_fusion = bf16[2,2,1152,2048]{3,2,1,0:T(8,128)(2,1)} fusion(bf16[2,1,1152,2048]{3,2,1,0:T(8,128)(2,1)S(1)} %bitcast.140, bf16[2,1,1152,2048]{3,2,1,0:T(8,128)(2,1)S(1)} %bitcast.141), kind=kLoop, calls=%fused_computation.33 | loop fusion | flops 9437184 | bytes 37748736 | tf_op jit(solution)/shard_map/stack | solution.py:63
  247.5 26.2 %all-gather.5.cloned.1.call-done = bf16[1024,2048]{1,0:T(8,128)(2,1)} async-done(((bf16[128,2048]{1,0:T(8,128)(2,1)}), bf16[1024,2048]{1,0:T(8,128)(2,1)}) %all-gather.5.cloned.1.call-update) | async-done | bytes 4194320 | tf_op jit(solution)/shard_map/all_gather | solution.py:35
  273.8 233.0 %while.11 = (s32[]{:T(128)}, bf16[16,2,128,128]{3,2,1,0:T(8,128)(2,1)S(1)}, s32[16]{0:T(128)S(1)}, bf16[2,128,2048]{2,1,0:T(8,128)(2,1)}, bf16[2,2,1152,2048]{3,...) while((s32[]{:T(128)}, ...), condition=%wide.region_5.6_spmd.clone, body=%wide.region_0.5_spmd.clone.sunk | while | flops 288914944 | bytes 46691272 | solution.py:101
  275.0 8.1 %fusion.61 = (bf16[1,2,1152,2048]{3,2,1,0:T(8,128)(2,1)S(1)}, bf16[1,2,1152,2048]{3,2,1,0:T(8,128)(2,1)S(1)}) fusion(bf16[2,2,1152,2048]{3,2,1,0:T(8,128)(2,1)} %get-tuple-element.208), kind=kLoop, calls=%fused_computation.67.clone.1 | loop fusion | bytes 37748736 | tf_op jit(solution)/shard_map/while/body/eval_jaxpr/slice | solution.py:71
  284.5 1.4 fusion.63
  287.0 1.3 fusion.67
  289.6 8.1 %fusion.61 = (bf16[1,2,1152,2048]{3,2,1,0:T(8,128)(2,1)S(1)}, bf16[1,2,1152,2048]{3,2,1,0:T(8,128)(2,1)S(1)}) fusion(bf16[2,2,1152,2048]{3,2,1,0:T(8,128)(2,1)} %get-tuple-element.208), kind=kLoop, calls=%fused_computation.67.clone.1 | loop fusion | bytes 37748736 | tf_op jit(solution)/shard_map/while/body/eval_jaxpr/slice | solution.py:71
  299.1 1.4 fusion.63
  301.5 1.3 fusion.67
  304.1 8.1 %fusion.61 = (bf16[1,2,1152,2048]{3,2,1,0:T(8,128)(2,1)S(1)}, bf16[1,2,1152,2048]{3,2,1,0:T(8,128)(2,1)S(1)}) fusion(bf16[2,2,1152,2048]{3,2,1,0:T(8,128)(2,1)} %get-tuple-element.208), kind=kLoop, calls=%fused_computation.67.clone.1 | loop fusion | bytes 37748736 | tf_op jit(solution)/shard_map/while/body/eval_jaxpr/slice | solution.py:71
  313.6 1.4 fusion.63
  316.1 1.3 fusion.67
  318.7 8.1 %fusion.61 = (bf16[1,2,1152,2048]{3,2,1,0:T(8,128)(2,1)S(1)}, bf16[1,2,1152,2048]{3,2,1,0:T(8,128)(2,1)S(1)}) fusion(bf16[2,2,1152,2048]{3,2,1,0:T(8,128)(2,1)} %get-tuple-element.208), kind=kLoop, calls=%fused_computation.67.clone.1 | loop fusion | bytes 37748736 | tf_op jit(solution)/shard_map/while/body/eval_jaxpr/slice | solution.py:71
  328.2 1.4 fusion.63
  330.6 1.3 fusion.67
  333.2 8.1 %fusion.61 = (bf16[1,2,1152,2048]{3,2,1,0:T(8,128)(2,1)S(1)}, bf16[1,2,1152,2048]{3,2,1,0:T(8,128)(2,1)S(1)}) fusion(bf16[2,2,1152,2048]{3,2,1,0:T(8,128)(2,1)} %get-tuple-element.208), kind=kLoop, calls=%fused_computation.67.clone.1 | loop fusion | bytes 37748736 | tf_op jit(solution)/shard_map/while/body/eval_jaxpr/slice | solution.py:71
  342.8 1.4 fusion.63
  345.2 1.3 fusion.67
  347.8 8.1 %fusion.61 = (bf16[1,2,1152,2048]{3,2,1,0:T(8,128)(2,1)S(1)}, bf16[1,2,1152,2048]{3,2,1,0:T(8,128)(2,1)S(1)}) fusion(bf16[2,2,1152,2048]{3,2,1,0:T(8,128)(2,1)} %get-tuple-element.208), kind=kLoop, calls=%fused_computation.67.clone.1 | loop fusion | bytes 37748736 | tf_op jit(solution)/shard_map/while/body/eval_jaxpr/slice | solution.py:71
  357.3 1.4 fusion.63
  359.8 1.3 fusion.67
  362.4 8.1 %fusion.61 = (bf16[1,2,1152,2048]{3,2,1,0:T(8,128)(2,1)S(1)}, bf16[1,2,1152,2048]{3,2,1,0:T(8,128)(2,1)S(1)}) fusion(bf16[2,2,1152,2048]{3,2,1,0:T(8,128)(2,1)} %get-tuple-element.208), kind=kLoop, calls=%fused_computation.67.clone.1 | loop fusion | bytes 37748736 | tf_op jit(solution)/shard_map/while/body/eval_jaxpr/slice | solution.py:71
  371.9 1.4 fusion.63
  374.4 1.3 fusion.67
  377.0 8.1 %fusion.61 = (bf16[1,2,1152,2048]{3,2,1,0:T(8,128)(2,1)S(1)}, bf16[1,2,1152,2048]{3,2,1,0:T(8,128)(2,1)S(1)}) fusion(bf16[2,2,1152,2048]{3,2,1,0:T(8,128)(2,1)} %get-tuple-element.208), kind=kLoop, calls=%fused_computation.67.clone.1 | loop fusion | bytes 37748736 | tf_op jit(solution)/shard_map/while/body/eval_jaxpr/slice | solution.py:71
  386.5 1.4 fusion.63
  388.9 1.3 fusion.67
  391.5 8.1 %fusion.61 = (bf16[1,2,1152,2048]{3,2,1,0:T(8,128)(2,1)S(1)}, bf16[1,2,1152,2048]{3,2,1,0:T(8,128)(2,1)S(1)}) fusion(bf16[2,2,1152,2048]{3,2,1,0:T(8,128)(2,1)} %get-tuple-element.208), kind=kLoop, calls=%fused_computation.67.clone.1 | loop fusion | bytes 37748736 | tf_op jit(solution)/shard_map/while/body/eval_jaxpr/slice | solution.py:71
  401.0 1.4 fusion.63
  403.5 1.3 fusion.67
  406.1 8.1 %fusion.61 = (bf16[1,2,1152,2048]{3,2,1,0:T(8,128)(2,1)S(1)}, bf16[1,2,1152,2048]{3,2,1,0:T(8,128)(2,1)S(1)}) fusion(bf16[2,2,1152,2048]{3,2,1,0:T(8,128)(2,1)} %get-tuple-element.208), kind=kLoop, calls=%fused_computation.67.clone.1 | loop fusion | bytes 37748736 | tf_op jit(solution)/shard_map/while/body/eval_jaxpr/slice | solution.py:71
  415.6 1.4 fusion.63
  418.0 1.3 fusion.67
  420.6 8.1 %fusion.61 = (bf16[1,2,1152,2048]{3,2,1,0:T(8,128)(2,1)S(1)}, bf16[1,2,1152,2048]{3,2,1,0:T(8,128)(2,1)S(1)}) fusion(bf16[2,2,1152,2048]{3,2,1,0:T(8,128)(2,1)} %get-tuple-element.208), kind=kLoop, calls=%fused_computation.67.clone.1 | loop fusion | bytes 37748736 | tf_op jit(solution)/shard_map/while/body/eval_jaxpr/slice | solution.py:71
  430.1 1.4 fusion.63
  432.6 1.3 fusion.67
  435.2 8.1 %fusion.61 = (bf16[1,2,1152,2048]{3,2,1,0:T(8,128)(2,1)S(1)}, bf16[1,2,1152,2048]{3,2,1,0:T(8,128)(2,1)S(1)}) fusion(bf16[2,2,1152,2048]{3,2,1,0:T(8,128)(2,1)} %get-tuple-element.208), kind=kLoop, calls=%fused_computation.67.clone.1 | loop fusion | bytes 37748736 | tf_op jit(solution)/shard_map/while/body/eval_jaxpr/slice | solution.py:71
  444.7 1.4 fusion.63
  447.1 1.3 fusion.67
  449.7 8.1 %fusion.61 = (bf16[1,2,1152,2048]{3,2,1,0:T(8,128)(2,1)S(1)}, bf16[1,2,1152,2048]{3,2,1,0:T(8,128)(2,1)S(1)}) fusion(bf16[2,2,1152,2048]{3,2,1,0:T(8,128)(2,1)} %get-tuple-element.208), kind=kLoop, calls=%fused_computation.67.clone.1 | loop fusion | bytes 37748736 | tf_op jit(solution)/shard_map/while/body/eval_jaxpr/slice | solution.py:71
  459.2 1.4 fusion.63
  461.7 1.3 fusion.67
  464.3 8.1 %fusion.61 = (bf16[1,2,1152,2048]{3,2,1,0:T(8,128)(2,1)S(1)}, bf16[1,2,1152,2048]{3,2,1,0:T(8,128)(2,1)S(1)}) fusion(bf16[2,2,1152,2048]{3,2,1,0:T(8,128)(2,1)} %get-tuple-element.208), kind=kLoop, calls=%fused_computation.67.clone.1 | loop fusion | bytes 37748736 | tf_op jit(solution)/shard_map/while/body/eval_jaxpr/slice | solution.py:71
  473.8 1.4 fusion.63
  476.3 1.3 fusion.67
  478.9 8.1 %fusion.61 = (bf16[1,2,1152,2048]{3,2,1,0:T(8,128)(2,1)S(1)}, bf16[1,2,1152,2048]{3,2,1,0:T(8,128)(2,1)S(1)}) fusion(bf16[2,2,1152,2048]{3,2,1,0:T(8,128)(2,1)} %get-tuple-element.208), kind=kLoop, calls=%fused_computation.67.clone.1 | loop fusion | bytes 37748736 | tf_op jit(solution)/shard_map/while/body/eval_jaxpr/slice | solution.py:71
  488.4 1.4 fusion.63
  490.8 1.3 fusion.67
  493.4 8.1 %fusion.61 = (bf16[1,2,1152,2048]{3,2,1,0:T(8,128)(2,1)S(1)}, bf16[1,2,1152,2048]{3,2,1,0:T(8,128)(2,1)S(1)}) fusion(bf16[2,2,1152,2048]{3,2,1,0:T(8,128)(2,1)} %get-tuple-element.208), kind=kLoop, calls=%fused_computation.67.clone.1 | loop fusion | bytes 37748736 | tf_op jit(solution)/shard_map/while/body/eval_jaxpr/slice | solution.py:71
  502.9 1.4 fusion.63
  505.4 1.3 fusion.67
  (172 shorter events, 59.8 us)
Async XLA Ops:
  6.5 20.4 %copy-start.2 = (s32[2,1,9]{2,1,0:T(1,128)S(1)}, s32[2,1,9]{2,1,0:T(1,128)}, u32[]{:S(2)}) copy-start(s32[2,1,9]{2,1,0:T(1,128)} %param.11) | copy-start | bytes 220
  6.5 241.0 %all-gather.3.cloned.1.call-start = ((), (), s32[]{:S(2)}) async-start(), calls=%async_computation | async-start | bytes 4718592 | tf_op jit(solution)/shard_map/all_gather | solution.py:34
  7.3 266.5 %all-gather.5.cloned.1.call-start = ((), (), s32[]{:S(2)}) async-start(), calls=%async_computation.1 | async-start | bytes 4718592 | tf_op jit(solution)/shard_map/all_gather | solution.py:35
  9.0 4.0 collective-permute-start
  10.8 5.8 %collective-permute-start.1 = (bf16[2,1,1,128,2048]{4,3,0,2,1:T(8,128)(2,1)S(1)}, bf16[2,1,1,128,2048]{4,3,0,2,1:T(8,128)(2,1)S(1)}, u32[]{:S(2)}, u32[]{:S(2)}) collective-permute-start(bf16[2,1,1,128,2048]{4,3,0,2,1:T(8,128)(2,1)S(1)} %get-tuple-element.98), channel_id=1, source_target_pairs={{8,0},{16,8},{24,16},{9,1},{17,9},{25,17},{10,2},{18,10},{26,18},{... | collective-permute-start | bytes 3145736 | tf_op jit(solution)/shard_map/ppermute | solution.py:20
  13.0 3.6 copy-start
  20.1 203.4 %collective-permute-start.2 = (bf16[2,4,1,128,2048]{4,3,0,2,1:T(8,128)(2,1)}, bf16[2,4,1,128,2048]{4,3,0,2,1:T(8,128)(2,1)}, u32[]{:S(2)}, u32[]{:S(2)}) collective-permute-start(bf16[2,4,1,128,2048]{4,3,0,2,1:T(8,128)(2,1)} %pad_maximum_fusion.1), channel_id=1, source_target_pairs={{0,1},{1,2},{2,3},{3,4},{4,5},{5,6},{6,7},{8,9},{9,10},{10,11},{11... | collective-permute-start | bytes 12582920 | tf_op jit(solution)/shard_map/ppermute | solution.py:18
  23.5 205.6 %collective-permute-start.3 = (bf16[2,4,1,128,2048]{4,3,0,2,1:T(8,128)(2,1)}, bf16[2,4,1,128,2048]{4,3,0,2,1:T(8,128)(2,1)}, u32[]{:S(2)}, u32[]{:S(2)}) collective-permute-start(bf16[2,4,1,128,2048]{4,3,0,2,1:T(8,128)(2,1)} %pad_maximum_fusion.1), channel_id=1, source_target_pairs={{1,0},{2,1},{3,2},{4,3},{5,4},{6,5},{7,6},{9,8},{10,9},{11,10},{12... | collective-permute-start | bytes 12582920 | tf_op jit(solution)/shard_map/ppermute | solution.py:20
  239.8 33.9 %copy-start.1 = (bf16[16,2,128,128]{3,2,1,0:T(8,128)(2,1)S(1)}, bf16[16,2,128,128]{3,2,1,0:T(8,128)(2,1)}, u32[]{:S(2)}) copy-start(bf16[16,2,128,128]{3,2,1,0:T(8,128)(2,1)} %custom-call.2) | copy-start | bytes 3145732
Sparse Core Ops, SparseCore 0:
  9.5 178.5 all-gather.2
  190.2 83.5 all-gather.4
where the time goes:
time: 520 us; the launch traced here: 516 us
  waiting for transfers between devices  220 us (42%)
  local copies, waits for them, and re-layouts  157 us (30%)
  matrix products  70.7 us (14%)
  between operations  23.8 us (5%)
  other arithmetic  23.1 us (4%)
  loops' own time  11.2 us (2%)
  starting transfers between devices  9.87 us (2%)
    ppermute x2, waiting for transfers between devices, padded_2(): lax.ppermute(tail, axis, [(i, (i + 1) % count) for i in range(ends)])  186 us
    slice x16, local copies, waits for them, and re-layouts, one_head(): near_values = lax.dynamic_slice_in_dim(window_kv[1], begin_at, HEAD_DIM, 2)  130 us
    all_gather x1, waiting for transfers between devices, body(): lax.all_gather(coarse_values, 'col', axis=0, tiled=True)  26.2 us
    dot_general x16, matrix products, one_head(): jnp.einsum('tqd,kd->tqk', query_head, far_key_head, preferred_element_typ...  22 us
    dot_general x16, matrix products, one_head(): jnp.einsum('tqk,kd->tqd', far_probs.astype(jnp.bfloat16), far_value_head,...  21.5 us
    dot_general x16, matrix products, one_head(): jnp.einsum('tqd,tkd->tqk', query_head, near_keys, preferred_element_type=...  20.5 us
    another operation x1, loops' own time, body(): result = lax.map(one_head, jnp.arange(HEADS))  11.2 us
    unnamed x16, local copies, waits for them, and re-layouts  10.4 us
  transfers between devices with their start and end apart: 6, of which 5 were waited for; matrix products, arithmetic and copies ran while one was open for 5% of the time, Pallas kernels for 0%

commit v1 on v0

v1 whole, which is shorter than its diff:
```python
import functools

import jax
import jax.numpy as jnp
from jax import lax
from jax.experimental import pallas as pl
from jax.experimental.pallas import tpu as pltpu
from jax.sharding import PartitionSpec as P

HEADS = 16
HEAD_DIM = 128
LOG2_SCALE = HEAD_DIM ** (-0.5) * 1.4426950408889634


def attend(
    pad,
    ok_ref,
    q_ref,
    own_ref,
    left_ref,
    right_ref,
    far_ref,
    out_ref,
):
    bands = q_ref.shape[1]
    rows_in_band = q_ref.shape[2]
    rows = bands * rows_in_band
    key_rows = own_ref.shape[1] * rows_in_band
    tile = q_ref.shape[3]

    def one_row(i, carry):
        band, sub = i // rows_in_band, i % rows_in_band
        q0 = q_ref[0, band, sub]
        q1 = q_ref[1, band, sub]
        qq = jnp.concatenate([q0, q1], axis=0)
        nt = (((1,), (1,)), ((), ()))

        def scores(a, b):
            return lax.dot_general(a, b, nt, preferred_element_type=jnp.float32)

        far = [
            scores(qq, far_ref[c, 0]) for c in range(far_ref.shape[0])
        ]
        parts = [[], []]
        for c, s in enumerate(far):
            parts[0].append((s[:tile], None, (2, c, 0)))
            parts[1].append((s[tile:], None, (2, c, 0)))
        for a in range(3):
            j = jnp.clip(i + pad + a - 1, 0, key_rows - 1)
            kb, ks = j // rows_in_band, j % rows_in_band
            for x in range(2):
                s = scores(qq, own_ref[x, kb, 0, ks])
                for xq in range(2):
                    flag = ok_ref[(i * 2 + xq) * 9 + a * 3 + 1 + x - xq]
                    parts[xq].append((s[xq * tile : (xq + 1) * tile], flag, (x, kb, ks)))
            s = scores(q0, left_ref[kb, 0, ks])
            parts[0].append((s, ok_ref[(i * 2 + 0) * 9 + a * 3], (3, kb, ks)))
            s = scores(q1, right_ref[kb, 0, ks])
            parts[1].append((s, ok_ref[(i * 2 + 1) * 9 + a * 3 + 2], (4, kb, ks)))
        for xq in range(2):
            tiles = [
                s if flag is None else jnp.where(flag > 0, s, -jnp.inf)
                for s, flag, _ in parts[xq]
            ]
            biggest = functools.reduce(jnp.maximum, tiles)
            m = jnp.max(biggest, axis=1, keepdims=True)
            total = None
            acc = None
            for s, (_, _, (kind, u, w)) in zip(tiles, parts[xq]):
                p = jnp.exp2((s - m) * LOG2_SCALE)
                total = p if total is None else total + p
                if kind == 2:
                    v = far_ref[u, 1]
                elif kind == 3:
                    v = left_ref[u, 1, w]
                elif kind == 4:
                    v = right_ref[u, 1, w]
                else:
                    v = own_ref[kind, u, 1, w]
                o = jnp.dot(p.astype(jnp.bfloat16), v, preferred_element_type=jnp.float32)
                acc = o if acc is None else acc + o
            total = jnp.sum(total, axis=1, keepdims=True)
            out_ref[xq, band, sub] = (acc / total).astype(out_ref.dtype)
        return carry

    lax.fori_loop(0, rows, one_row, 0)


def attention(ok, q, own, left, right, far, pad):
    heads = q.shape[-1] // HEAD_DIM

    def spec(a):
        lead = a.shape[:-1]
        return pl.BlockSpec(lead + (HEAD_DIM,), lambda h, s, n=len(lead): (0,) * n + (h,))

    flops = 4 * 2 * q.shape[1] * q.shape[2] * 128 * 128 * 17 * 128 * heads
    return pl.pallas_call(
        functools.partial(attend, pad),
        grid_spec=pltpu.PrefetchScalarGridSpec(
            num_scalar_prefetch=1,
            grid=(heads,),
            in_specs=[spec(a) for a in (q, own, left, right, far)],
            out_specs=spec(q),
        ),
        out_shape=jax.ShapeDtypeStruct(q.shape, q.dtype),
        compiler_params=pltpu.CompilerParams(vmem_limit_bytes=56 * 1024 * 1024),
        cost_estimate=pl.CostEstimate(
            flops=flops, bytes_accessed=8 * 1024 * 1024, transcendentals=flops // 512
        ),
        name="attend",
    )(ok, q, own, left, right, far)


def moves(count, step):
    return [(i, i + step) for i in range(count) if 0 <= i + step < count]


def body(queries, fine_keys, fine_values, keep_flags, coarse_keys, coarse_values):
    rows_tiles, _, tile, width = queries.shape
    nrow, ncol = lax.axis_size("row"), lax.axis_size("col")
    band = min(4, nrow)
    planes = ncol // 2
    parts = band * 2
    part = width // parts
    row_at, col_at = lax.axis_index("row"), lax.axis_index("col")
    axes = ("row", "col")
    groups = [
        [(g * band + r) * ncol + 2 * z + x for x in range(2) for r in range(band)]
        for g in range(nrow // band)
        for z in range(planes)
    ]

    def by_part(a):
        return jnp.moveaxis(a.reshape(a.shape[:-1] + (parts, part)), -2, 0)

    def exchange(a):
        return lax.all_to_all(a, axes, 0, 0, axis_index_groups=groups, tiled=True)

    kv = jnp.stack([by_part(fine_keys[:, 0]), by_part(fine_values[:, 0])], 1)
    own = exchange(kv).reshape(2, band, 2, rows_tiles, tile, part)
    q = exchange(by_part(queries[:, 0])).reshape(2, band, rows_tiles, tile, part)
    flags = lax.all_gather(keep_flags, axes, axis=0, axis_index_groups=groups)
    flags = flags.reshape(2, band * rows_tiles, 9)

    left = lax.ppermute(own[1], "col", moves(ncol, 2))
    right = lax.ppermute(own[0], "col", moves(ncol, -2))

    mine = jnp.stack([by_part(coarse_keys), by_part(coarse_values)], 1)
    mine = mine.reshape((2, band) + mine.shape[1:])
    mine = lax.dynamic_index_in_dim(mine, row_at % band, 1, keepdims=False)
    far = jnp.concatenate([mine] * planes, 0)
    far = lax.all_to_all(far, "col", 0, 0, tiled=True)

    pad = 0
    if nrow > band:
        pad = 1

        def widen(a):
            line = jnp.moveaxis(a, 1, 0)
            line = line.reshape((2, band * rows_tiles) + line.shape[3:])
            above = lax.ppermute(line[:, -1:], "row", moves(nrow, band))
            below = lax.ppermute(line[:, :1], "row", moves(nrow, -band))
            extra = [line[:, :1]] * ((-2) % rows_tiles)
            line = jnp.concatenate([above, line, below] + extra, 1)
            line = line.reshape((2, -1, rows_tiles) + line.shape[2:])
            return jnp.moveaxis(line, 0, 1)

        own = jnp.stack([widen(own[0]), widen(own[1])])
        left, right = widen(left), widen(right)

    rows = jnp.arange(band * rows_tiles)[None, :, None] + (row_at // band) * band * rows_tiles
    cols = jnp.arange(2)[:, None, None] + (col_at // 2) * 2
    step = jnp.arange(9)[None, None, :]
    key_rows = rows + step // 3 - 1
    key_cols = cols + step % 3 - 1
    inside = (
        (key_rows >= 0)
        & (key_rows < rows_tiles * nrow)
        & (key_cols >= 0)
        & (key_cols < ncol)
    )
    ok = (inside & ((flags > 0) | (step == 4))).astype(jnp.int32)
    ok = jnp.moveaxis(ok, 0, 1).reshape(-1)

    out = attention(ok, q, own, left, right, far, pad)
    out = exchange(out.reshape((parts, rows_tiles, tile, part)))
    return jnp.moveaxis(out, 0, -2).reshape(queries.shape)


def solution(mesh):
    placed = (
        P("row", "col", None, None),
        P("row", "col", None, None),
        P("row", "col", None, None),
        P("row", "col", None),
        P("col", None),
        P("col", None),
    )
    return jax.shard_map(
        body, mesh=mesh, in_specs=placed, out_specs=P("row", "col", None, None), check_vma=False
    )
```

time: 520 us -> 148 us (0.28)
  waiting for transfers between devices: 220 us -> 59.1 us
  local copies, waits for them, and re-layouts: 157 us -> 14.9 us
  matrix products: 70.7 us -> 0 us
  blocking collectives: 0 us -> 26.9 us
  Pallas kernels: 0 us -> 23.9 us
  between operations: 23.8 us -> 0.22 us
  other arithmetic: 23.1 us -> 2.81 us
  loops' own time: 11.2 us -> 0 us
  starting transfers between devices: 9.87 us -> 19.9 us
    ppermute x4 -> x2, waiting for transfers between devices: 193 us -> 23.5 us  [the longest x1 23.5 us: body(): right = lax.ppermute(own[0], 'col', moves(ncol, -2))]
    slice x17 -> x1, local copies, waits for them, and re-layouts: 131 us -> 1.49 us  [body(): right = lax.ppermute(own[0], 'col', moves(ncol, -2))]
    dot_general x64 -> x0, matrix products: 70.7 us -> none  [the longest x16 22 us: one_head(): jnp.einsum('tqd,kd->tqk', query_head, far_key_head, preferred_element_typ...]
    all_to_all x0 -> x3, waiting for transfers between devices: none -> 35.5 us  [the longest x2 30.2 us: exchange(): return lax.all_to_all(a, axes, 0, 0, axis_index_groups=groups, tiled=True)]
    all_gather x2 -> x0, waiting for transfers between devices: 26.2 us -> none  [the longest x1 26.2 us: body(): lax.all_gather(coarse_values, 'col', axis=0, tiled=True)]
    pallas_call x0 -> x1, Pallas kernels: none -> 23.9 us  [attention(): pl.pallas_call(functools.partial(attend, pad), grid_spec=pltpu.PrefetchSc...]
    all_to_all x0 -> x1, blocking collectives: none -> 18.1 us  [exchange(): return lax.all_to_all(a, axes, 0, 0, axis_index_groups=groups, tiled=True)]
    all_to_all x0 -> x3, starting transfers between devices: none -> 14.1 us  [the longest x2 7.84 us: exchange(): return lax.all_to_all(a, axes, 0, 0, axis_index_groups=groups, tiled=True)]
  transfers between devices with their start and end apart: 6 -> 5, of which waited for: 5 -> 4; matrix products, arithmetic and copies ran while one was open for 5% -> 8% of each run, Pallas kernels for 0% -> 0%
where the time goes in v1:
time: 148 us
  waiting for transfers between devices  59.1 us (40%)
  blocking collectives  26.9 us (18%)
  Pallas kernels  23.9 us (16%)
  starting transfers between devices  19.9 us (13%)
  local copies, waits for them, and re-layouts  14.9 us (10%)
  other arithmetic  2.81 us (2%)
    all_to_all x2, waiting for transfers between devices, exchange(): return lax.all_to_all(a, axes, 0, 0, axis_index_groups=groups, tiled=True)  30.2 us
    pallas_call x1, Pallas kernels, attention(): pl.pallas_call(functools.partial(attend, pad), grid_spec=pltpu.PrefetchSc...  23.9 us
    ppermute x1, waiting for transfers between devices, body(): right = lax.ppermute(own[0], 'col', moves(ncol, -2))  23.5 us
    all_to_all x1, blocking collectives, exchange(): return lax.all_to_all(a, axes, 0, 0, axis_index_groups=groups, tiled=True)  18.1 us
    all_gather x1, blocking collectives, body(): flags = lax.all_gather(keep_flags, axes, axis=0, axis_index_groups=groups)  8.85 us
    all_to_all x2, starting transfers between devices, exchange(): return lax.all_to_all(a, axes, 0, 0, axis_index_groups=groups, tiled=True)  7.84 us
    unnamed x17, local copies, waits for them, and re-layouts  7.09 us
    all_to_all x1, starting transfers between devices, body(): far = lax.all_to_all(far, 'col', 0, 0, tiled=True)  6.24 us
  transfers between devices with their start and end apart: 5, of which 4 were waited for; matrix products, arithmetic and copies ran while one was open for 8% of the time, Pallas kernels for 0%

profile of v1, /device:TPU:8, one launch (start us, length us, event | category | flops | bytes accessed | tf_op | source)
XLA Modules:
  0.0 147.7 jit_solution(2958723222231092791)
XLA Ops:
  0.0 1.5 %copy.44 = bf16[32,8,8,256]{3,2,1,0:T(8,128)(2,1)S(1)} copy(bf16[32,8,8,256]{3,1,2,0:T(8,128)(2,1)} %bitcast.52) | data formatting | bytes 2097152
  1.5 0.0 copy-start.1
  1.5 1.2 copy.47
  2.7 4.2 %all-to-all-start = ((bf16[8,2,128,256]{3,2,1,0:T(8,128)(2,1)}), bf16[8,2,128,256]{3,2,1,0:T(8,128)(2,1)}, u32[]{:S(2)}, u32[]{:S(2)}) async-start(bf16[8,2,128,256]{3,2,1,0:T(8,128)(2,1)} %bitcast.40), calls=%async_computation | async-start | bytes 2097152 | tf_op jit(solution)/shard_map/all_to_all | solution.py:137
  7.0 0.0 copy-done.1
  7.0 0.7 copy.34
  7.7 0.5 copy.35
  8.2 1.6 %copy.36 = bf16[2,1,128,2048]{2,3,0,1:T(8,128)(2,1)S(1)} copy(bf16[2,1,128,2048]{3,2,1,0:T(8,128)(2,1)} %param.8) | data formatting | bytes 2097152 | tf_op args[2]
  9.8 0.5 copy.37
  10.4 1.5 %pad_maximum_fusion = bf16[8,2,2,128,256]{4,3,2,1,0:T(8,128)(2,1)} fusion(bf16[8,1,2,128,256]{4,3,2,1,0:T(8,128)(2,1)S(1)} %bitcast.47, bf16[8,1,2,128,256]{4,3,2,1,0:T(8,128)(2,1)S(1)} %bitcast.46), kind=kLoop, calls=%fused_computation | loop fusion | flops 1048576 | bytes 4194304 | tf_op jit(solution)/shard_map/stack | solution.py:139
  11.9 0.0 copy-start.3
  11.9 9.6 %all-to-all-done = bf16[8,2,128,256]{3,2,1,0:T(8,128)(2,1)} async-done(((bf16[8,2,128,256]{3,2,1,0:T(8,128)(2,1)}), bf16[8,2,128,256]{3,2,1,0:T(8,128)(2,1)}, u32[]{:S(2)}, u32[]{:S(2)}) %all-to-all-start) | async-done | bytes 1048608 | tf_op jit(solution)/shard_map/all_to_all | solution.py:137
  21.4 3.6 %all-to-all-start.1 = ((bf16[8,2,2,128,256]{4,3,2,1,0:T(8,128)(2,1)}), bf16[8,2,2,128,256]{4,3,2,1,0:T(8,128)(2,1)S(1)}, u32[]{:S(2)}, u32[]{:S(2)}) async-start(bf16[8,2,2,128,256]{4,3,2,1,0:T(8,128)(2,1)} %pad_maximum_fusion), calls=%async_computation.1 | async-start | bytes 4194304 | tf_op jit(solution)/shard_map/all_to_all | solution.py:137
  25.1 0.0 copy-done.3
  25.1 0.3 copy.38
  25.4 0.2 copy.39
  25.6 2.0 %copy.40 = bf16[128,2048]{0,1:T(8,128)(2,1)} copy(bf16[128,2048]{1,0:T(8,128)(2,1)} %param.11) | data formatting | bytes 1048576 | tf_op args[5]
  27.6 1.2 copy.41
  28.9 1.1 pad_maximum_fusion.1
  30.0 20.7 %all-to-all-done.1 = bf16[8,2,2,128,256]{4,3,2,1,0:T(8,128)(2,1)S(1)} async-done(((bf16[8,2,2,128,256]{4,3,2,1,0:T(8,128)(2,1)}), bf16[8,2,2,128,256]{4,3,2,1,0:T(8,128)(2,1)S(1)}, u32[]{:S(2)}, u32[]{:S(2)}) %all-to-all-start.1) | async-done | bytes 2097184 | tf_op jit(solution)/shard_map/all_to_all | solution.py:137
  50.7 0.0 copy-start
  50.7 6.2 %all-to-all-start.2 = ((bf16[8,2,128,256]{3,2,1,0:T(8,128)(2,1)}), bf16[8,2,128,256]{3,2,1,0:T(8,128)(2,1)S(1)}, u32[]{:S(2)}, u32[]{:S(2)}) async-start(bf16[8,2,128,256]{3,2,1,0:T(8,128)(2,1)} %pad_maximum_fusion.1), calls=%async_computation.2 | async-start | bytes 2097152 | tf_op jit(solution)/shard_map/all_to_all | solution.py:152
  56.9 0.0 copy-start.4
  56.9 1.5 %fusion.7 = (bf16[4,2,2,128,256]{4,3,2,1,0:T(8,128)(2,1)}, bf16[4,2,2,128,256]{4,3,2,1,0:T(8,128)(2,1)}) fusion(bf16[8,2,2,128,256]{4,3,2,1,0:T(8,128)(2,1)S(1)} %all-to-all-done.1), kind=kLoop, calls=%fused_computation.25 | loop fusion | bytes 4194304 | tf_op jit(solution)/shard_map/slice | solution.py:146
  58.4 0.0 copy-done
  58.4 1.9 %collective-permute-start.1 = (bf16[4,2,2,128,256]{4,3,2,1,0:T(8,128)(2,1)}, bf16[4,2,2,128,256]{4,3,2,1,0:T(8,128)(2,1)S(1)}, u32[]{:S(2)}, u32[]{:S(2)}) collective-permute-start(bf16[4,2,2,128,256]{4,3,2,1,0:T(8,128)(2,1)} %get-tuple-element.5), channel_id=1, source_target_pairs={{2,0},{3,1},{4,2},{5,3},{6,4},{7,5},{10,8},{11,9},{12,10},{13,11},... | collective-permute-start | bytes 3145736 | tf_op jit(solution)/shard_map/ppermute | solution.py:146
  60.3 3.9 %collective-permute-start = (bf16[4,2,2,128,256]{4,3,2,1,0:T(8,128)(2,1)}, bf16[4,2,2,128,256]{4,3,2,1,0:T(8,128)(2,1)}, u32[]{:S(2)}, u32[]{:S(2)}) collective-permute-start(bf16[4,2,2,128,256]{4,3,2,1,0:T(8,128)(2,1)} %get-tuple-element.6), channel_id=1, source_target_pairs={{0,2},{1,3},{2,4},{3,5},{4,6},{5,7},{8,10},{9,11},{10,12},{11,13},... | collective-permute-start | bytes 3145736 | tf_op jit(solution)/shard_map/ppermute | solution.py:145
  64.3 0.0 copy-done.4
  64.3 8.9 %all-gather = s32[16,1,9]{2,1,0:T(1,128)S(1)} all-gather(s32[2,1,9]{2,1,0:T(1,128)S(1)} %copy-done.4), channel_id=2, replica_groups={{0,8,16,24,1,9,17,25},{2,10,18,26,3,11,19,27},{4,12,20,28,5,13,21,29},{..., dimensions={0}, use_global_device_ids=true | all-gather | bytes 648 | tf_op jit(solution)/shard_map/all_gather | solution.py:142
  73.2 0.1 fusion.4
  73.3 0.1 fusion.6
  73.4 0.7 reshape.194.ok_ref
  74.0 5.3 %all-to-all-done.2.far_ref = bf16[8,2,128,256]{3,2,1,0:T(8,128)(2,1)S(1)} async-done(((bf16[8,2,128,256]{3,2,1,0:T(8,128)(2,1)}), bf16[8,2,128,256]{3,2,1,0:T(8,128)(2,1)S(1)}, u32[]{:S(2)}, u32[]{:S(2)}) %all-to-all-start.2) | async-done | bytes 1048608 | tf_op jit(solution)/shard_map/all_to_all | solution.py:152
  79.3 0.0 copy-start.2
  79.3 23.5 %collective-permute-done.1.right_ref = bf16[4,2,2,128,256]{4,3,2,1,0:T(8,128)(2,1)S(1)} collective-permute-done((bf16[4,2,2,128,256]{4,3,2,1,0:T(8,128)(2,1)}, bf16[4,2,2,128,256]{4,3,2,1,0:T(8,128)(2,1)S(1)}, u32[]{:S(2)}, u32[]{:S(2)}) %collective-permute-start.1) | collective-permute-done | bytes 1048608 | tf_op jit(solution)/shard_map/ppermute | solution.py:146
  102.9 0.0 copy-start.5
  102.9 0.0 collective-permute-done.left_ref
  102.9 0.0 copy-done.2
  102.9 1.0 copy-done.5
  103.8 23.9 %attend.1 = bf16[2,4,2,128,256]{4,3,2,1,0:T(8,128)(2,1)} custom-call(s32[144]{0:T(256)} %reshape.194.ok_ref, bf16[2,4,2,128,256]{4,3,2,1,0:T(8,128)(2,1)} %bitcast.4.q_ref, bf16[2,4,2,2,128,256]{5,4,3,2,1,0:T(8,128)(2,1)} %bitcast.41, bf16[4,2,2,128,256]{4,3,2,1,0:T(8,128)(2,1)} %collective-permute-done.left_ref, bf16[4,2,2,128,256]{4,3,2,1,0:T(8,128)(2,1)} %copy-done.5, ...), custom_call_target="tpu_custom_call" | custom-call | flops 4563402752 | bytes 8388608 | tf_op jit(solution)/shard_map/attend/pallas_call | solution.py:97
  127.7 18.1 %all_to_all.20 = bf16[8,2,128,256]{3,2,1,0:T(8,128)(2,1)S(1)} all-to-all(bf16[8,2,128,256]{3,2,1,0:T(8,128)(2,1)} %bitcast.53), channel_id=1, replica_groups={{0,8,16,24,1,9,17,25},{2,10,18,26,3,11,19,27},{4,12,20,28,5,13,21,29},{..., dimensions={0} | all-to-all | bytes 2097152 | tf_op jit(solution)/shard_map/all_to_all | solution.py:137
  145.8 0.6 copy.43
  146.4 1.3 reshape.192
  (8 shorter events, 0.1 us)
Async XLA Ops:
  1.5 5.5 %copy-start.1 = (bf16[2,1,128,2048]{3,2,1,0:T(8,128)(2,1)S(1)}, bf16[2,1,128,2048]{3,2,1,0:T(8,128)(2,1)}, u32[]{:S(2)}) copy-start(bf16[2,1,128,2048]{3,2,1,0:T(8,128)(2,1)} %param.7) | copy-start | bytes 3145732
  2.7 18.7 %all-to-all-start = ((bf16[8,2,128,256]{3,2,1,0:T(8,128)(2,1)}), bf16[8,2,128,256]{3,2,1,0:T(8,128)(2,1)}, u32[]{:S(2)}, u32[]{:S(2)}) async-start(bf16[8,2,128,256]{3,2,1,0:T(8,128)(2,1)} %bitcast.40), calls=%async_computation | async-start | bytes 2097152 | tf_op jit(solution)/shard_map/all_to_all | solution.py:137
  11.9 13.2 %copy-start.3 = (bf16[128,2048]{1,0:T(8,128)(2,1)S(1)}, bf16[128,2048]{1,0:T(8,128)(2,1)}, u32[]{:S(2)}) copy-start(bf16[128,2048]{1,0:T(8,128)(2,1)} %param.10) | copy-start | bytes 1572868
  21.4 29.2 %all-to-all-start.1 = ((bf16[8,2,2,128,256]{4,3,2,1,0:T(8,128)(2,1)}), bf16[8,2,2,128,256]{4,3,2,1,0:T(8,128)(2,1)S(1)}, u32[]{:S(2)}, u32[]{:S(2)}) async-start(bf16[8,2,2,128,256]{4,3,2,1,0:T(8,128)(2,1)} %pad_maximum_fusion), calls=%async_computation.1 | async-start | bytes 4194304 | tf_op jit(solution)/shard_map/all_to_all | solution.py:137
  50.7 7.7 %copy-start = (bf16[8,2,2,128,256]{4,3,2,1,0:T(8,128)(2,1)}, bf16[8,2,2,128,256]{4,3,2,1,0:T(8,128)(2,1)S(1)}, u32[]{:S(2)}) copy-start(bf16[8,2,2,128,256]{4,3,2,1,0:T(8,128)(2,1)S(1)} %all-to-all-done.1) | copy-start | bytes 6291460
  50.7 28.7 %all-to-all-start.2 = ((bf16[8,2,128,256]{3,2,1,0:T(8,128)(2,1)}), bf16[8,2,128,256]{3,2,1,0:T(8,128)(2,1)S(1)}, u32[]{:S(2)}, u32[]{:S(2)}) async-start(bf16[8,2,128,256]{3,2,1,0:T(8,128)(2,1)} %pad_maximum_fusion.1), calls=%async_computation.2 | async-start | bytes 2097152 | tf_op jit(solution)/shard_map/all_to_all | solution.py:152
  56.9 7.4 %copy-start.4 = (s32[2,1,9]{2,1,0:T(1,128)S(1)}, s32[2,1,9]{2,1,0:T(1,128)}, u32[]{:S(2)}) copy-start(s32[2,1,9]{2,1,0:T(1,128)} %param.9) | copy-start | bytes 220
  58.4 44.5 %collective-permute-start.1 = (bf16[4,2,2,128,256]{4,3,2,1,0:T(8,128)(2,1)}, bf16[4,2,2,128,256]{4,3,2,1,0:T(8,128)(2,1)S(1)}, u32[]{:S(2)}, u32[]{:S(2)}) collective-permute-start(bf16[4,2,2,128,256]{4,3,2,1,0:T(8,128)(2,1)} %get-tuple-element.5), channel_id=1, source_target_pairs={{2,0},{3,1},{4,2},{5,3},{6,4},{7,5},{10,8},{11,9},{12,10},{13,11},... | collective-permute-start | bytes 3145736 | tf_op jit(solution)/shard_map/ppermute | solution.py:146
  60.3 42.5 %collective-permute-start = (bf16[4,2,2,128,256]{4,3,2,1,0:T(8,128)(2,1)}, bf16[4,2,2,128,256]{4,3,2,1,0:T(8,128)(2,1)}, u32[]{:S(2)}, u32[]{:S(2)}) collective-permute-start(bf16[4,2,2,128,256]{4,3,2,1,0:T(8,128)(2,1)} %get-tuple-element.6), channel_id=1, source_target_pairs={{0,2},{1,3},{2,4},{3,5},{4,6},{5,7},{8,10},{9,11},{10,12},{11,13},... | collective-permute-start | bytes 3145736 | tf_op jit(solution)/shard_map/ppermute | solution.py:145
  79.3 23.5 %copy-start.2 = (bf16[8,2,128,256]{3,2,1,0:T(8,128)(2,1)}, bf16[8,2,128,256]{3,2,1,0:T(8,128)(2,1)S(1)}, u32[]{:S(2)}) copy-start(bf16[8,2,128,256]{3,2,1,0:T(8,128)(2,1)S(1)} %all-to-all-done.2.far_ref) | copy-start | bytes 3145732
  102.9 1.0 copy-start.5

commit v2 on v1

v2 whole, which is shorter than its diff:
```python
import functools

import jax
import jax.numpy as jnp
from jax import lax
from jax.experimental import pallas as pl
from jax.experimental.pallas import tpu as pltpu
from jax.sharding import PartitionSpec as P

HEADS = 16
HEAD_DIM = 128
LOG2_SCALE = HEAD_DIM ** (-0.5) * 1.4426950408889634


NT = (((1,), (1,)), ((), ()))


def scores(a, b):
    return lax.dot_general(a, b, NT, preferred_element_type=jnp.float32)


def softmax_terms(pieces, flags, m):
    tiles = [
        s if flag is None else jnp.where(flag > 0, s, -jnp.inf) for s, flag in zip(pieces, flags)
    ]
    top = jnp.max(functools.reduce(jnp.maximum, tiles), axis=1, keepdims=True)
    m = top if m is None else jnp.maximum(m, top)
    powers, total = [], None
    for s in tiles:
        p = jnp.exp2((s - m) * LOG2_SCALE)
        total = p if total is None else total + p
        powers.append(p.astype(jnp.bfloat16))
    return m, jnp.sum(total, axis=1, keepdims=True), powers


def key_rows_of(i, pad, key_rows, rows_in_band):
    rows = [(a, i + pad + a - 1) for a in range(3)]
    return [(a, j // rows_in_band, j % rows_in_band) for a, j in rows if 0 <= j < key_rows]


def attend_near(pad, planes, ok_ref, q_ref, own_ref, *refs):
    far_refs, (acc_ref, stat_ref) = refs[:planes], refs[planes:]
    _, bands, rows_in_band, tile, _ = acc_ref.shape
    key_rows = own_ref.shape[1] * rows_in_band
    shards = [(f, c) for f in far_refs for c in range(2)]
    lane = lax.broadcasted_iota(jnp.int32, (tile, tile), 1)
    stat = jnp.zeros((tile, tile), jnp.float32)
    for i in range(bands * rows_in_band):
        band, sub = i // rows_in_band, i % rows_in_band
        at = key_rows_of(i, pad, key_rows, rows_in_band)
        qq = jnp.concatenate([q_ref[x, band, sub * tile : (sub + 1) * tile] for x in range(2)], 0)
        far = scores(qq, jnp.concatenate([f[c, 0] for f, c in shards], 0))
        near = scores(
            qq, jnp.concatenate([own_ref[x, kb, 0, ks] for _, kb, ks in at for x in range(2)], 0)
        )
        values = jnp.concatenate(
            [f[c, 1] for f, c in shards]
            + [own_ref[x, kb, 1, ks] for _, kb, ks in at for x in range(2)],
            0,
        )
        for xq in range(2):
            mine = slice(xq * tile, (xq + 1) * tile)
            pieces = [far[mine, n * tile : (n + 1) * tile] for n in range(len(shards))]
            pieces += [near[mine, n * tile : (n + 1) * tile] for n in range(2 * len(at))]
            flags = [None] * len(shards) + [
                ok_ref[(i * 2 + xq) * 9 + a * 3 + 1 + x - xq] for a, _, _ in at for x in range(2)
            ]
            m, total, powers = softmax_terms(pieces, flags, None)
            acc_ref[xq, band, sub] = jnp.dot(
                jnp.concatenate(powers, 1), values, preferred_element_type=jnp.float32
            )
            n = i * 2 + xq
            stat = jnp.where(lane == n, m, jnp.where(lane == n + tile // 2, total, stat))
    stat_ref[0] = stat


def attend_sides(pad, ok_ref, q_ref, left_ref, right_ref, acc_ref, stat_ref, out_ref):
    _, bands, rows_in_band, tile, _ = out_ref.shape
    rows = bands * rows_in_band
    key_rows = left_ref.shape[0] * rows_in_band
    lane = lax.broadcasted_iota(jnp.int32, (tile, tile), 1)
    stat = stat_ref[0]
    for xq, side in ((0, left_ref), (1, right_ref)):
        near_rows = [
            [i for i in range(rows) if abs(i + pad - j) <= 1] for j in range(key_rows)
        ]
        near_rows = {j: found for j, found in enumerate(near_rows) if found}
        pieces = {}
        for j, found in near_rows.items():
            qs = [
                q_ref[xq, i // rows_in_band, i % rows_in_band * tile : (i % rows_in_band + 1) * tile]
                for i in found
            ]
            s = scores(jnp.concatenate(qs, 0), side[j // rows_in_band, 0, j % rows_in_band])
            for u, i in enumerate(found):
                pieces[i, j] = s[u * tile : (u + 1) * tile]
        shrinks, totals = {}, {}
        for i in range(rows):
            n = i * 2 + xq
            m_near = jnp.max(jnp.where(lane == n, stat, -jnp.inf), axis=1, keepdims=True)
            near = jnp.max(jnp.where(lane == n + tile // 2, stat, -jnp.inf), axis=1, keepdims=True)
            at = [j for j in near_rows if (i, j) in pieces]
            flags = [ok_ref[n * 9 + (j - i - pad + 1) * 3 + 2 * xq] for j in at]
            m, total, powers = softmax_terms([pieces[i, j] for j in at], flags, m_near)
            for u, j in enumerate(at):
                pieces[i, j] = powers[u]
            shrinks[i] = jnp.exp2((m_near - m) * LOG2_SCALE)
            totals[i] = total + near * shrinks[i]
        more = {}
        for j, found in near_rows.items():
            o = jnp.dot(
                jnp.concatenate([pieces[i, j] for i in found], 0),
                side[j // rows_in_band, 1, j % rows_in_band],
                preferred_element_type=jnp.float32,
            )
            for u, i in enumerate(found):
                o_i = o[u * tile : (u + 1) * tile]
                more[i] = more[i] + o_i if i in more else o_i
        for i in range(rows):
            band, sub = i // rows_in_band, i % rows_in_band
            out = (acc_ref[xq, band, sub] * shrinks[i] + more[i]) / totals[i]
            out_ref[xq, band, sub] = out.astype(out_ref.dtype)


def by_head(a):
    lead = a.shape[:-1]
    return pl.BlockSpec(lead + (HEAD_DIM,), lambda h, s, n=len(lead): (0,) * n + (h,))


def call(kernel, name, ok, operands, in_specs, out_shape, out_specs, heads, tiles):
    flops = 4 * tiles * heads * 128 * 128 * HEAD_DIM
    return pl.pallas_call(
        kernel,
        grid_spec=pltpu.PrefetchScalarGridSpec(
            num_scalar_prefetch=1,
            grid=(heads,),
            in_specs=in_specs,
            out_specs=out_specs,
        ),
        out_shape=out_shape,
        compiler_params=pltpu.CompilerParams(vmem_limit_bytes=56 * 1024 * 1024),
        cost_estimate=pl.CostEstimate(
            flops=flops, bytes_accessed=8 * 1024 * 1024, transcendentals=flops // 512
        ),
        name=name,
    )(ok, *operands)


def near_part(ok, q, own, far, pad, shape):
    heads, tile = shape[-1] // HEAD_DIM, shape[-2]
    acc = jax.ShapeDtypeStruct(shape, jnp.float32)
    stat = jax.ShapeDtypeStruct((heads, tile, tile), jnp.float32)
    stat_spec = pl.BlockSpec((1, tile, tile), lambda h, s: (h, 0, 0))
    operands = (q, own, *far)
    tiles = shape[0] * shape[1] * shape[2] * (6 + 2 * len(far))
    return call(
        functools.partial(attend_near, pad, len(far)), "attend_near", ok, operands,
        [by_head(a) for a in operands], (acc, stat), (by_head(acc), stat_spec), heads, tiles,
    )


def side_part(ok, q, left, right, acc, stat, pad):
    heads, tile = acc.shape[-1] // HEAD_DIM, acc.shape[-2]
    out = jax.ShapeDtypeStruct(acc.shape, q.dtype)
    stat_spec = pl.BlockSpec((1, tile, tile), lambda h, s: (h, 0, 0))
    operands = (q, left, right, acc)
    tiles = acc.shape[0] * acc.shape[1] * acc.shape[2] * 3
    return call(
        functools.partial(attend_sides, pad), "attend_sides", ok, (*operands, stat),
        [by_head(a) for a in operands] + [stat_spec], out, by_head(out), heads, tiles,
    )


def moves(count, step):
    return [(i, i + step) for i in range(count) if 0 <= i + step < count]


def body(queries, fine_keys, fine_values, keep_flags, coarse_keys, coarse_values):
    rows_tiles, _, tile, width = queries.shape
    nrow, ncol = lax.axis_size("row"), lax.axis_size("col")
    band = min(4, nrow)
    planes = ncol // 2
    parts = band * 2
    part = width // parts
    row_at, col_at = lax.axis_index("row"), lax.axis_index("col")
    axes = ("row", "col")
    groups = [
        [(g * band + r) * ncol + 2 * z + x for x in range(2) for r in range(band)]
        for g in range(nrow // band)
        for z in range(planes)
    ]

    def by_part(a):
        return jnp.moveaxis(a.reshape(a.shape[:-1] + (parts, part)), -2, 0)

    def exchange(a):
        return lax.all_to_all(a, axes, 0, 0, axis_index_groups=groups, tiled=True)

    mine = jnp.stack([by_part(coarse_keys), by_part(coarse_values)], 1)
    mine = mine.reshape((2, band) + mine.shape[1:])
    mine = lax.dynamic_index_in_dim(mine, row_at % band, 1, keepdims=False)
    here = lax.dynamic_index_in_dim(mine, col_at % 2, 0, keepdims=False)
    away = lax.dynamic_index_in_dim(mine, 1 - col_at % 2, 0, keepdims=False)
    there = lax.ppermute(away, "col", [(c, c ^ 1) for c in range(ncol)])
    kv = jnp.stack([by_part(fine_keys[:, 0]), by_part(fine_values[:, 0])], 1)
    kv, there = lax.optimization_barrier((kv, there))
    own = exchange(kv)
    pair = jnp.stack([here, there])
    far = [pair] + [
        lax.ppermute(pair, "col", [(c, (c + 2 * d) % ncol) for c in range(ncol)])
        for d in range(1, planes)
    ]
    count = rows_tiles * 9
    notes = jnp.pad(keep_flags.astype(jnp.bfloat16).reshape(1, count), ((0, 15), (0, part - count)))
    queries_out = jnp.concatenate(
        [
            by_part(queries.reshape(rows_tiles * tile, width)),
            jnp.broadcast_to(notes, (parts, 16, part)),
        ],
        1,
    )
    queries_out, own, *far = lax.optimization_barrier((queries_out, own, *far))
    q = exchange(queries_out)
    flags = q[:, rows_tiles * tile, :count].reshape(2, band * rows_tiles, 9)
    q = q.reshape(2, band, rows_tiles * tile + 16, part)
    own = own.reshape(2, band, 2, rows_tiles, tile, part)

    left = lax.ppermute(own[1], "col", moves(ncol, 2))
    right = lax.ppermute(own[0], "col", moves(ncol, -2))

    pad = 0
    if nrow > band:
        pad = 1

        def widen(a):
            line = jnp.moveaxis(a, 1, 0)
            line = line.reshape((2, band * rows_tiles) + line.shape[3:])
            above = lax.ppermute(line[:, -1:], "row", moves(nrow, band))
            below = lax.ppermute(line[:, :1], "row", moves(nrow, -band))
            extra = [line[:, :1]] * ((-2) % rows_tiles)
            line = jnp.concatenate([above, line, below] + extra, 1)
            line = line.reshape((2, -1, rows_tiles) + line.shape[2:])
            return jnp.moveaxis(line, 0, 1)

        own = jnp.stack([widen(own[0]), widen(own[1])])
        left, right = widen(left), widen(right)

    rows = jnp.arange(band * rows_tiles)[None, :, None] + (row_at // band) * band * rows_tiles
    cols = jnp.arange(2)[:, None, None] + (col_at // 2) * 2
    step = jnp.arange(9)[None, None, :]
    key_rows = rows + step // 3 - 1
    key_cols = cols + step % 3 - 1
    inside = (
        (key_rows >= 0)
        & (key_rows < rows_tiles * nrow)
        & (key_cols >= 0)
        & (key_cols < ncol)
    )
    ok = (inside & ((flags > 0) | (step == 4))).astype(jnp.int32)
    ok = jnp.moveaxis(ok, 0, 1).reshape(-1)

    shape = (2, band, rows_tiles, tile, part)
    acc, stat = near_part(ok, q, own, far, pad, shape)
    out = side_part(ok, q, left, right, acc, stat, pad)
    out = exchange(out.reshape((parts, rows_tiles, tile, part)))
    return jnp.moveaxis(out, 0, -2).reshape(queries.shape)


def solution(mesh):
    placed = (
        P("row", "col", None, None),
        P("row", "col", None, None),
        P("row", "col", None, None),
        P("row", "col", None),
        P("col", None),
        P("col", None),
    )
    return jax.shard_map(
        body, mesh=mesh, in_specs=placed, out_specs=P("row", "col", None, None), check_vma=False
    )
```

time: 148 us -> 104 us (0.70)
  waiting for transfers between devices: 59.1 us -> 26.1 us
  blocking collectives: 26.9 us -> 18.4 us
  Pallas kernels: 23.9 us -> 20.7 us
  local copies, waits for them, and re-layouts: 14.9 us -> 12 us
    ppermute x1, waiting for transfers between devices: 23.5 us -> 0.01 us  [body(): right = lax.ppermute(own[0], 'col', moves(ncol, -2))]
    all_to_all x2, waiting for transfers between devices: 30.2 us -> 7.09 us  [exchange(): return lax.all_to_all(a, axes, 0, 0, axis_index_groups=groups, tiled=True)]
    ppermute x0 -> x4, waiting for transfers between devices: none -> 17.5 us  [the longest x3 17.5 us: body(): lax.ppermute(pair, 'col', [(c, (c + 2 * d) % ncol) for c in range(ncol)])]
    all_gather x1 -> x0, blocking collectives: 8.85 us -> none  [body(): flags = lax.all_gather(keep_flags, axes, axis=0, axis_index_groups=groups)]
    ppermute x0 -> x4, starting transfers between devices: none -> 7.15 us  [the longest x3 5.6 us: body(): lax.ppermute(pair, 'col', [(c, (c + 2 * d) % ncol) for c in range(ncol)])]
    all_to_all x1 -> x0, starting transfers between devices: 6.24 us -> none  [body(): far = lax.all_to_all(far, 'col', 0, 0, tiled=True)]
    all_to_all x1 -> x0, waiting for transfers between devices: 5.3 us -> none  [body(): far = lax.all_to_all(far, 'col', 0, 0, tiled=True)]
    pallas_call x1 -> x2, Pallas kernels: 23.9 us -> 20.7 us  [call(): pl.pallas_call(kernel, grid_spec=pltpu.PrefetchScalarGridSpec(num_scalar_...]
  transfers between devices with their start and end apart: 5 -> 8, of which waited for: 4 -> 5; matrix products, arithmetic and copies ran while one was open for 8% -> 10% of each run, Pallas kernels for 0% -> 14%
where the time goes in v2:
time: 104 us; the launch traced here: 103 us
  waiting for transfers between devices  26.1 us (25%)
  starting transfers between devices  21.2 us (20%)
  Pallas kernels  20.7 us (20%)
  blocking collectives  18.4 us (18%)
  local copies, waits for them, and re-layouts  12 us (12%)
  other arithmetic  4.06 us (4%)
    pallas_call x2, Pallas kernels, call(): pl.pallas_call(kernel, grid_spec=pltpu.PrefetchScalarGridSpec(num_scalar_...  20.7 us
    all_to_all x1, blocking collectives, exchange(): return lax.all_to_all(a, axes, 0, 0, axis_index_groups=groups, tiled=True)  18.4 us
    ppermute x3, waiting for transfers between devices, body(): lax.ppermute(pair, 'col', [(c, (c + 2 * d) % ncol) for c in range(ncol)])  17.5 us
    all_to_all x2, starting transfers between devices, exchange(): return lax.all_to_all(a, axes, 0, 0, axis_index_groups=groups, tiled=True)  7.62 us
    all_to_all x2, waiting for transfers between devices, exchange(): return lax.all_to_all(a, axes, 0, 0, axis_index_groups=groups, tiled=True)  7.09 us
    ppermute x3, starting transfers between devices, body(): lax.ppermute(pair, 'col', [(c, (c + 2 * d) % ncol) for c in range(ncol)])  5.6 us
    unnamed x27, local copies, waits for them, and re-layouts  4.99 us
    ppermute x1, starting transfers between devices, body(): left = lax.ppermute(own[1], 'col', moves(ncol, 2))  3.25 us
  transfers between devices with their start and end apart: 8, of which 5 were waited for; matrix products, arithmetic and copies ran while one was open for 10% of the time, Pallas kernels for 14%

profile of v2, /device:TPU:8, one launch (start us, length us, event | category | flops | bytes accessed | tf_op | source)
XLA Modules:
  0.0 102.7 jit_solution(7286235881695717289)
XLA Ops:
  0.0 0.0 copy-start.7
  0.0 1.2 %copy.38 = bf16[16,8,8,256]{3,2,1,0:T(8,128)(2,1)S(1)} copy(bf16[16,8,8,256]{3,1,2,0:T(8,128)(2,1)} %bitcast.52) | data formatting | bytes 1048576
  1.2 0.0 copy-start.2
  1.2 0.1 copy.32
  1.3 0.0 copy-done.7
  1.4 0.1 copy.39
  1.5 0.1 copy.33
  1.6 0.0 copy-start.3
  1.6 1.6 %collective-permute-start = (bf16[2,128,256]{2,1,0:T(8,128)(2,1)S(1)}, bf16[2,128,256]{2,1,0:T(8,128)(2,1)S(1)}, u32[]{:S(2)}, u32[]{:S(2)}) collective-permute-start(bf16[2,128,256]{2,1,0:T(8,128)(2,1)S(1)} %get-tuple-element.28), channel_id=1, source_target_pairs={{0,1},{1,0},{2,3},{3,2},{4,5},{5,4},{6,7},{7,6},{8,9},{9,8},{10,11... | collective-permute-start | bytes 393224 | tf_op jit(solution)/shard_map/ppermute | solution.py:204
  3.2 0.0 copy-done.2
  3.2 0.7 copy.28
  3.9 0.5 copy.29
  4.4 0.0 copy-done.3
  4.4 0.7 copy.30
  5.1 0.5 copy.31
  5.6 1.5 %pad_maximum_fusion = bf16[8,2,2,128,256]{4,3,2,1,0:T(8,128)(2,1)} fusion(bf16[8,1,2,128,256]{4,3,2,1,0:T(8,128)(2,1)S(1)} %bitcast.46, bf16[8,1,2,128,256]{4,3,2,1,0:T(8,128)(2,1)S(1)} %bitcast.45), kind=kLoop, calls=%fused_computation | loop fusion | flops 1048576 | bytes 4194304 | tf_op jit(solution)/shard_map/stack | solution.py:205
  7.1 0.0 copy-start.10
  7.1 0.0 copy-start.4
  7.1 0.0 collective-permute-done
  7.1 0.0 copy-start.9
  7.2 3.7 %all-to-all-start = ((bf16[8,2,2,128,256]{4,3,2,1,0:T(8,128)(2,1)}), bf16[8,2,2,128,256]{4,3,2,1,0:T(8,128)(2,1)S(1)}, u32[]{:S(2)}, u32[]{:S(2)}) async-start(bf16[8,2,2,128,256]{4,3,2,1,0:T(8,128)(2,1)} %pad_maximum_fusion), calls=%async_computation | async-start | bytes 4194304 | tf_op jit(solution)/shard_map/all_to_all | solution.py:197
  10.9 0.0 copy-done.10
  11.0 0.0 copy-done.9
  11.0 0.9 pad_maximum_fusion.2.refs_0_
  11.9 0.0 copy-start.8
  11.9 0.5 collective-permute-start.3
  12.4 2.6 %collective-permute-start.2 = (bf16[2,2,128,256]{3,2,1,0:T(8,128)(2,1)S(1)}, bf16[2,2,128,256]{3,2,1,0:T(8,128)(2,1)}, u32[]{:S(2)}, u32[]{:S(2)}) collective-permute-start(bf16[2,2,128,256]{3,2,1,0:T(8,128)(2,1)S(1)} %pad_maximum_fusion.2.refs_0_), channel_id=1, source_target_pairs={{0,4},{1,5},{2,6},{3,7},{4,0},{5,1},{6,2},{7,3},{8,12},{9,13},{10,... | collective-permute-start | bytes 786440 | tf_op jit(solution)/shard_map/ppermute | solution.py:210
  15.0 2.5 %collective-permute-start.1 = (bf16[2,2,128,256]{3,2,1,0:T(8,128)(2,1)S(1)}, bf16[2,2,128,256]{3,2,1,0:T(8,128)(2,1)}, u32[]{:S(2)}, u32[]{:S(2)}) collective-permute-start(bf16[2,2,128,256]{3,2,1,0:T(8,128)(2,1)S(1)} %pad_maximum_fusion.2.refs_0_), channel_id=1, source_target_pairs={{0,2},{1,3},{2,4},{3,5},{4,6},{5,7},{6,0},{7,1},{8,10},{9,11},{10,... | collective-permute-start | bytes 786440 | tf_op jit(solution)/shard_map/ppermute | solution.py:210
  17.5 0.1 reshape.190
  17.6 0.0 copy-done.4
  17.6 1.3 %copy.37 = bf16[32,8,8,256]{3,2,1,0:T(8,128)(2,1)} copy(bf16[32,8,8,256]{3,1,2,0:T(8,128)(2,1)S(1)} %bitcast.51) | data formatting | bytes 2097152
  18.9 1.3 %pad_maximum_fusion.1 = bf16[8,272,256]{2,0,1:T(8,128)(2,1)S(1)} fusion(bf16[8,16,256]{2,0,1:T(8,128)(2,1)S(1)} %broadcast_in_dim.2, bf16[8,256,256]{2,0,1:T(8,128)(2,1)} %bitcast.40), kind=kLoop, calls=%fused_computation.5 | loop fusion | flops 557056 | bytes 2228224 | tf_op jit(solution)/shard_map/concatenate | solution.py:215
  20.2 0.0 copy-done.8
  20.2 1.1 %collective-permute-done.3.refs_3_ = bf16[2,2,128,256]{3,2,1,0:T(8,128)(2,1)} collective-permute-done((bf16[2,2,128,256]{3,2,1,0:T(8,128)(2,1)S(1)}, bf16[2,2,128,256]{3,2,1,0:T(8,128)(2,1)}, u32[]{:S(2)}, u32[]{:S(2)}) %collective-permute-start.3) | collective-permute-done | bytes 262176 | tf_op jit(solution)/shard_map/ppermute | solution.py:210
  21.3 11.6 %collective-permute-done.2.refs_2_ = bf16[2,2,128,256]{3,2,1,0:T(8,128)(2,1)} collective-permute-done((bf16[2,2,128,256]{3,2,1,0:T(8,128)(2,1)S(1)}, bf16[2,2,128,256]{3,2,1,0:T(8,128)(2,1)}, u32[]{:S(2)}, u32[]{:S(2)}) %collective-permute-start.2) | collective-permute-done | bytes 262176 | tf_op jit(solution)/shard_map/ppermute | solution.py:210
  32.9 4.8 %collective-permute-done.1.refs_1_ = bf16[2,2,128,256]{3,2,1,0:T(8,128)(2,1)} collective-permute-done((bf16[2,2,128,256]{3,2,1,0:T(8,128)(2,1)S(1)}, bf16[2,2,128,256]{3,2,1,0:T(8,128)(2,1)}, u32[]{:S(2)}, u32[]{:S(2)}) %collective-permute-start.1) | collective-permute-done | bytes 262176 | tf_op jit(solution)/shard_map/ppermute | solution.py:210
  37.7 0.0 all-to-all-done
  37.7 0.0 copy-start
  37.7 1.4 %copy.34 = bf16[8,272,256]{2,1,0:T(8,128)(2,1)} copy(bf16[8,272,256]{2,0,1:T(8,128)(2,1)S(1)} %pad_maximum_fusion.1) | data formatting | bytes 2228224 | tf_op jit(solution)/shard_map/optimization_barrier | solution.py:222
  39.1 3.9 %all-to-all-start.1 = ((bf16[8,272,256]{2,1,0:T(8,128)(2,1)}), bf16[8,272,256]{2,1,0:T(8,128)(2,1)S(1)}, u32[]{:S(2)}, u32[]{:S(2)}) async-start(bf16[8,272,256]{2,1,0:T(8,128)(2,1)} %copy.34), calls=%async_computation.1 | async-start | bytes 2228224 | tf_op jit(solution)/shard_map/all_to_all | solution.py:197
  43.0 0.1 fusion.6
  43.1 0.0 copy-done
  43.1 1.5 %fusion.9 = (bf16[4,2,2,128,256]{4,3,2,1,0:T(8,128)(2,1)}, bf16[4,2,2,128,256]{4,3,2,1,0:T(8,128)(2,1)}) fusion(bf16[8,2,2,128,256]{4,3,2,1,0:T(8,128)(2,1)S(1)} %all-to-all-done), kind=kLoop, calls=%fused_computation.29 | loop fusion | bytes 4194304 | tf_op jit(solution)/shard_map/slice | solution.py:229
  44.5 3.2 %collective-permute-start.5 = (bf16[4,2,2,128,256]{4,3,2,1,0:T(8,128)(2,1)}, bf16[4,2,2,128,256]{4,3,2,1,0:T(8,128)(2,1)S(1)}, u32[]{:S(2)}, u32[]{:S(2)}) collective-permute-start(bf16[4,2,2,128,256]{4,3,2,1,0:T(8,128)(2,1)} %get-tuple-element.25), channel_id=1, source_target_pairs={{2,0},{3,1},{4,2},{5,3},{6,4},{7,5},{10,8},{11,9},{12,10},{13,11},... | collective-permute-start | bytes 3145736 | tf_op jit(solution)/shard_map/ppermute | solution.py:229
  47.7 3.2 %collective-permute-start.4 = (bf16[4,2,2,128,256]{4,3,2,1,0:T(8,128)(2,1)}, bf16[4,2,2,128,256]{4,3,2,1,0:T(8,128)(2,1)S(1)}, u32[]{:S(2)}, u32[]{:S(2)}) collective-permute-start(bf16[4,2,2,128,256]{4,3,2,1,0:T(8,128)(2,1)} %get-tuple-element.26), channel_id=1, source_target_pairs={{0,2},{1,3},{2,4},{3,5},{4,6},{5,7},{8,10},{9,11},{10,12},{11,13},... | collective-permute-start | bytes 3145736 | tf_op jit(solution)/shard_map/ppermute | solution.py:228
  51.0 0.1 fusion.8
  51.1 7.1 %all-to-all-done.1 = bf16[8,272,256]{2,1,0:T(8,128)(2,1)S(1)} async-done(((bf16[8,272,256]{2,1,0:T(8,128)(2,1)}), bf16[8,272,256]{2,1,0:T(8,128)(2,1)S(1)}, u32[]{:S(2)}, u32[]{:S(2)}) %all-to-all-start.1) | async-done | bytes 1114144 | tf_op jit(solution)/shard_map/all_to_all | solution.py:197
  58.2 0.0 copy-start.1
  58.2 0.1 gt.11
  58.3 0.8 reshape.200.ok_ref
  59.1 0.1 copy-done.1
  59.2 14.4 %attend_near.1 = (f32[2,4,2,128,256]{4,3,2,1,0:T(8,128)}, f32[2,128,128]{2,1,0:T(8,128)}) custom-call(s32[144]{0:T(256)} %reshape.200.ok_ref, bf16[2,4,272,256]{3,2,1,0:T(8,128)(2,1)} %bitcast.38, bf16[2,4,2,2,128,256]{5,4,3,2,1,0:T(8,128)(2,1)} %bitcast.37, bf16[2,2,128,256]{3,2,1,0:T(8,128)(2,1)} %copy-done.8, ...), custom_call_target="tpu_custom_call" | custom-call | flops 3758096384 | bytes 8388608 | tf_op jit(solution)/shard_map/attend_near/pallas_call | solution.py:132
  73.6 0.0 collective-permute-done.5.right_ref
  73.6 0.0 copy-start.5
  73.6 1.5 %collective-permute-done.4.left_ref = bf16[4,2,2,128,256]{4,3,2,1,0:T(8,128)(2,1)S(1)} collective-permute-done((bf16[4,2,2,128,256]{4,3,2,1,0:T(8,128)(2,1)}, bf16[4,2,2,128,256]{4,3,2,1,0:T(8,128)(2,1)S(1)}, u32[]{:S(2)}, u32[]{:S(2)}) %collective-permute-start.4) | collective-permute-done | bytes 1048608 | tf_op jit(solution)/shard_map/ppermute | solution.py:228
  75.1 0.0 copy-start.6
  75.1 0.0 copy-done.5
  75.1 1.0 copy-done.6
  76.1 6.3 %attend_sides.1 = bf16[2,4,2,128,256]{4,3,2,1,0:T(8,128)(2,1)} custom-call(s32[144]{0:T(256)} %reshape.200.ok_ref, bf16[2,4,272,256]{3,2,1,0:T(8,128)(2,1)} %bitcast.39, bf16[4,2,2,128,256]{4,3,2,1,0:T(8,128)(2,1)} %copy-done.6, bf16[4,2,2,128,256]{4,3,2,1,0:T(8,128)(2,1)} %copy-done.5, f32[2,4,2,128,256]{4,3,2,1,0:T(8,128)} %get-tuple-element.23.acc_ref, ...), custom_call_target="tpu_custom_call" | custom-call | flops 805306368 | bytes 8388608 | tf_op jit(solution)/shard_map/attend_sides/pallas_call | solution.py:132
  82.4 18.4 %all_to_all.15 = bf16[8,2,128,256]{3,2,1,0:T(8,128)(2,1)S(1)} all-to-all(bf16[8,2,128,256]{3,2,1,0:T(8,128)(2,1)} %bitcast.44), channel_id=1, replica_groups={{0,8,16,24,1,9,17,25},{2,10,18,26,3,11,19,27},{4,12,20,28,5,13,21,29},{..., dimensions={0} | all-to-all | bytes 2097152 | tf_op jit(solution)/shard_map/all_to_all | solution.py:197
  100.8 0.6 copy.36
  101.4 1.3 %reshape.198 = bf16[2,1,128,2048]{3,2,1,0:T(8,128)(2,1)} reshape(bf16[2,128,8,256]{3,2,1,0:T(8,128)(2,1)S(1)} %copy.36) | data formatting | bytes 2097152 | tf_op jit(solution)/shard_map/reshape | solution.py:266
  (12 shorter events, 0.1 us)
Async XLA Ops:
  0.0 1.3 %copy-start.7 = (bf16[128,2048]{1,0:T(8,128)(2,1)S(1)}, bf16[128,2048]{1,0:T(8,128)(2,1)}, u32[]{:S(2)}) copy-start(bf16[128,2048]{1,0:T(8,128)(2,1)} %param.11) | copy-start | bytes 1572868
  1.2 2.0 %copy-start.2 = (bf16[2,1,128,2048]{3,2,1,0:T(8,128)(2,1)S(1)}, bf16[2,1,128,2048]{3,2,1,0:T(8,128)(2,1)}, u32[]{:S(2)}) copy-start(bf16[2,1,128,2048]{3,2,1,0:T(8,128)(2,1)} %param.7) | copy-start | bytes 3145732
  1.6 2.8 %copy-start.3 = (bf16[2,1,128,2048]{3,2,1,0:T(8,128)(2,1)S(1)}, bf16[2,1,128,2048]{3,2,1,0:T(8,128)(2,1)}, u32[]{:S(2)}) copy-start(bf16[2,1,128,2048]{3,2,1,0:T(8,128)(2,1)} %param.8) | copy-start | bytes 3145732
  1.6 5.5 %collective-permute-start = (bf16[2,128,256]{2,1,0:T(8,128)(2,1)S(1)}, bf16[2,128,256]{2,1,0:T(8,128)(2,1)S(1)}, u32[]{:S(2)}, u32[]{:S(2)}) collective-permute-start(bf16[2,128,256]{2,1,0:T(8,128)(2,1)S(1)} %get-tuple-element.28), channel_id=1, source_target_pairs={{0,1},{1,0},{2,3},{3,2},{4,5},{5,4},{6,7},{7,6},{8,9},{9,8},{10,11... | collective-permute-start | bytes 393224 | tf_op jit(solution)/shard_map/ppermute | solution.py:204
  7.1 3.8 %copy-start.10 = (s32[2,1,9]{2,1,0:T(1,128)S(1)}, s32[2,1,9]{2,1,0:T(1,128)}, u32[]{:S(2)}) copy-start(s32[2,1,9]{2,1,0:T(1,128)} %param.9) | copy-start | bytes 220
  7.1 10.5 %copy-start.4 = (bf16[2,1,128,2048]{3,2,1,0:T(8,128)(2,1)S(1)}, bf16[2,1,128,2048]{3,2,1,0:T(8,128)(2,1)}, u32[]{:S(2)}) copy-start(bf16[2,1,128,2048]{3,2,1,0:T(8,128)(2,1)} %param.6) | copy-start | bytes 3145732
  7.1 3.8 %copy-start.9 = (bf16[2,128,256]{2,1,0:T(8,128)(2,1)}, bf16[2,128,256]{2,1,0:T(8,128)(2,1)S(1)}, u32[]{:S(2)}) copy-start(bf16[2,128,256]{2,1,0:T(8,128)(2,1)S(1)} %collective-permute-done) | copy-start | bytes 393220
  7.2 30.6 %all-to-all-start = ((bf16[8,2,2,128,256]{4,3,2,1,0:T(8,128)(2,1)}), bf16[8,2,2,128,256]{4,3,2,1,0:T(8,128)(2,1)S(1)}, u32[]{:S(2)}, u32[]{:S(2)}) async-start(bf16[8,2,2,128,256]{4,3,2,1,0:T(8,128)(2,1)} %pad_maximum_fusion), calls=%async_computation | async-start | bytes 4194304 | tf_op jit(solution)/shard_map/all_to_all | solution.py:197
  11.9 8.3 %copy-start.8 = (bf16[2,2,128,256]{3,2,1,0:T(8,128)(2,1)}, bf16[2,2,128,256]{3,2,1,0:T(8,128)(2,1)S(1)}, u32[]{:S(2)}) copy-start(bf16[2,2,128,256]{3,2,1,0:T(8,128)(2,1)S(1)} %pad_maximum_fusion.2.refs_0_) | copy-start | bytes 786436
  11.9 9.4 %collective-permute-start.3 = (bf16[2,2,128,256]{3,2,1,0:T(8,128)(2,1)S(1)}, bf16[2,2,128,256]{3,2,1,0:T(8,128)(2,1)}, u32[]{:S(2)}, u32[]{:S(2)}) collective-permute-start(bf16[2,2,128,256]{3,2,1,0:T(8,128)(2,1)S(1)} %pad_maximum_fusion.2.refs_0_), channel_id=1, source_target_pairs={{0,6},{1,7},{2,0},{3,1},{4,2},{5,3},{6,4},{7,5},{8,14},{9,15},{10,... | collective-permute-start | bytes 786440 | tf_op jit(solution)/shard_map/ppermute | solution.py:210
  12.4 20.5 %collective-permute-start.2 = (bf16[2,2,128,256]{3,2,1,0:T(8,128)(2,1)S(1)}, bf16[2,2,128,256]{3,2,1,0:T(8,128)(2,1)}, u32[]{:S(2)}, u32[]{:S(2)}) collective-permute-start(bf16[2,2,128,256]{3,2,1,0:T(8,128)(2,1)S(1)} %pad_maximum_fusion.2.refs_0_), channel_id=1, source_target_pairs={{0,4},{1,5},{2,6},{3,7},{4,0},{5,1},{6,2},{7,3},{8,12},{9,13},{10,... | collective-permute-start | bytes 786440 | tf_op jit(solution)/shard_map/ppermute | solution.py:210
  15.0 22.7 %collective-permute-start.1 = (bf16[2,2,128,256]{3,2,1,0:T(8,128)(2,1)S(1)}, bf16[2,2,128,256]{3,2,1,0:T(8,128)(2,1)}, u32[]{:S(2)}, u32[]{:S(2)}) collective-permute-start(bf16[2,2,128,256]{3,2,1,0:T(8,128)(2,1)S(1)} %pad_maximum_fusion.2.refs_0_), channel_id=1, source_target_pairs={{0,2},{1,3},{2,4},{3,5},{4,6},{5,7},{6,0},{7,1},{8,10},{9,11},{10,... | collective-permute-start | bytes 786440 | tf_op jit(solution)/shard_map/ppermute | solution.py:210
  37.7 5.3 %copy-start = (bf16[8,2,2,128,256]{4,3,2,1,0:T(8,128)(2,1)}, bf16[8,2,2,128,256]{4,3,2,1,0:T(8,128)(2,1)S(1)}, u32[]{:S(2)}) copy-start(bf16[8,2,2,128,256]{4,3,2,1,0:T(8,128)(2,1)S(1)} %all-to-all-done) | copy-start | bytes 6291460
  39.1 19.0 %all-to-all-start.1 = ((bf16[8,272,256]{2,1,0:T(8,128)(2,1)}), bf16[8,272,256]{2,1,0:T(8,128)(2,1)S(1)}, u32[]{:S(2)}, u32[]{:S(2)}) async-start(bf16[8,272,256]{2,1,0:T(8,128)(2,1)} %copy.34), calls=%async_computation.1 | async-start | bytes 2228224 | tf_op jit(solution)/shard_map/all_to_all | solution.py:197
  44.5 29.0 %collective-permute-start.5 = (bf16[4,2,2,128,256]{4,3,2,1,0:T(8,128)(2,1)}, bf16[4,2,2,128,256]{4,3,2,1,0:T(8,128)(2,1)S(1)}, u32[]{:S(2)}, u32[]{:S(2)}) collective-permute-start(bf16[4,2,2,128,256]{4,3,2,1,0:T(8,128)(2,1)} %get-tuple-element.25), channel_id=1, source_target_pairs={{2,0},{3,1},{4,2},{5,3},{6,4},{7,5},{10,8},{11,9},{12,10},{13,11},... | collective-permute-start | bytes 3145736 | tf_op jit(solution)/shard_map/ppermute | solution.py:229
  47.7 27.4 %collective-permute-start.4 = (bf16[4,2,2,128,256]{4,3,2,1,0:T(8,128)(2,1)}, bf16[4,2,2,128,256]{4,3,2,1,0:T(8,128)(2,1)S(1)}, u32[]{:S(2)}, u32[]{:S(2)}) collective-permute-start(bf16[4,2,2,128,256]{4,3,2,1,0:T(8,128)(2,1)} %get-tuple-element.26), channel_id=1, source_target_pairs={{0,2},{1,3},{2,4},{3,5},{4,6},{5,7},{8,10},{9,11},{10,12},{11,13},... | collective-permute-start | bytes 3145736 | tf_op jit(solution)/shard_map/ppermute | solution.py:228
  58.2 1.0 copy-start.1
  73.6 1.5 %copy-start.5 = (bf16[4,2,2,128,256]{4,3,2,1,0:T(8,128)(2,1)}, bf16[4,2,2,128,256]{4,3,2,1,0:T(8,128)(2,1)S(1)}, u32[]{:S(2)}) copy-start(bf16[4,2,2,128,256]{4,3,2,1,0:T(8,128)(2,1)S(1)} %collective-permute-done.5.right_ref) | copy-start | bytes 3145732
  75.1 1.0 copy-start.6

commit v3 on v2

v3 whole, which is shorter than its diff:
```python
import functools

import jax
import jax.numpy as jnp
from jax import lax
from jax.experimental import pallas as pl
from jax.experimental.pallas import tpu as pltpu
from jax.sharding import PartitionSpec as P

HEADS = 16
HEAD_DIM = 128
LOG2_SCALE = HEAD_DIM ** (-0.5) * 1.4426950408889634


NT = (((1,), (1,)), ((), ()))
NOTE_ROWS = 32


def scores(a, b):
    return lax.dot_general(a, b, NT, preferred_element_type=jnp.float32)


def softmax_terms(pieces, masks, m):
    tiles = [s if ok is None else jnp.where(ok, s, -jnp.inf) for s, ok in zip(pieces, masks)]
    top = jnp.max(functools.reduce(jnp.maximum, tiles), axis=1, keepdims=True)
    m = top if m is None else jnp.maximum(m, top)
    powers, total = [], None
    for s in tiles:
        p = jnp.exp2((s - m) * LOG2_SCALE)
        total = p if total is None else total + p
        powers.append(p.astype(jnp.bfloat16))
    return m, jnp.sum(total, axis=1, keepdims=True), powers


def at_head(ref, h):
    return ref.at[..., h * HEAD_DIM : (h + 1) * HEAD_DIM]


class Band:
    def __init__(self, first, second, rows_in_band, tile):
        self.first, self.second, self.rows, self.tile = first, second, rows_in_band, tile
        self.cut = rows_in_band // 2

    def at(self, ref, band, n):
        return ref[band, n * self.tile : (n + 1) * self.tile]

    def key(self, band, sub):
        return self.at(self.first, band, sub)

    def value(self, band, sub):
        if sub < self.cut:
            return self.at(self.first, band, self.rows + sub)
        return self.at(self.second, band, sub - self.cut)

    def query(self, band, sub):
        return self.at(self.second, band, self.rows - self.cut + sub)

    def notes(self, band):
        start = (2 * self.rows - self.cut) * self.tile
        return self.second[band, start : start + NOTE_ROWS].astype(jnp.float32)


def attend_near(pad, rows_in_band, q_all, own_all, own_rest, *refs):
    far_all, acc_ref, stat_ref = refs[:-2], refs[-2], refs[-1]
    heads, _, rows, tile, _ = acc_ref.shape
    key_rows = own_all.shape[1] * rows_in_band
    lane = lax.broadcasted_iota(jnp.int32, (tile, tile), 1)
    for h in range(heads):
        own, qs_of = [
            [
                Band(at_head(first, h).at[x], at_head(second, h).at[x], rows_in_band, tile)
                for x in range(2)
            ]
            for first, second in ((own_all, own_rest), (own_all, q_all))
        ]
        shards = [at_head(f, h).at[c] for f in far_all for c in range(2)]
        stat = jnp.zeros((tile, tile), jnp.float32)
        for first in range(0, rows, rows_in_band):
            band = first // rows_in_band
            tiles = [(sub, x) for sub in range(rows_in_band) for x in range(2)]
            qs = [qs_of[x].query(band, sub) for sub, x in tiles]
            far = scores(jnp.concatenate(qs, 0), jnp.concatenate([f[0] for f in shards], 0))
            far_powers, near_sums = [], []
            for sub in range(rows_in_band):
                i = first + sub
                at = [(a, i + pad + a - 1) for a in range(3)]
                at = [(a, j // rows_in_band, j % rows_in_band) for a, j in at if 0 <= j < key_rows]
                window = [(a, kb, ks, x) for a, kb, ks in at for x in range(2)]
                near = scores(
                    jnp.concatenate(qs[2 * sub : 2 * sub + 2], 0),
                    jnp.concatenate([own[x].key(kb, ks) for _, kb, ks, x in window], 0),
                )
                near_powers = []
                for xq in range(2):
                    mine = slice((2 * sub + xq) * tile, (2 * sub + xq + 1) * tile)
                    pieces = [far[mine, n * tile : (n + 1) * tile] for n in range(len(shards))]
                    mine = slice(xq * tile, (xq + 1) * tile)
                    pieces += [near[mine, n * tile : (n + 1) * tile] for n in range(len(window))]
                    notes = qs_of[xq].notes(band)
                    masks = [None] * len(shards)
                    for a, _, _, x in window:
                        n = sub * 9 + (x ^ xq) * 3 + a
                        masks.append(None if x == xq and a == 1 else notes[n : n + 1] > 0)
                    m, total, powers = softmax_terms(pieces, masks, None)
                    far_powers.append(jnp.concatenate(powers[: len(shards)], 1))
                    near_powers.append(jnp.concatenate(powers[len(shards) :], 1))
                    n = i * 2 + xq
                    stat = jnp.where(lane == n, m, jnp.where(lane == n + tile // 2, total, stat))
                near_sums.append(
                    jnp.dot(
                        jnp.concatenate(near_powers, 0),
                        jnp.concatenate([own[x].value(kb, ks) for _, kb, ks, x in window], 0),
                        preferred_element_type=jnp.float32,
                    )
                )
            sums = jnp.dot(
                jnp.concatenate(far_powers, 0),
                jnp.concatenate([f[1] for f in shards], 0),
                preferred_element_type=jnp.float32,
            ) + jnp.concatenate(near_sums, 0)
            for u, (sub, x) in enumerate(tiles):
                acc_ref[h, x, first + sub] = sums[u * tile : (u + 1) * tile]
        stat_ref[h] = stat


def attend_sides(pad, rows_in_band, q_all, *refs):
    sides, (acc_ref, stat_ref, out_ref) = refs[:4], refs[4:]
    heads, _, rows, tile, _ = acc_ref.shape
    key_rows = sides[0].shape[0] * rows_in_band
    lane = lax.broadcasted_iota(jnp.int32, (tile, tile), 1)
    near_rows = [[i for i in range(rows) if abs(i + pad - j) <= 1] for j in range(key_rows)]
    near_rows = {j: found for j, found in enumerate(near_rows) if found}
    for h, xq in [(h, xq) for h in range(heads) for xq in range(2)]:
        stat = stat_ref[h]
        first, second = [at_head(a, h) for a in sides[2 * xq : 2 * xq + 2]]
        side = Band(first, second, rows_in_band, tile)
        mine = Band(None, at_head(q_all, h).at[xq], rows_in_band, tile)
        pieces = {}
        for j, found in near_rows.items():
            qs = [mine.query(i // rows_in_band, i % rows_in_band) for i in found]
            s = scores(jnp.concatenate(qs, 0), side.key(j // rows_in_band, j % rows_in_band))
            for u, i in enumerate(found):
                pieces[i, j] = s[u * tile : (u + 1) * tile]
        shrinks, totals = {}, {}
        for i in range(rows):
            n = i * 2 + xq
            m_near = jnp.max(jnp.where(lane == n, stat, -jnp.inf), axis=1, keepdims=True)
            near = jnp.max(jnp.where(lane == n + tile // 2, stat, -jnp.inf), axis=1, keepdims=True)
            at = [j for j in near_rows if (i, j) in pieces]
            notes = mine.notes(i // rows_in_band)
            masks = []
            for j in at:
                n = i % rows_in_band * 9 + 6 + j - i - pad + 1
                masks.append(notes[n : n + 1] > 0)
            m, total, powers = softmax_terms([pieces[i, j] for j in at], masks, m_near)
            for u, j in enumerate(at):
                pieces[i, j] = powers[u]
            shrinks[i] = jnp.exp2((m_near - m) * LOG2_SCALE)
            totals[i] = total + near * shrinks[i]
        more = {}
        for j, found in near_rows.items():
            o = jnp.dot(
                jnp.concatenate([pieces[i, j] for i in found], 0),
                side.value(j // rows_in_band, j % rows_in_band),
                preferred_element_type=jnp.float32,
            )
            for u, i in enumerate(found):
                o_i = o[u * tile : (u + 1) * tile]
                more[i] = more[i] + o_i if i in more else o_i
        for i in range(rows):
            out = (acc_ref[h, xq, i] * shrinks[i] + more[i]) / totals[i]
            band, start = i // rows_in_band, i % rows_in_band * tile
            out_ref[xq, band, start : start + tile, h * HEAD_DIM : (h + 1) * HEAD_DIM] = out.astype(
                out_ref.dtype
            )


VMEM = pl.BlockSpec(memory_space=pltpu.VMEM)


def call(kernel, name, operands, out_shape, tiles):
    flops = 4 * tiles * 128 * 128 * HEAD_DIM
    return pl.pallas_call(
        kernel,
        in_specs=[VMEM] * len(operands),
        out_specs=jax.tree.map(lambda _: VMEM, out_shape),
        out_shape=out_shape,
        compiler_params=pltpu.CompilerParams(vmem_limit_bytes=40 * 1024 * 1024),
        cost_estimate=pl.CostEstimate(
            flops=flops, bytes_accessed=4 * 1024 * 1024, transcendentals=flops // 512
        ),
        name=name,
    )(*operands)


def start_pack(pieces, out_ref, sem):
    part, copies, at = out_ref.shape[-1], [], 0
    for n, (ref, first, end) in enumerate(pieces):
        for p in range(out_ref.shape[0]):
            copies.append(
                pltpu.make_async_copy(
                    ref.at[first:end, p * part : (p + 1) * part],
                    out_ref.at[p, at : at + end - first],
                    sem.at[n * out_ref.shape[0] + p],
                )
            )
        at += end - first
    for copy in copies:
        copy.start()
    return copies, at


def pack_first(cut, k_ref, v_ref, out_ref, sem):
    for copy in start_pack(((k_ref, 0, k_ref.shape[0]), (v_ref, 0, cut)), out_ref, sem)[0]:
        copy.wait()


def pack_second(cut, row_size, col_size, flags_ref, v_ref, q_ref, out_ref, sem):
    rows = q_ref.shape[0]
    copies, at = start_pack(((v_ref, cut, rows), (q_ref, 0, rows)), out_ref, sem)
    row_at, col_at = lax.axis_index("row"), lax.axis_index("col")
    tiles = flags_ref.shape[0]
    line = lax.broadcasted_iota(jnp.int32, (NOTE_ROWS, out_ref.shape[-1]), 0)
    notes = jnp.zeros(line.shape, jnp.float32)
    inner = 1 - 2 * (col_at % 2)
    for t in range(tiles):
        for kind, b in enumerate((0, inner, -inner)):
            for a in range(3):
                row, col = row_at * tiles + t + a - 1, col_at + b
                ok = (row >= 0) & (row < row_size * tiles) & (col >= 0) & (col < col_size)
                if kind or a != 1:
                    ok = ok & (flags_ref[t, 0, a * 3 + 1 + b] > 0)
                notes = jnp.where(line == t * 9 + kind * 3 + a, jnp.where(ok, 1.0, 0.0), notes)
    notes = notes.astype(out_ref.dtype)
    for p in range(out_ref.shape[0]):
        out_ref[p, at:] = notes
    for copy in copies:
        copy.wait()


def packed(kernel, name, small, arrays, parts, rows):
    width = arrays[0].shape[1]
    return pl.pallas_call(
        kernel,
        in_specs=[pl.BlockSpec(memory_space=pltpu.SMEM)] * len(small)
        + [pl.BlockSpec(memory_space=pltpu.HBM)] * len(arrays),
        out_specs=VMEM,
        out_shape=jax.ShapeDtypeStruct(
            (parts, rows, width // parts), arrays[0].dtype
        ),
        scratch_shapes=[pltpu.SemaphoreType.DMA((len(arrays) * parts,))],
        compiler_params=pltpu.CompilerParams(vmem_limit_bytes=60 * 1024 * 1024),
        cost_estimate=pl.CostEstimate(flops=0, bytes_accessed=3 * 1024 * 1024, transcendentals=0),
        name=name,
    )(*small, *arrays)


def unpack(got_ref, out_ref):
    part = got_ref.shape[-1]
    for p in range(got_ref.shape[0]):
        out_ref[:, p * part : (p + 1) * part] = got_ref[p]


def moves(count, step):
    return [(i, i + step) for i in range(count) if 0 <= i + step < count]


def body(queries, fine_keys, fine_values, keep_flags, coarse_keys, coarse_values):
    rows_tiles, _, tile, width = queries.shape
    nrow, ncol = lax.axis_size("row"), lax.axis_size("col")
    band = min(4, nrow)
    planes = ncol // 2
    parts = band * 2
    part = width // parts
    rows = rows_tiles * tile
    row_at, col_at = lax.axis_index("row"), lax.axis_index("col")
    x_at, r_at = col_at % 2, row_at % band
    axes = ("row", "col")
    pad = 1 if nrow > band else 0
    groups = [
        [(g * band + r) * ncol + 2 * z + x for x in range(2) for r in range(band)]
        for g in range(nrow // band)
        for z in range(planes)
    ]

    def exchange(a):
        return lax.all_to_all(a, axes, 0, 0, axis_index_groups=groups, tiled=True)

    def coarse_of(x):
        at = (x * band + r_at) * part
        return jnp.stack(
            [lax.dynamic_slice_in_dim(c, at, part, 1) for c in (coarse_keys, coarse_values)]
        )

    here, away = coarse_of(x_at), coarse_of(1 - x_at)
    there = lax.ppermute(away, "col", [(c, c ^ 1) for c in range(ncol)])

    k, v, q = [a.reshape(rows, width) for a in (fine_keys, fine_values, queries)]
    cut = rows_tiles // 2 * tile
    sent = packed(functools.partial(pack_first, cut), "pack_first", (), (k, v), parts, rows + cut)
    sent, there = lax.optimization_barrier((sent, there))
    own = exchange(sent).reshape(2, band, rows + cut, part)
    pair = jnp.stack([here, there])
    far = [pair] + [
        lax.ppermute(pair, "col", [(c, (c + 2 * d) % ncol) for c in range(ncol)])
        for d in range(1, planes)
    ]

    def widen(a):
        line = a.reshape(band, 2, rows_tiles, tile, part)
        line = jnp.moveaxis(line, 1, 0).reshape(2, band * rows_tiles, tile, part)
        above = lax.ppermute(line[:, -1:], "row", moves(nrow, band))
        below = lax.ppermute(line[:, :1], "row", moves(nrow, -band))
        extra = [line[:, :1]] * ((-2) % rows_tiles)
        line = jnp.concatenate([above, line, below] + extra, 1)
        line = jnp.moveaxis(line.reshape(2, -1, rows_tiles, tile, part), 0, 1)
        return line.reshape(-1, 2 * rows, part)

    sent = packed(
        functools.partial(pack_second, cut, nrow, ncol),
        "pack_second",
        (keep_flags,),
        (v, q),
        parts,
        2 * rows - cut + NOTE_ROWS,
    )
    sent, far[2] = lax.optimization_barrier((sent, far[2]))
    q = exchange(sent).reshape(2, band, 2 * rows - cut + NOTE_ROWS, part)
    right_going, left_going = moves(ncol, 2), moves(ncol, -2)
    left, right = lax.ppermute(own[1], "col", right_going), lax.ppermute(own[0], "col", left_going)
    rest = q[:, :, : rows - cut]
    rest, far = lax.optimization_barrier((rest, far))
    left_rest = lax.ppermute(rest[1], "col", right_going)
    right_rest = lax.ppermute(rest[0], "col", left_going)
    own_rest = q
    if pad:

        def widened(first, second):
            both = widen(jnp.concatenate([first, second], 1))
            return both[:, : rows + cut], both[:, rows + cut :]

        left, left_rest = widened(left, left_rest)
        right, right_rest = widened(right, right_rest)
        wide = [widened(own[x], rest[x]) for x in range(2)]
        own, own_rest = jnp.stack([w[0] for w in wide]), jnp.stack([w[1] for w in wide])

    count, heads = band * rows_tiles, part // HEAD_DIM
    acc = jax.ShapeDtypeStruct((heads, 2, count, tile, HEAD_DIM), jnp.float32)
    stat = jax.ShapeDtypeStruct((heads, tile, tile), jnp.float32)
    acc, stat = call(
        functools.partial(attend_near, pad, rows_tiles),
        "attend_near",
        (q, own, own_rest, *far),
        (acc, stat),
        heads * 2 * count * (6 + 2 * planes),
    )
    out = call(
        functools.partial(attend_sides, pad, rows_tiles),
        "attend_sides",
        (q, left, left_rest, right, right_rest, acc, stat),
        jax.ShapeDtypeStruct((2, band, rows, part), queries.dtype),
        heads * 2 * count * 3,
    )
    out = exchange(out.reshape(parts, rows, part))
    out = call(unpack, "unpack", (out,), jax.ShapeDtypeStruct((rows, width), queries.dtype), 0)
    return out.reshape(queries.shape)


def solution(mesh):
    placed = (
        P("row", "col", None, None),
        P("row", "col", None, None),
        P("row", "col", None, None),
        P("row", "col", None),
        P("col", None),
        P("col", None),
    )
    return jax.shard_map(
        body, mesh=mesh, in_specs=placed, out_specs=P("row", "col", None, None), check_vma=False
    )
```

time: 104 us -> 98.4 us (0.946)
  local copies, waits for them, and re-layouts: 12 us -> 2.97 us
  starting transfers between devices: 21.2 us -> 26.2 us
  Pallas kernels: 20.7 us -> 25.1 us
  other arithmetic: 4.06 us -> 0.06 us
  blocking collectives: 18.4 us -> 17.1 us
    ppermute x3, waiting for transfers between devices: 17.5 us -> 8.26 us  [body(): lax.ppermute(pair, 'col', [(c, (c + 2 * d) % ncol) for c in range(ncol)])]
    all_to_all x2, waiting for transfers between devices: 7.09 us -> 16.3 us  [exchange(): return lax.all_to_all(a, axes, 0, 0, axis_index_groups=groups, tiled=True)]
    ppermute x2 -> x4, starting transfers between devices: 6.4 us -> 12.6 us  [the longest x1 3.48 us: body(): left_rest = lax.ppermute(rest[1], 'col', right_going)]
    pallas_call x2 -> x5, Pallas kernels: 20.7 us -> 25.1 us  [the longest x3 18.9 us: call(): pl.pallas_call(kernel, in_specs=[VMEM] * len(operands), out_specs=jax.tre...]
    unnamed x27 -> x4, local copies, waits for them, and re-layouts: 4.99 us -> 0.7 us
    reshape x4 -> x0, local copies, waits for them, and re-layouts: 2.19 us -> none  [the longest x1 1.31 us: body(): return jnp.moveaxis(out, 0, -2).reshape(queries.shape)]
    ppermute x2 -> x4, waiting for transfers between devices: 1.52 us -> 0.01 us  [the longest x1 0.01 us: body(): left_rest = lax.ppermute(rest[1], 'col', right_going)]
    another operation x1, other arithmetic: 1.53 us -> 0.02 us  [coarse_of(): jnp.stack([lax.dynamic_slice_in_dim(c, at, part, 1) for c in (coarse_keys...]
  transfers between devices with their start and end apart: 8 -> 10, of which waited for: 5 -> 4; matrix products, arithmetic and copies ran while one was open for 10% -> 1% of each run, Pallas kernels for 14% -> 19%
where the time goes in v3:
time: 98.4 us; the launch traced here: 97.1 us
  starting transfers between devices  26.2 us (27%)
  waiting for transfers between devices  25.6 us (26%)
  Pallas kernels  25.1 us (26%)
  blocking collectives  17.1 us (17%)
  local copies, waits for them, and re-layouts  2.97 us (3%)
    pallas_call x3, Pallas kernels, call(): pl.pallas_call(kernel, in_specs=[VMEM] * len(operands), out_specs=jax.tre...  18.9 us
    all_to_all x1, blocking collectives, exchange(): return lax.all_to_all(a, axes, 0, 0, axis_index_groups=groups, tiled=True)  17.1 us
    all_to_all x2, waiting for transfers between devices, exchange(): return lax.all_to_all(a, axes, 0, 0, axis_index_groups=groups, tiled=True)  16.3 us
    ppermute x3, waiting for transfers between devices, body(): lax.ppermute(pair, 'col', [(c, (c + 2 * d) % ncol) for c in range(ncol)])  8.26 us
    all_to_all x2, starting transfers between devices, exchange(): return lax.all_to_all(a, axes, 0, 0, axis_index_groups=groups, tiled=True)  7.31 us
    pallas_call x2, Pallas kernels, packed(): pl.pallas_call(kernel, in_specs=[pl.BlockSpec(memory_space=pltpu.SMEM)] *...  6.19 us
    ppermute x3, starting transfers between devices, body(): lax.ppermute(pair, 'col', [(c, (c + 2 * d) % ncol) for c in range(ncol)])  4.73 us
    ppermute x1, starting transfers between devices, body(): left_rest = lax.ppermute(rest[1], 'col', right_going)  3.48 us
  transfers between devices with their start and end apart: 10, of which 4 were waited for; matrix products, arithmetic and copies ran while one was open for 1% of the time, Pallas kernels for 19%

profile of v3, /device:TPU:8, one launch (start us, length us, event | category | flops | bytes accessed | tf_op | source)
XLA Modules:
  0.0 97.1 jit_solution(13478639240430793178)
XLA Ops:
  0.0 1.0 dynamic-slice_bitcast_fusion.2
  1.0 1.6 %collective-permute-start = (bf16[2,128,256]{2,1,0:T(8,128)(2,1)S(1)}, bf16[2,128,256]{2,1,0:T(8,128)(2,1)S(1)}, u32[]{:S(2)}, u32[]{:S(2)}) collective-permute-start(bf16[2,128,256]{2,1,0:T(8,128)(2,1)S(1)} %pad_maximum_fusion.1), channel_id=1, source_target_pairs={{0,1},{1,0},{2,3},{3,2},{4,5},{5,4},{6,7},{7,6},{8,9},{9,8},{10,11... | collective-permute-start | bytes 393224 | tf_op jit(solution)/shard_map/ppermute | solution.py:296
  2.5 2.7 %pack_first.1 = bf16[8,384,256]{2,1,0:T(8,128)(2,1)} custom-call(bf16[256,2048]{1,0:T(8,128)(2,1)} %bitcast.32, bf16[256,2048]{1,0:T(8,128)(2,1)} %bitcast.30), custom_call_target="tpu_custom_call" | custom-call | bytes 3145728 | tf_op jit(solution)/shard_map/pack_first/pallas_call | solution.py:243
  5.2 1.0 %collective-permute-done = bf16[2,128,256]{2,1,0:T(8,128)(2,1)S(1)} collective-permute-done((bf16[2,128,256]{2,1,0:T(8,128)(2,1)S(1)}, bf16[2,128,256]{2,1,0:T(8,128)(2,1)S(1)}, u32[]{:S(2)}, u32[]{:S(2)}) %collective-permute-start) | collective-permute-done | bytes 131104 | tf_op jit(solution)/shard_map/ppermute | solution.py:296
  6.3 3.7 %all-to-all-start.1 = ((bf16[8,384,256]{2,1,0:T(8,128)(2,1)}), bf16[8,384,256]{2,1,0:T(8,128)(2,1)S(1)}, u32[]{:S(2)}, u32[]{:S(2)}) async-start(bf16[8,384,256]{2,1,0:T(8,128)(2,1)} %pack_first.1), calls=%async_computation.1 | async-start | bytes 3145728 | tf_op jit(solution)/shard_map/all_to_all | solution.py:287
  10.1 2.7 %collective-permute-start.1 = (bf16[2,2,128,256]{3,2,1,0:T(8,128)(2,1)S(1)}, bf16[2,2,128,256]{3,2,1,0:T(8,128)(2,1)S(1)}, u32[]{:S(2)}, u32[]{:S(2)}) collective-permute-start(bf16[2,2,128,256]{3,2,1,0:T(8,128)(2,1)S(1)} %pad_maximum_fusion.refs_0_), channel_id=1, source_target_pairs={{0,4},{1,5},{2,6},{3,7},{4,0},{5,1},{6,2},{7,3},{8,12},{9,13},{10,... | collective-permute-start | bytes 786440 | tf_op jit(solution)/shard_map/ppermute | solution.py:305
  12.7 3.5 %pack_second.1 = bf16[8,416,256]{2,1,0:T(8,128)(2,1)} custom-call(s32[2,1,9]{2,1,0:T(1,128)} %flags_ref.1, bf16[256,2048]{1,0:T(8,128)(2,1)} %bitcast.31, bf16[256,2048]{1,0:T(8,128)(2,1)} %bitcast.33), custom_call_target="tpu_custom_call" | custom-call | bytes 3145728 | tf_op jit(solution)/shard_map/pack_second/pallas_call | solution.py:243
  16.2 8.3 %collective-permute-done.1.refs_2_ = bf16[2,2,128,256]{3,2,1,0:T(8,128)(2,1)S(1)} collective-permute-done((bf16[2,2,128,256]{3,2,1,0:T(8,128)(2,1)S(1)}, bf16[2,2,128,256]{3,2,1,0:T(8,128)(2,1)S(1)}, u32[]{:S(2)}, u32[]{:S(2)}) %collective-permute-start.1) | collective-permute-done | bytes 262176 | tf_op jit(solution)/shard_map/ppermute | solution.py:305
  24.5 0.0 copy-start
  24.5 0.7 copy-done
  25.2 4.9 %all-to-all-done.1 = bf16[8,384,256]{2,1,0:T(8,128)(2,1)S(1)} async-done(((bf16[8,384,256]{2,1,0:T(8,128)(2,1)}), bf16[8,384,256]{2,1,0:T(8,128)(2,1)S(1)}, u32[]{:S(2)}, u32[]{:S(2)}) %all-to-all-start.1) | async-done | bytes 1572896 | tf_op jit(solution)/shard_map/all_to_all | solution.py:287
  30.1 3.6 %all-to-all-start = ((bf16[8,416,256]{2,1,0:T(8,128)(2,1)}), bf16[8,416,256]{2,1,0:T(8,128)(2,1)S(1)}, u32[]{:S(2)}, u32[]{:S(2)}) async-start(bf16[8,416,256]{2,1,0:T(8,128)(2,1)} %pack_second.1), calls=%async_computation | async-start | bytes 3407872 | tf_op jit(solution)/shard_map/all_to_all | solution.py:287
  33.7 1.6 %collective-permute-start.3 = (bf16[2,2,128,256]{3,2,1,0:T(8,128)(2,1)S(1)}, bf16[2,2,128,256]{3,2,1,0:T(8,128)(2,1)}, u32[]{:S(2)}, u32[]{:S(2)}) collective-permute-start(bf16[2,2,128,256]{3,2,1,0:T(8,128)(2,1)S(1)} %pad_maximum_fusion.refs_0_), channel_id=1, source_target_pairs={{0,2},{1,3},{2,4},{3,5},{4,6},{5,7},{6,0},{7,1},{8,10},{9,11},{10,... | collective-permute-start | bytes 786440 | tf_op jit(solution)/shard_map/ppermute | solution.py:305
  35.3 0.4 collective-permute-start.4
  35.8 1.2 %fusion = (bf16[4,384,256]{2,1,0:T(8,128)(2,1)}, bf16[4,384,256]{2,1,0:T(8,128)(2,1)}) fusion(bf16[8,384,256]{2,1,0:T(8,128)(2,1)S(1)} %all-to-all-done.1), kind=kLoop, calls=%fused_computation.9 | loop fusion | bytes 3145728 | tf_op jit(solution)/shard_map/slice | solution.py:330
  37.0 3.5 %collective-permute-start.2 = (bf16[4,384,256]{2,1,0:T(8,128)(2,1)}, bf16[4,384,256]{2,1,0:T(8,128)(2,1)}, u32[]{:S(2)}, u32[]{:S(2)}) collective-permute-start(bf16[4,384,256]{2,1,0:T(8,128)(2,1)} %get-tuple-element.28), channel_id=1, source_target_pairs={{0,2},{1,3},{2,4},{3,5},{4,6},{5,7},{8,10},{9,11},{10,12},{11,13},... | collective-permute-start | bytes 2359304 | tf_op jit(solution)/shard_map/ppermute | solution.py:330
  40.5 3.2 %collective-permute-start.6 = (bf16[4,384,256]{2,1,0:T(8,128)(2,1)}, bf16[4,384,256]{2,1,0:T(8,128)(2,1)}, u32[]{:S(2)}, u32[]{:S(2)}) collective-permute-start(bf16[4,384,256]{2,1,0:T(8,128)(2,1)} %get-tuple-element.27), channel_id=1, source_target_pairs={{2,0},{3,1},{4,2},{5,3},{6,4},{7,5},{10,8},{11,9},{12,10},{13,11},... | collective-permute-start | bytes 2359304 | tf_op jit(solution)/shard_map/ppermute | solution.py:330
  43.7 11.3 %all-to-all-done = bf16[8,416,256]{2,1,0:T(8,128)(2,1)S(1)} async-done(((bf16[8,416,256]{2,1,0:T(8,128)(2,1)}), bf16[8,416,256]{2,1,0:T(8,128)(2,1)S(1)}, u32[]{:S(2)}, u32[]{:S(2)}) %all-to-all-start) | async-done | bytes 1703968 | tf_op jit(solution)/shard_map/all_to_all | solution.py:287
  55.1 0.0 copy-start.1
  55.1 0.0 collective-permute-done.3.refs_1_
  55.1 0.0 collective-permute-done.4.refs_3_
  55.2 3.5 %collective-permute-start.5 = (bf16[4,128,256]{2,1,0:T(8,128)(2,1)S(1)}, bf16[4,128,256]{2,1,0:T(8,128)(2,1)S(1)}, u32[]{:S(2)}, u32[]{:S(2)}) collective-permute-start(bf16[4,128,256]{2,1,0:T(8,128)(2,1)S(1)} %get-tuple-element.30), channel_id=1, source_target_pairs={{0,2},{1,3},{2,4},{3,5},{4,6},{5,7},{8,10},{9,11},{10,12},{11,13},... | collective-permute-start | bytes 786440 | tf_op jit(solution)/shard_map/ppermute | solution.py:333
  58.7 2.4 %collective-permute-start.7 = (bf16[4,128,256]{2,1,0:T(8,128)(2,1)S(1)}, bf16[4,128,256]{2,1,0:T(8,128)(2,1)S(1)}, u32[]{:S(2)}, u32[]{:S(2)}) collective-permute-start(bf16[4,128,256]{2,1,0:T(8,128)(2,1)S(1)} %get-tuple-element.29), channel_id=1, source_target_pairs={{2,0},{3,1},{4,2},{5,3},{6,4},{7,5},{10,8},{11,9},{12,10},{13,11},... | collective-permute-start | bytes 786440 | tf_op jit(solution)/shard_map/ppermute | solution.py:334
  61.1 0.0 copy-done.1
  61.1 12.4 %attend_near.1 = (f32[2,2,8,128,128]{4,3,2,1,0:T(8,128)S(1)}, f32[2,128,128]{2,1,0:T(8,128)S(1)}) custom-call(bf16[2,4,416,256]{3,2,1,0:T(8,128)(2,1)S(1)} %bitcast.25, bf16[2,4,384,256]{3,2,1,0:T(8,128)(2,1)S(1)} %bitcast.28, bf16[2,4,416,256]{3,2,1,0:T(8,128)(2,1)S(1)} %bitcast.26, bf16[2,2,128,256]{3,2,1,0:T(8,128)(2,1)S(1)} %pad_maximum_fusion.refs_0_, ...), custom_call_target="tpu_custom_call" | custom-call | flops 3758096384 | bytes 4194304 | tf_op jit(solution)/shard_map/attend_near/pallas_call | solution.py:183
  73.5 0.0 collective-permute-done.5.refs_1_
  73.5 0.0 collective-permute-done.7.refs_3_
  73.5 0.0 collective-permute-done.2.refs_0_
  73.5 0.0 collective-permute-done.6.refs_2_
  73.5 5.3 %attend_sides.1 = bf16[2,4,256,256]{3,2,1,0:T(8,128)(2,1)S(1)} custom-call(bf16[2,4,416,256]{3,2,1,0:T(8,128)(2,1)S(1)} %bitcast.27, bf16[4,384,256]{2,1,0:T(8,128)(2,1)} %collective-permute-done.2.refs_0_, bf16[4,128,256]{2,1,0:T(8,128)(2,1)S(1)} %collective-permute-done.5.refs_1_, bf16[4,384,256]{2,1,0:T(8,128)(2,1)} %collective-permute-done.6.refs_2_, ...), custom_call_target="tpu_custom_call" | custom-call | flops 805306368 | bytes 4194304 | tf_op jit(solution)/shard_map/attend_sides/pallas_call | solution.py:183
  78.9 17.1 %all_to_all.15.got_ref = bf16[8,256,256]{2,1,0:T(8,128)(2,1)S(1)} all-to-all(bf16[8,256,256]{2,1,0:T(8,128)(2,1)S(1)} %bitcast.29), channel_id=1, replica_groups={{0,8,16,24,1,9,17,25},{2,10,18,26,3,11,19,27},{4,12,20,28,5,13,21,29},{..., dimensions={0} | all-to-all | bytes 2097152 | tf_op jit(solution)/shard_map/all_to_all | solution.py:287
  96.0 1.1 %unpack.1 = bf16[256,2048]{1,0:T(8,128)(2,1)} custom-call(bf16[8,256,256]{2,1,0:T(8,128)(2,1)S(1)} %all_to_all.15.got_ref), custom_call_target="tpu_custom_call" | custom-call | bytes 4194304 | tf_op jit(solution)/shard_map/unpack/pallas_call | solution.py:183
  (5 shorter events, 0.1 us)
Async XLA Ops:
  1.0 5.3 %collective-permute-start = (bf16[2,128,256]{2,1,0:T(8,128)(2,1)S(1)}, bf16[2,128,256]{2,1,0:T(8,128)(2,1)S(1)}, u32[]{:S(2)}, u32[]{:S(2)}) collective-permute-start(bf16[2,128,256]{2,1,0:T(8,128)(2,1)S(1)} %pad_maximum_fusion.1), channel_id=1, source_target_pairs={{0,1},{1,0},{2,3},{3,2},{4,5},{5,4},{6,7},{7,6},{8,9},{9,8},{10,11... | collective-permute-start | bytes 393224 | tf_op jit(solution)/shard_map/ppermute | solution.py:296
  6.3 23.8 %all-to-all-start.1 = ((bf16[8,384,256]{2,1,0:T(8,128)(2,1)}), bf16[8,384,256]{2,1,0:T(8,128)(2,1)S(1)}, u32[]{:S(2)}, u32[]{:S(2)}) async-start(bf16[8,384,256]{2,1,0:T(8,128)(2,1)} %pack_first.1), calls=%async_computation.1 | async-start | bytes 3145728 | tf_op jit(solution)/shard_map/all_to_all | solution.py:287
  10.1 14.4 %collective-permute-start.1 = (bf16[2,2,128,256]{3,2,1,0:T(8,128)(2,1)S(1)}, bf16[2,2,128,256]{3,2,1,0:T(8,128)(2,1)S(1)}, u32[]{:S(2)}, u32[]{:S(2)}) collective-permute-start(bf16[2,2,128,256]{3,2,1,0:T(8,128)(2,1)S(1)} %pad_maximum_fusion.refs_0_), channel_id=1, source_target_pairs={{0,4},{1,5},{2,6},{3,7},{4,0},{5,1},{6,2},{7,3},{8,12},{9,13},{10,... | collective-permute-start | bytes 786440 | tf_op jit(solution)/shard_map/ppermute | solution.py:305
  24.5 0.7 copy-start
  30.1 25.0 %all-to-all-start = ((bf16[8,416,256]{2,1,0:T(8,128)(2,1)}), bf16[8,416,256]{2,1,0:T(8,128)(2,1)S(1)}, u32[]{:S(2)}, u32[]{:S(2)}) async-start(bf16[8,416,256]{2,1,0:T(8,128)(2,1)} %pack_second.1), calls=%async_computation | async-start | bytes 3407872 | tf_op jit(solution)/shard_map/all_to_all | solution.py:287
  33.7 21.4 %collective-permute-start.3 = (bf16[2,2,128,256]{3,2,1,0:T(8,128)(2,1)S(1)}, bf16[2,2,128,256]{3,2,1,0:T(8,128)(2,1)}, u32[]{:S(2)}, u32[]{:S(2)}) collective-permute-start(bf16[2,2,128,256]{3,2,1,0:T(8,128)(2,1)S(1)} %pad_maximum_fusion.refs_0_), channel_id=1, source_target_pairs={{0,2},{1,3},{2,4},{3,5},{4,6},{5,7},{6,0},{7,1},{8,10},{9,11},{10,... | collective-permute-start | bytes 786440 | tf_op jit(solution)/shard_map/ppermute | solution.py:305
  35.3 19.8 %collective-permute-start.4 = (bf16[2,2,128,256]{3,2,1,0:T(8,128)(2,1)S(1)}, bf16[2,2,128,256]{3,2,1,0:T(8,128)(2,1)}, u32[]{:S(2)}, u32[]{:S(2)}) collective-permute-start(bf16[2,2,128,256]{3,2,1,0:T(8,128)(2,1)S(1)} %pad_maximum_fusion.refs_0_), channel_id=1, source_target_pairs={{0,6},{1,7},{2,0},{3,1},{4,2},{5,3},{6,4},{7,5},{8,14},{9,15},{10,... | collective-permute-start | bytes 786440 | tf_op jit(solution)/shard_map/ppermute | solution.py:305
  37.0 36.5 %collective-permute-start.2 = (bf16[4,384,256]{2,1,0:T(8,128)(2,1)}, bf16[4,384,256]{2,1,0:T(8,128)(2,1)}, u32[]{:S(2)}, u32[]{:S(2)}) collective-permute-start(bf16[4,384,256]{2,1,0:T(8,128)(2,1)} %get-tuple-element.28), channel_id=1, source_target_pairs={{0,2},{1,3},{2,4},{3,5},{4,6},{5,7},{8,10},{9,11},{10,12},{11,13},... | collective-permute-start | bytes 2359304 | tf_op jit(solution)/shard_map/ppermute | solution.py:330
  40.5 33.0 %collective-permute-start.6 = (bf16[4,384,256]{2,1,0:T(8,128)(2,1)}, bf16[4,384,256]{2,1,0:T(8,128)(2,1)}, u32[]{:S(2)}, u32[]{:S(2)}) collective-permute-start(bf16[4,384,256]{2,1,0:T(8,128)(2,1)} %get-tuple-element.27), channel_id=1, source_target_pairs={{2,0},{3,1},{4,2},{5,3},{6,4},{7,5},{10,8},{11,9},{12,10},{13,11},... | collective-permute-start | bytes 2359304 | tf_op jit(solution)/shard_map/ppermute | solution.py:330
  55.1 6.0 %copy-start.1 = (bf16[2,2,128,256]{3,2,1,0:T(8,128)(2,1)S(1)}, bf16[2,2,128,256]{3,2,1,0:T(8,128)(2,1)}, u32[]{:S(2)}) copy-start(bf16[2,2,128,256]{3,2,1,0:T(8,128)(2,1)} %copy-done) | copy-start | bytes 786436
  55.2 18.3 %collective-permute-start.5 = (bf16[4,128,256]{2,1,0:T(8,128)(2,1)S(1)}, bf16[4,128,256]{2,1,0:T(8,128)(2,1)S(1)}, u32[]{:S(2)}, u32[]{:S(2)}) collective-permute-start(bf16[4,128,256]{2,1,0:T(8,128)(2,1)S(1)} %get-tuple-element.30), channel_id=1, source_target_pairs={{0,2},{1,3},{2,4},{3,5},{4,6},{5,7},{8,10},{9,11},{10,12},{11,13},... | collective-permute-start | bytes 786440 | tf_op jit(solution)/shard_map/ppermute | solution.py:333
  58.7 14.8 %collective-permute-start.7 = (bf16[4,128,256]{2,1,0:T(8,128)(2,1)S(1)}, bf16[4,128,256]{2,1,0:T(8,128)(2,1)S(1)}, u32[]{:S(2)}, u32[]{:S(2)}) collective-permute-start(bf16[4,128,256]{2,1,0:T(8,128)(2,1)S(1)} %get-tuple-element.29), channel_id=1, source_target_pairs={{2,0},{3,1},{4,2},{5,3},{6,4},{7,5},{10,8},{11,9},{12,10},{13,11},... | collective-permute-start | bytes 786440 | tf_op jit(solution)/shard_map/ppermute | solution.py:334

commit v4 on v3

--- a/solution.py
+++ b/solution.py
@@ -13,7 +13,7 @@
 
 
 NT = (((1,), (1,)), ((), ()))
-NOTE_ROWS = 32
+NOTE_ROWS = 16
 
 
 def scores(a, b):
@@ -37,8 +37,9 @@
 
 
 class Band:
-    def __init__(self, first, second, rows_in_band, tile):
+    def __init__(self, first, second, rows_in_band, tile, whole=None):
         self.first, self.second, self.rows, self.tile = first, second, rows_in_band, tile
+        self.whole = whole
         self.cut = rows_in_band // 2
 
     def at(self, ref, band, n):
@@ -55,9 +56,10 @@
     def query(self, band, sub):
         return self.at(self.second, band, self.rows - self.cut + sub)
 
-    def notes(self, band):
-        start = (2 * self.rows - self.cut) * self.tile
-        return self.second[band, start : start + NOTE_ROWS].astype(jnp.float32)
+    def notes(self, band, sub):
+        start, lane = (2 * self.rows - self.cut) * self.tile, sub * HEAD_DIM
+        notes = self.whole[band, start : start + NOTE_ROWS, lane : lane + HEAD_DIM]
+        return notes.astype(jnp.float32)
 
 
 def attend_near(pad, rows_in_band, q_all, own_all, own_rest, *refs):
@@ -68,7 +70,7 @@
     for h in range(heads):
         own, qs_of = [
             [
-                Band(at_head(first, h).at[x], at_head(second, h).at[x], rows_in_band, tile)
+                Band(at_head(first, h).at[x], at_head(second, h).at[x], rows_in_band, tile, q_all.at[x])
                 for x in range(2)
             ]
             for first, second in ((own_all, own_rest), (own_all, q_all))
@@ -96,10 +98,10 @@
                     pieces = [far[mine, n * tile : (n + 1) * tile] for n in range(len(shards))]
                     mine = slice(xq * tile, (xq + 1) * tile)
                     pieces += [near[mine, n * tile : (n + 1) * tile] for n in range(len(window))]
-                    notes = qs_of[xq].notes(band)
+                    notes = qs_of[xq].notes(band, sub)
                     masks = [None] * len(shards)
                     for a, _, _, x in window:
-                        n = sub * 9 + (x ^ xq) * 3 + a
+                        n = (x ^ xq) * 3 + a
                         masks.append(None if x == xq and a == 1 else notes[n : n + 1] > 0)
                     m, total, powers = softmax_terms(pieces, masks, None)
                     far_powers.append(jnp.concatenate(powers[: len(shards)], 1))
@@ -124,17 +126,26 @@
 
 
 def attend_sides(pad, rows_in_band, q_all, *refs):
-    sides, (acc_ref, stat_ref, out_ref) = refs[:4], refs[4:]
+    far_sides, (acc_ref, stat_ref, out_ref), sides, sem = refs[:4], refs[4:7], refs[7:11], refs[11]
+    copies = [
+        pltpu.make_async_copy(source, target, sem.at[n])
+        for n, (source, target) in enumerate(zip(far_sides, sides))
+    ]
+    for copy in copies:
+        copy.start()
     heads, _, rows, tile, _ = acc_ref.shape
     key_rows = sides[0].shape[0] * rows_in_band
     lane = lax.broadcasted_iota(jnp.int32, (tile, tile), 1)
     near_rows = [[i for i in range(rows) if abs(i + pad - j) <= 1] for j in range(key_rows)]
     near_rows = {j: found for j, found in enumerate(near_rows) if found}
-    for h, xq in [(h, xq) for h in range(heads) for xq in range(2)]:
+    for h, xq in [(h, xq) for xq in range(2) for h in range(heads)]:
+        if h == 0:
+            copies[2 * xq].wait()
+            copies[2 * xq + 1].wait()
         stat = stat_ref[h]
         first, second = [at_head(a, h) for a in sides[2 * xq : 2 * xq + 2]]
         side = Band(first, second, rows_in_band, tile)
-        mine = Band(None, at_head(q_all, h).at[xq], rows_in_band, tile)
+        mine = Band(None, at_head(q_all, h).at[xq], rows_in_band, tile, q_all.at[xq])
         pieces = {}
         for j, found in near_rows.items():
             qs = [mine.query(i // rows_in_band, i % rows_in_band) for i in found]
@@ -147,10 +158,10 @@
             m_near = jnp.max(jnp.where(lane == n, stat, -jnp.inf), axis=1, keepdims=True)
             near = jnp.max(jnp.where(lane == n + tile // 2, stat, -jnp.inf), axis=1, keepdims=True)
             at = [j for j in near_rows if (i, j) in pieces]
-            notes = mine.notes(i // rows_in_band)
+            notes = mine.notes(i // rows_in_band, i % rows_in_band)
             masks = []
             for j in at:
-                n = i % rows_in_band * 9 + 6 + j - i - pad + 1
+                n = 6 + j - i - pad + 1
                 masks.append(notes[n : n + 1] > 0)
             m, total, powers = softmax_terms([pieces[i, j] for j in at], masks, m_near)
             for u, j in enumerate(at):
@@ -178,13 +189,14 @@
 VMEM = pl.BlockSpec(memory_space=pltpu.VMEM)
 
 
-def call(kernel, name, operands, out_shape, tiles):
+def call(kernel, name, operands, out_shape, tiles, specs=None, scratch=()):
     flops = 4 * tiles * 128 * 128 * HEAD_DIM
     return pl.pallas_call(
         kernel,
-        in_specs=[VMEM] * len(operands),
+        in_specs=specs or [VMEM] * len(operands),
         out_specs=jax.tree.map(lambda _: VMEM, out_shape),
         out_shape=out_shape,
+        scratch_shapes=scratch,
         compiler_params=pltpu.CompilerParams(vmem_limit_bytes=40 * 1024 * 1024),
         cost_estimate=pl.CostEstimate(
             flops=flops, bytes_accessed=4 * 1024 * 1024, transcendentals=flops // 512
@@ -220,20 +232,22 @@
     copies, at = start_pack(((v_ref, cut, rows), (q_ref, 0, rows)), out_ref, sem)
     row_at, col_at = lax.axis_index("row"), lax.axis_index("col")
     tiles = flags_ref.shape[0]
-    line = lax.broadcasted_iota(jnp.int32, (NOTE_ROWS, out_ref.shape[-1]), 0)
-    notes = jnp.zeros(line.shape, jnp.float32)
+    line = lax.broadcasted_iota(jnp.int32, (NOTE_ROWS, HEAD_DIM), 0)
+    blocks = []
     inner = 1 - 2 * (col_at % 2)
     for t in range(tiles):
+        notes = jnp.zeros(line.shape, jnp.float32)
         for kind, b in enumerate((0, inner, -inner)):
             for a in range(3):
                 row, col = row_at * tiles + t + a - 1, col_at + b
                 ok = (row >= 0) & (row < row_size * tiles) & (col >= 0) & (col < col_size)
                 if kind or a != 1:
                     ok = ok & (flags_ref[t, 0, a * 3 + 1 + b] > 0)
-                notes = jnp.where(line == t * 9 + kind * 3 + a, jnp.where(ok, 1.0, 0.0), notes)
-    notes = notes.astype(out_ref.dtype)
+                notes = jnp.where(line == kind * 3 + a, jnp.where(ok, 1.0, 0.0), notes)
+        blocks.append(notes.astype(out_ref.dtype))
     for p in range(out_ref.shape[0]):
-        out_ref[p, at:] = notes
+        for t, notes in enumerate(blocks):
+            out_ref[p, at:, t * HEAD_DIM : (t + 1) * HEAD_DIM] = notes
     for copy in copies:
         copy.wait()
 
@@ -354,12 +368,15 @@
         (acc, stat),
         heads * 2 * count * (6 + 2 * planes),
     )
+    sides = (left, left_rest, right, right_rest)
     out = call(
         functools.partial(attend_sides, pad, rows_tiles),
         "attend_sides",
-        (q, left, left_rest, right, right_rest, acc, stat),
+        (q, *sides, acc, stat),
         jax.ShapeDtypeStruct((2, band, rows, part), queries.dtype),
         heads * 2 * count * 3,
+        [VMEM] + [pl.BlockSpec(memory_space=pl.ANY)] * 4 + [VMEM] * 2,
+        [pltpu.VMEM(a.shape, a.dtype) for a in sides] + [pltpu.SemaphoreType.DMA((4,))],
     )
     out = exchange(out.reshape(parts, rows, part))
     out = call(unpack, "unpack", (out,), jax.ShapeDtypeStruct((rows, width), queries.dtype), 0)

time: 98.4 us -> 97.3 us (0.989)
  Pallas kernels: 25.1 us -> 24 us
    pallas_call x3, Pallas kernels: 18.9 us -> 17.8 us  [call(): pl.pallas_call(kernel, in_specs=specs or [VMEM] * len(operands), out_spec...]
where the time goes in v4:
time: 97.3 us; the launch traced here: 95.4 us
  starting transfers between devices  26.2 us (27%)
  waiting for transfers between devices  24.9 us (26%)
  Pallas kernels  24 us (25%)
  blocking collectives  17.1 us (18%)
  local copies, waits for them, and re-layouts  2.96 us (3%)
    pallas_call x3, Pallas kernels, call(): pl.pallas_call(kernel, in_specs=specs or [VMEM] * len(operands), out_spec...  17.8 us
    all_to_all x1, blocking collectives, exchange(): return lax.all_to_all(a, axes, 0, 0, axis_index_groups=groups, tiled=True)  17.1 us
    all_to_all x2, waiting for transfers between devices, exchange(): return lax.all_to_all(a, axes, 0, 0, axis_index_groups=groups, tiled=True)  15.6 us
    ppermute x3, waiting for transfers between devices, body(): lax.ppermute(pair, 'col', [(c, (c + 2 * d) % ncol) for c in range(ncol)])  8.28 us
    all_to_all x2, starting transfers between devices, exchange(): return lax.all_to_all(a, axes, 0, 0, axis_index_groups=groups, tiled=True)  7.31 us
    pallas_call x2, Pallas kernels, packed(): pl.pallas_call(kernel, in_specs=[pl.BlockSpec(memory_space=pltpu.SMEM)] *...  6.16 us
    ppermute x3, starting transfers between devices, body(): lax.ppermute(pair, 'col', [(c, (c + 2 * d) % ncol) for c in range(ncol)])  4.73 us
    ppermute x1, starting transfers between devices, body(): left_rest = lax.ppermute(rest[1], 'col', right_going)  3.48 us
  transfers between devices with their start and end apart: 10, of which 4 were waited for; matrix products, arithmetic and copies ran while one was open for 1% of the time, Pallas kernels for 19%

profile of v4, /device:TPU:8, one launch (start us, length us, event | category | flops | bytes accessed | tf_op | source)
XLA Modules:
  0.0 95.4 jit_solution(9161652524612266445)
XLA Ops:
  0.0 1.0 %dynamic-slice_bitcast_fusion.2 = (bf16[1,128,256]{2,1,0:T(8,128)(2,1)S(1)}, bf16[1,128,256]{2,1,0:T(8,128)(2,1)S(1)}, bf16[1,128,256]{2,1,0:T(8,128)(2,1)S(1)}, bf16[1,128,256]{2,1,0:T(8,128)(2,1)S(1)}) fusion(bf16[128,2048]{1,0:T(8,128)(2,1)} %param.11, s32[]{:T(128)S(6)} %select_n.21, s32[]{:T(128)S(6)} %select_n.22, bf16[128,2048]{1,0:T(8,128)(2,1)} %param.10), kind=kLoop, calls=%fused_computation.7 | loop fusion | bytes 524296 | tf_op jit(solution)/shard_map/stack | solution.py:305
  1.0 1.6 %collective-permute-start = (bf16[2,128,256]{2,1,0:T(8,128)(2,1)S(1)}, bf16[2,128,256]{2,1,0:T(8,128)(2,1)S(1)}, u32[]{:S(2)}, u32[]{:S(2)}) collective-permute-start(bf16[2,128,256]{2,1,0:T(8,128)(2,1)S(1)} %pad_maximum_fusion.1), channel_id=1, source_target_pairs={{0,1},{1,0},{2,3},{3,2},{4,5},{5,4},{6,7},{7,6},{8,9},{9,8},{10,11... | collective-permute-start | bytes 393224 | tf_op jit(solution)/shard_map/ppermute | solution.py:310
  2.5 2.7 %pack_first.1 = bf16[8,384,256]{2,1,0:T(8,128)(2,1)} custom-call(bf16[256,2048]{1,0:T(8,128)(2,1)} %bitcast.32, bf16[256,2048]{1,0:T(8,128)(2,1)} %bitcast.30), custom_call_target="tpu_custom_call" | custom-call | bytes 3145728 | tf_op jit(solution)/shard_map/pack_first/pallas_call | solution.py:257
  5.2 1.1 %collective-permute-done = bf16[2,128,256]{2,1,0:T(8,128)(2,1)S(1)} collective-permute-done((bf16[2,128,256]{2,1,0:T(8,128)(2,1)S(1)}, bf16[2,128,256]{2,1,0:T(8,128)(2,1)S(1)}, u32[]{:S(2)}, u32[]{:S(2)}) %collective-permute-start) | collective-permute-done | bytes 131104 | tf_op jit(solution)/shard_map/ppermute | solution.py:310
  6.3 3.7 %all-to-all-start.1 = ((bf16[8,384,256]{2,1,0:T(8,128)(2,1)}), bf16[8,384,256]{2,1,0:T(8,128)(2,1)S(1)}, u32[]{:S(2)}, u32[]{:S(2)}) async-start(bf16[8,384,256]{2,1,0:T(8,128)(2,1)} %pack_first.1), calls=%async_computation.1 | async-start | bytes 3145728 | tf_op jit(solution)/shard_map/all_to_all | solution.py:301
  10.1 2.7 %collective-permute-start.1 = (bf16[2,2,128,256]{3,2,1,0:T(8,128)(2,1)S(1)}, bf16[2,2,128,256]{3,2,1,0:T(8,128)(2,1)S(1)}, u32[]{:S(2)}, u32[]{:S(2)}) collective-permute-start(bf16[2,2,128,256]{3,2,1,0:T(8,128)(2,1)S(1)} %pad_maximum_fusion.refs_0_), channel_id=1, source_target_pairs={{0,4},{1,5},{2,6},{3,7},{4,0},{5,1},{6,2},{7,3},{8,12},{9,13},{10,... | collective-permute-start | bytes 786440 | tf_op jit(solution)/shard_map/ppermute | solution.py:319
  12.7 3.5 %pack_second.1 = bf16[8,400,256]{2,1,0:T(8,128)(2,1)} custom-call(s32[2,1,9]{2,1,0:T(1,128)} %flags_ref.1, bf16[256,2048]{1,0:T(8,128)(2,1)} %bitcast.31, bf16[256,2048]{1,0:T(8,128)(2,1)} %bitcast.33), custom_call_target="tpu_custom_call" | custom-call | bytes 3145728 | tf_op jit(solution)/shard_map/pack_second/pallas_call | solution.py:257
  16.2 8.3 %collective-permute-done.1.refs_2_ = bf16[2,2,128,256]{3,2,1,0:T(8,128)(2,1)S(1)} collective-permute-done((bf16[2,2,128,256]{3,2,1,0:T(8,128)(2,1)S(1)}, bf16[2,2,128,256]{3,2,1,0:T(8,128)(2,1)S(1)}, u32[]{:S(2)}, u32[]{:S(2)}) %collective-permute-start.1) | collective-permute-done | bytes 262176 | tf_op jit(solution)/shard_map/ppermute | solution.py:319
  24.5 0.0 copy-start
  24.5 0.7 copy-done
  25.2 4.9 %all-to-all-done.1 = bf16[8,384,256]{2,1,0:T(8,128)(2,1)S(1)} async-done(((bf16[8,384,256]{2,1,0:T(8,128)(2,1)}), bf16[8,384,256]{2,1,0:T(8,128)(2,1)S(1)}, u32[]{:S(2)}, u32[]{:S(2)}) %all-to-all-start.1) | async-done | bytes 1572896 | tf_op jit(solution)/shard_map/all_to_all | solution.py:301
  30.1 3.6 %all-to-all-start = ((bf16[8,400,256]{2,1,0:T(8,128)(2,1)}), bf16[8,400,256]{2,1,0:T(8,128)(2,1)S(1)}, u32[]{:S(2)}, u32[]{:S(2)}) async-start(bf16[8,400,256]{2,1,0:T(8,128)(2,1)} %pack_second.1), calls=%async_computation | async-start | bytes 3276800 | tf_op jit(solution)/shard_map/all_to_all | solution.py:301
  33.7 1.6 %collective-permute-start.3 = (bf16[2,2,128,256]{3,2,1,0:T(8,128)(2,1)S(1)}, bf16[2,2,128,256]{3,2,1,0:T(8,128)(2,1)}, u32[]{:S(2)}, u32[]{:S(2)}) collective-permute-start(bf16[2,2,128,256]{3,2,1,0:T(8,128)(2,1)S(1)} %pad_maximum_fusion.refs_0_), channel_id=1, source_target_pairs={{0,2},{1,3},{2,4},{3,5},{4,6},{5,7},{6,0},{7,1},{8,10},{9,11},{10,... | collective-permute-start | bytes 786440 | tf_op jit(solution)/shard_map/ppermute | solution.py:319
  35.3 0.4 collective-permute-start.4
  35.8 1.2 %fusion = (bf16[4,384,256]{2,1,0:T(8,128)(2,1)}, bf16[4,384,256]{2,1,0:T(8,128)(2,1)}) fusion(bf16[8,384,256]{2,1,0:T(8,128)(2,1)S(1)} %all-to-all-done.1), kind=kLoop, calls=%fused_computation.9 | loop fusion | bytes 3145728 | tf_op jit(solution)/shard_map/slice | solution.py:344
  37.0 3.5 %collective-permute-start.2 = (bf16[4,384,256]{2,1,0:T(8,128)(2,1)}, bf16[4,384,256]{2,1,0:T(8,128)(2,1)}, u32[]{:S(2)}, u32[]{:S(2)}) collective-permute-start(bf16[4,384,256]{2,1,0:T(8,128)(2,1)} %get-tuple-element.28), channel_id=1, source_target_pairs={{0,2},{1,3},{2,4},{3,5},{4,6},{5,7},{8,10},{9,11},{10,12},{11,13},... | collective-permute-start | bytes 2359304 | tf_op jit(solution)/shard_map/ppermute | solution.py:344
  40.5 3.2 %collective-permute-start.6 = (bf16[4,384,256]{2,1,0:T(8,128)(2,1)}, bf16[4,384,256]{2,1,0:T(8,128)(2,1)}, u32[]{:S(2)}, u32[]{:S(2)}) collective-permute-start(bf16[4,384,256]{2,1,0:T(8,128)(2,1)} %get-tuple-element.27), channel_id=1, source_target_pairs={{2,0},{3,1},{4,2},{5,3},{6,4},{7,5},{10,8},{11,9},{12,10},{13,11},... | collective-permute-start | bytes 2359304 | tf_op jit(solution)/shard_map/ppermute | solution.py:344
  43.7 10.7 %all-to-all-done = bf16[8,400,256]{2,1,0:T(8,128)(2,1)S(1)} async-done(((bf16[8,400,256]{2,1,0:T(8,128)(2,1)}), bf16[8,400,256]{2,1,0:T(8,128)(2,1)S(1)}, u32[]{:S(2)}, u32[]{:S(2)}) %all-to-all-start) | async-done | bytes 1638432 | tf_op jit(solution)/shard_map/all_to_all | solution.py:301
  54.4 0.0 copy-start.1
  54.4 0.0 collective-permute-done.3.refs_1_
  54.4 0.0 collective-permute-done.4.refs_3_
  54.5 3.5 %collective-permute-start.5 = (bf16[4,128,256]{2,1,0:T(8,128)(2,1)S(1)}, bf16[4,128,256]{2,1,0:T(8,128)(2,1)S(1)}, u32[]{:S(2)}, u32[]{:S(2)}) collective-permute-start(bf16[4,128,256]{2,1,0:T(8,128)(2,1)S(1)} %get-tuple-element.30), channel_id=1, source_target_pairs={{0,2},{1,3},{2,4},{3,5},{4,6},{5,7},{8,10},{9,11},{10,12},{11,13},... | collective-permute-start | bytes 786440 | tf_op jit(solution)/shard_map/ppermute | solution.py:347
  58.0 2.4 %collective-permute-start.7 = (bf16[4,128,256]{2,1,0:T(8,128)(2,1)S(1)}, bf16[4,128,256]{2,1,0:T(8,128)(2,1)S(1)}, u32[]{:S(2)}, u32[]{:S(2)}) collective-permute-start(bf16[4,128,256]{2,1,0:T(8,128)(2,1)S(1)} %get-tuple-element.29), channel_id=1, source_target_pairs={{2,0},{3,1},{4,2},{5,3},{6,4},{7,5},{10,8},{11,9},{12,10},{13,11},... | collective-permute-start | bytes 786440 | tf_op jit(solution)/shard_map/ppermute | solution.py:348
  60.4 0.0 copy-done.1
  60.4 12.4 %attend_near.1 = (f32[2,2,8,128,128]{4,3,2,1,0:T(8,128)S(1)}, f32[2,128,128]{2,1,0:T(8,128)S(1)}) custom-call(bf16[2,4,400,256]{3,2,1,0:T(8,128)(2,1)S(1)} %bitcast.25, bf16[2,4,384,256]{3,2,1,0:T(8,128)(2,1)S(1)} %bitcast.28, bf16[2,4,400,256]{3,2,1,0:T(8,128)(2,1)S(1)} %bitcast.26, bf16[2,2,128,256]{3,2,1,0:T(8,128)(2,1)S(1)} %pad_maximum_fusion.refs_0_, ...), custom_call_target="tpu_custom_call" | custom-call | flops 3758096384 | bytes 4194304 | tf_op jit(solution)/shard_map/attend_near/pallas_call | solution.py:194
  72.8 0.0 collective-permute-done.5.refs_1_
  72.8 0.0 collective-permute-done.7.refs_3_
  72.8 0.0 collective-permute-done.2.refs_0_
  72.8 0.0 collective-permute-done.6.refs_2_
  72.8 4.3 %attend_sides.1 = bf16[2,4,256,256]{3,2,1,0:T(8,128)(2,1)S(1)} custom-call(bf16[2,4,400,256]{3,2,1,0:T(8,128)(2,1)S(1)} %bitcast.27, bf16[4,384,256]{2,1,0:T(8,128)(2,1)} %collective-permute-done.2.refs_0_, bf16[4,128,256]{2,1,0:T(8,128)(2,1)S(1)} %collective-permute-done.5.refs_1_, bf16[4,384,256]{2,1,0:T(8,128)(2,1)} %collective-permute-done.6.refs_2_, ...), custom_call_target="tpu_custom_call" | custom-call | flops 805306368 | bytes 4194304 | tf_op jit(solution)/shard_map/attend_sides/pallas_call | solution.py:194
  77.1 17.1 %all_to_all.15.got_ref = bf16[8,256,256]{2,1,0:T(8,128)(2,1)S(1)} all-to-all(bf16[8,256,256]{2,1,0:T(8,128)(2,1)S(1)} %bitcast.29), channel_id=1, replica_groups={{0,8,16,24,1,9,17,25},{2,10,18,26,3,11,19,27},{4,12,20,28,5,13,21,29},{..., dimensions={0} | all-to-all | bytes 2097152 | tf_op jit(solution)/shard_map/all_to_all | solution.py:301
  94.3 1.1 %unpack.1 = bf16[256,2048]{1,0:T(8,128)(2,1)} custom-call(bf16[8,256,256]{2,1,0:T(8,128)(2,1)S(1)} %all_to_all.15.got_ref), custom_call_target="tpu_custom_call" | custom-call | bytes 4194304 | tf_op jit(solution)/shard_map/unpack/pallas_call | solution.py:194
  (5 shorter events, 0.1 us)
Async XLA Ops:
  1.0 5.3 %collective-permute-start = (bf16[2,128,256]{2,1,0:T(8,128)(2,1)S(1)}, bf16[2,128,256]{2,1,0:T(8,128)(2,1)S(1)}, u32[]{:S(2)}, u32[]{:S(2)}) collective-permute-start(bf16[2,128,256]{2,1,0:T(8,128)(2,1)S(1)} %pad_maximum_fusion.1), channel_id=1, source_target_pairs={{0,1},{1,0},{2,3},{3,2},{4,5},{5,4},{6,7},{7,6},{8,9},{9,8},{10,11... | collective-permute-start | bytes 393224 | tf_op jit(solution)/shard_map/ppermute | solution.py:310
  6.3 23.8 %all-to-all-start.1 = ((bf16[8,384,256]{2,1,0:T(8,128)(2,1)}), bf16[8,384,256]{2,1,0:T(8,128)(2,1)S(1)}, u32[]{:S(2)}, u32[]{:S(2)}) async-start(bf16[8,384,256]{2,1,0:T(8,128)(2,1)} %pack_first.1), calls=%async_computation.1 | async-start | bytes 3145728 | tf_op jit(solution)/shard_map/all_to_all | solution.py:301
  10.1 14.4 %collective-permute-start.1 = (bf16[2,2,128,256]{3,2,1,0:T(8,128)(2,1)S(1)}, bf16[2,2,128,256]{3,2,1,0:T(8,128)(2,1)S(1)}, u32[]{:S(2)}, u32[]{:S(2)}) collective-permute-start(bf16[2,2,128,256]{3,2,1,0:T(8,128)(2,1)S(1)} %pad_maximum_fusion.refs_0_), channel_id=1, source_target_pairs={{0,4},{1,5},{2,6},{3,7},{4,0},{5,1},{6,2},{7,3},{8,12},{9,13},{10,... | collective-permute-start | bytes 786440 | tf_op jit(solution)/shard_map/ppermute | solution.py:319
  24.5 0.7 copy-start
  30.1 24.3 %all-to-all-start = ((bf16[8,400,256]{2,1,0:T(8,128)(2,1)}), bf16[8,400,256]{2,1,0:T(8,128)(2,1)S(1)}, u32[]{:S(2)}, u32[]{:S(2)}) async-start(bf16[8,400,256]{2,1,0:T(8,128)(2,1)} %pack_second.1), calls=%async_computation | async-start | bytes 3276800 | tf_op jit(solution)/shard_map/all_to_all | solution.py:301
  33.7 20.7 %collective-permute-start.3 = (bf16[2,2,128,256]{3,2,1,0:T(8,128)(2,1)S(1)}, bf16[2,2,128,256]{3,2,1,0:T(8,128)(2,1)}, u32[]{:S(2)}, u32[]{:S(2)}) collective-permute-start(bf16[2,2,128,256]{3,2,1,0:T(8,128)(2,1)S(1)} %pad_maximum_fusion.refs_0_), channel_id=1, source_target_pairs={{0,2},{1,3},{2,4},{3,5},{4,6},{5,7},{6,0},{7,1},{8,10},{9,11},{10,... | collective-permute-start | bytes 786440 | tf_op jit(solution)/shard_map/ppermute | solution.py:319
  35.3 19.1 %collective-permute-start.4 = (bf16[2,2,128,256]{3,2,1,0:T(8,128)(2,1)S(1)}, bf16[2,2,128,256]{3,2,1,0:T(8,128)(2,1)}, u32[]{:S(2)}, u32[]{:S(2)}) collective-permute-start(bf16[2,2,128,256]{3,2,1,0:T(8,128)(2,1)S(1)} %pad_maximum_fusion.refs_0_), channel_id=1, source_target_pairs={{0,6},{1,7},{2,0},{3,1},{4,2},{5,3},{6,4},{7,5},{8,14},{9,15},{10,... | collective-permute-start | bytes 786440 | tf_op jit(solution)/shard_map/ppermute | solution.py:319
  37.0 35.8 %collective-permute-start.2 = (bf16[4,384,256]{2,1,0:T(8,128)(2,1)}, bf16[4,384,256]{2,1,0:T(8,128)(2,1)}, u32[]{:S(2)}, u32[]{:S(2)}) collective-permute-start(bf16[4,384,256]{2,1,0:T(8,128)(2,1)} %get-tuple-element.28), channel_id=1, source_target_pairs={{0,2},{1,3},{2,4},{3,5},{4,6},{5,7},{8,10},{9,11},{10,12},{11,13},... | collective-permute-start | bytes 2359304 | tf_op jit(solution)/shard_map/ppermute | solution.py:344
  40.5 32.4 %collective-permute-start.6 = (bf16[4,384,256]{2,1,0:T(8,128)(2,1)}, bf16[4,384,256]{2,1,0:T(8,128)(2,1)}, u32[]{:S(2)}, u32[]{:S(2)}) collective-permute-start(bf16[4,384,256]{2,1,0:T(8,128)(2,1)} %get-tuple-element.27), channel_id=1, source_target_pairs={{2,0},{3,1},{4,2},{5,3},{6,4},{7,5},{10,8},{11,9},{12,10},{13,11},... | collective-permute-start | bytes 2359304 | tf_op jit(solution)/shard_map/ppermute | solution.py:344
  54.4 6.0 %copy-start.1 = (bf16[2,2,128,256]{3,2,1,0:T(8,128)(2,1)S(1)}, bf16[2,2,128,256]{3,2,1,0:T(8,128)(2,1)}, u32[]{:S(2)}) copy-start(bf16[2,2,128,256]{3,2,1,0:T(8,128)(2,1)} %copy-done) | copy-start | bytes 786436
  54.5 18.3 %collective-permute-start.5 = (bf16[4,128,256]{2,1,0:T(8,128)(2,1)S(1)}, bf16[4,128,256]{2,1,0:T(8,128)(2,1)S(1)}, u32[]{:S(2)}, u32[]{:S(2)}) collective-permute-start(bf16[4,128,256]{2,1,0:T(8,128)(2,1)S(1)} %get-tuple-element.30), channel_id=1, source_target_pairs={{0,2},{1,3},{2,4},{3,5},{4,6},{5,7},{8,10},{9,11},{10,12},{11,13},... | collective-permute-start | bytes 786440 | tf_op jit(solution)/shard_map/ppermute | solution.py:347
  58.0 14.8 %collective-permute-start.7 = (bf16[4,128,256]{2,1,0:T(8,128)(2,1)S(1)}, bf16[4,128,256]{2,1,0:T(8,128)(2,1)S(1)}, u32[]{:S(2)}, u32[]{:S(2)}) collective-permute-start(bf16[4,128,256]{2,1,0:T(8,128)(2,1)S(1)} %get-tuple-element.29), channel_id=1, source_target_pairs={{2,0},{3,1},{4,2},{5,3},{6,4},{7,5},{10,8},{11,9},{12,10},{13,11},... | collective-permute-start | bytes 786440 | tf_op jit(solution)/shard_map/ppermute | solution.py:348

commit v5 on v4

--- a/solution.py
+++ b/solution.py
@@ -63,7 +63,15 @@
 
 
 def attend_near(pad, rows_in_band, q_all, own_all, own_rest, *refs):
-    far_all, acc_ref, stat_ref = refs[:-2], refs[-2], refs[-1]
+    planes = len(refs) // 2 - 1
+    far_out, (acc_ref, stat_ref) = refs[:planes], refs[planes : planes + 2]
+    far_all, sem = refs[planes + 2 : -1], refs[-1]
+    copies = [
+        pltpu.make_async_copy(source, target, sem.at[n])
+        for n, (source, target) in enumerate(zip(far_out, far_all))
+    ]
+    for copy in copies:
+        copy.start()
     heads, _, rows, tile, _ = acc_ref.shape
     key_rows = own_all.shape[1] * rows_in_band
     lane = lax.broadcasted_iota(jnp.int32, (tile, tile), 1)
@@ -81,17 +89,25 @@
             band = first // rows_in_band
             tiles = [(sub, x) for sub in range(rows_in_band) for x in range(2)]
             qs = [qs_of[x].query(band, sub) for sub, x in tiles]
+            windows, nears = [], []
+            for sub in range(rows_in_band):
+                at = [(a, first + sub + pad + a - 1) for a in range(3)]
+                at = [(a, j // rows_in_band, j % rows_in_band) for a, j in at if 0 <= j < key_rows]
+                window = [(a, kb, ks, x) for a, kb, ks in at for x in range(2)]
+                windows.append(window)
+                nears.append(
+                    scores(
+                        jnp.concatenate(qs[2 * sub : 2 * sub + 2], 0),
+                        jnp.concatenate([own[x].key(kb, ks) for _, kb, ks, x in window], 0),
+                    )
+                )
+            if h == 0 and first == 0:
+                for copy in copies:
+                    copy.wait()
             far = scores(jnp.concatenate(qs, 0), jnp.concatenate([f[0] for f in shards], 0))
             far_powers, near_sums = [], []
             for sub in range(rows_in_band):
-                i = first + sub
-                at = [(a, i + pad + a - 1) for a in range(3)]
-                at = [(a, j // rows_in_band, j % rows_in_band) for a, j in at if 0 <= j < key_rows]
-                window = [(a, kb, ks, x) for a, kb, ks in at for x in range(2)]
-                near = scores(
-                    jnp.concatenate(qs[2 * sub : 2 * sub + 2], 0),
-                    jnp.concatenate([own[x].key(kb, ks) for _, kb, ks, x in window], 0),
-                )
+                i, window, near = first + sub, windows[sub], nears[sub]
                 near_powers = []
                 for xq in range(2):
                     mine = slice((2 * sub + xq) * tile, (2 * sub + xq + 1) * tile)
@@ -338,7 +354,7 @@
         parts,
         2 * rows - cut + NOTE_ROWS,
     )
-    sent, far[2] = lax.optimization_barrier((sent, far[2]))
+    sent, far[1], far[2] = lax.optimization_barrier((sent, far[1], far[2]))
     q = exchange(sent).reshape(2, band, 2 * rows - cut + NOTE_ROWS, part)
     right_going, left_going = moves(ncol, 2), moves(ncol, -2)
     left, right = lax.ppermute(own[1], "col", right_going), lax.ppermute(own[0], "col", left_going)
@@ -367,6 +383,8 @@
         (q, own, own_rest, *far),
         (acc, stat),
         heads * 2 * count * (6 + 2 * planes),
+        [VMEM] * 3 + [pl.BlockSpec(memory_space=pl.ANY)] * planes,
+        [pltpu.VMEM(a.shape, a.dtype) for a in far] + [pltpu.SemaphoreType.DMA((planes,))],
     )
     sides = (left, left_rest, right, right_rest)
     out = call(

time: 97.3 us -> 95.7 us (0.984); the launches traced: 95.4 us -> 94.8 us
  starting transfers between devices: 26.2 us -> 28.3 us
  waiting for transfers between devices: 24.9 us -> 22.9 us
  Pallas kernels: 24 us -> 22.6 us
    all_to_all x2, waiting for transfers between devices: 15.6 us -> 9.82 us  [exchange(): return lax.all_to_all(a, axes, 0, 0, axis_index_groups=groups, tiled=True)]
    ppermute x3, waiting for transfers between devices: 8.28 us -> 12 us  [body(): lax.ppermute(pair, 'col', [(c, (c + 2 * d) % ncol) for c in range(ncol)])]
    ppermute x1, starting transfers between devices: 3.23 us -> 4.8 us  [body(): lax.ppermute(own[0], 'col', left_going)]
    ppermute x1, starting transfers between devices: 3.47 us -> 1.91 us  [body(): lax.ppermute(own[1], 'col', right_going)]
    pallas_call x3, Pallas kernels: 17.8 us -> 16.4 us  [call(): pl.pallas_call(kernel, in_specs=specs or [VMEM] * len(operands), out_spec...]
    ppermute x3, starting transfers between devices: 4.73 us -> 6.09 us  [body(): lax.ppermute(pair, 'col', [(c, (c + 2 * d) % ncol) for c in range(ncol)])]
  transfers between devices with their start and end apart: 10 -> 10, of which waited for: 4 -> 5; matrix products, arithmetic and copies ran while one was open for 1% -> 1% of each run, Pallas kernels for 19% -> 18%
where the time goes in v5:
time: 95.7 us; the launch traced here: 94.8 us
  starting transfers between devices  28.3 us (30%)
  waiting for transfers between devices  22.9 us (24%)
  Pallas kernels  22.6 us (24%)
  blocking collectives  17.1 us (18%)
  local copies, waits for them, and re-layouts  3.69 us (4%)
    all_to_all x1, blocking collectives, exchange(): return lax.all_to_all(a, axes, 0, 0, axis_index_groups=groups, tiled=True)  17.1 us
    pallas_call x3, Pallas kernels, call(): pl.pallas_call(kernel, in_specs=specs or [VMEM] * len(operands), out_spec...  16.4 us
    ppermute x3, waiting for transfers between devices, body(): lax.ppermute(pair, 'col', [(c, (c + 2 * d) % ncol) for c in range(ncol)])  12 us
    all_to_all x2, waiting for transfers between devices, exchange(): return lax.all_to_all(a, axes, 0, 0, axis_index_groups=groups, tiled=True)  9.82 us
    all_to_all x2, starting transfers between devices, exchange(): return lax.all_to_all(a, axes, 0, 0, axis_index_groups=groups, tiled=True)  7.35 us
    pallas_call x2, Pallas kernels, packed(): pl.pallas_call(kernel, in_specs=[pl.BlockSpec(memory_space=pltpu.SMEM)] *...  6.16 us
    ppermute x3, starting transfers between devices, body(): lax.ppermute(pair, 'col', [(c, (c + 2 * d) % ncol) for c in range(ncol)])  6.09 us
    ppermute x1, starting transfers between devices, body(): lax.ppermute(own[0], 'col', left_going)  4.8 us
  transfers between devices with their start and end apart: 10, of which 5 were waited for; matrix products, arithmetic and copies ran while one was open for 1% of the time, Pallas kernels for 18%

profile of v5, /device:TPU:8, one launch (start us, length us, event | category | flops | bytes accessed | tf_op | source)
XLA Modules:
  0.0 94.8 jit_solution(17689890446842600259)
XLA Ops:
  0.0 1.0 %dynamic-slice_bitcast_fusion.2 = (bf16[1,128,256]{2,1,0:T(8,128)(2,1)S(1)}, bf16[1,128,256]{2,1,0:T(8,128)(2,1)S(1)}, bf16[1,128,256]{2,1,0:T(8,128)(2,1)S(1)}, bf16[1,128,256]{2,1,0:T(8,128)(2,1)S(1)}) fusion(bf16[128,2048]{1,0:T(8,128)(2,1)} %param.11, s32[]{:T(128)S(6)} %select_n.21, s32[]{:T(128)S(6)} %select_n.22, bf16[128,2048]{1,0:T(8,128)(2,1)} %param.10), kind=kLoop, calls=%fused_computation.7 | loop fusion | bytes 524296 | tf_op jit(solution)/shard_map/stack | solution.py:321
  1.0 1.6 %collective-permute-start = (bf16[2,128,256]{2,1,0:T(8,128)(2,1)S(1)}, bf16[2,128,256]{2,1,0:T(8,128)(2,1)S(1)}, u32[]{:S(2)}, u32[]{:S(2)}) collective-permute-start(bf16[2,128,256]{2,1,0:T(8,128)(2,1)S(1)} %pad_maximum_fusion.1), channel_id=1, source_target_pairs={{0,1},{1,0},{2,3},{3,2},{4,5},{5,4},{6,7},{7,6},{8,9},{9,8},{10,11... | collective-permute-start | bytes 393224 | tf_op jit(solution)/shard_map/ppermute | solution.py:326
  2.5 2.7 %pack_first.1 = bf16[8,384,256]{2,1,0:T(8,128)(2,1)} custom-call(bf16[256,2048]{1,0:T(8,128)(2,1)} %bitcast.32, bf16[256,2048]{1,0:T(8,128)(2,1)} %bitcast.30), custom_call_target="tpu_custom_call" | custom-call | bytes 3145728 | tf_op jit(solution)/shard_map/pack_first/pallas_call | solution.py:273
  5.2 1.1 %collective-permute-done = bf16[2,128,256]{2,1,0:T(8,128)(2,1)S(1)} collective-permute-done((bf16[2,128,256]{2,1,0:T(8,128)(2,1)S(1)}, bf16[2,128,256]{2,1,0:T(8,128)(2,1)S(1)}, u32[]{:S(2)}, u32[]{:S(2)}) %collective-permute-start) | collective-permute-done | bytes 131104 | tf_op jit(solution)/shard_map/ppermute | solution.py:326
  6.3 3.7 %all-to-all-start.1 = ((bf16[8,384,256]{2,1,0:T(8,128)(2,1)}), bf16[8,384,256]{2,1,0:T(8,128)(2,1)S(1)}, u32[]{:S(2)}, u32[]{:S(2)}) async-start(bf16[8,384,256]{2,1,0:T(8,128)(2,1)} %pack_first.1), calls=%async_computation.1 | async-start | bytes 3145728 | tf_op jit(solution)/shard_map/all_to_all | solution.py:317
  10.1 1.6 %collective-permute-start.1 = (bf16[2,2,128,256]{3,2,1,0:T(8,128)(2,1)S(1)}, bf16[2,2,128,256]{3,2,1,0:T(8,128)(2,1)S(1)}, u32[]{:S(2)}, u32[]{:S(2)}) collective-permute-start(bf16[2,2,128,256]{3,2,1,0:T(8,128)(2,1)S(1)} %pad_maximum_fusion.refs_0_), channel_id=1, source_target_pairs={{0,2},{1,3},{2,4},{3,5},{4,6},{5,7},{6,0},{7,1},{8,10},{9,11},{10,... | collective-permute-start | bytes 786440 | tf_op jit(solution)/shard_map/ppermute | solution.py:335
  11.7 1.2 %collective-permute-start.2 = (bf16[2,2,128,256]{3,2,1,0:T(8,128)(2,1)S(1)}, bf16[2,2,128,256]{3,2,1,0:T(8,128)(2,1)S(1)}, u32[]{:S(2)}, u32[]{:S(2)}) collective-permute-start(bf16[2,2,128,256]{3,2,1,0:T(8,128)(2,1)S(1)} %pad_maximum_fusion.refs_0_), channel_id=1, source_target_pairs={{0,4},{1,5},{2,6},{3,7},{4,0},{5,1},{6,2},{7,3},{8,12},{9,13},{10,... | collective-permute-start | bytes 786440 | tf_op jit(solution)/shard_map/ppermute | solution.py:335
  12.9 3.5 %pack_second.1 = bf16[8,400,256]{2,1,0:T(8,128)(2,1)} custom-call(s32[2,1,9]{2,1,0:T(1,128)} %flags_ref.1, bf16[256,2048]{1,0:T(8,128)(2,1)} %bitcast.31, bf16[256,2048]{1,0:T(8,128)(2,1)} %bitcast.33), custom_call_target="tpu_custom_call" | custom-call | bytes 3145728 | tf_op jit(solution)/shard_map/pack_second/pallas_call | solution.py:273
  16.4 7.4 %collective-permute-done.1.refs_1_ = bf16[2,2,128,256]{3,2,1,0:T(8,128)(2,1)S(1)} collective-permute-done((bf16[2,2,128,256]{3,2,1,0:T(8,128)(2,1)S(1)}, bf16[2,2,128,256]{3,2,1,0:T(8,128)(2,1)S(1)}, u32[]{:S(2)}, u32[]{:S(2)}) %collective-permute-start.1) | collective-permute-done | bytes 262176 | tf_op jit(solution)/shard_map/ppermute | solution.py:335
  23.8 0.0 copy-start
  23.8 0.7 copy-done
  24.5 4.7 %collective-permute-done.2.refs_2_ = bf16[2,2,128,256]{3,2,1,0:T(8,128)(2,1)S(1)} collective-permute-done((bf16[2,2,128,256]{3,2,1,0:T(8,128)(2,1)S(1)}, bf16[2,2,128,256]{3,2,1,0:T(8,128)(2,1)S(1)}, u32[]{:S(2)}, u32[]{:S(2)}) %collective-permute-start.2) | collective-permute-done | bytes 262176 | tf_op jit(solution)/shard_map/ppermute | solution.py:335
  29.2 0.0 copy-start.2
  29.2 0.7 copy-done.2
  29.9 0.2 all-to-all-done.1
  30.1 3.6 %all-to-all-start = ((bf16[8,400,256]{2,1,0:T(8,128)(2,1)}), bf16[8,400,256]{2,1,0:T(8,128)(2,1)S(1)}, u32[]{:S(2)}, u32[]{:S(2)}) async-start(bf16[8,400,256]{2,1,0:T(8,128)(2,1)} %pack_second.1), calls=%async_computation | async-start | bytes 3276800 | tf_op jit(solution)/shard_map/all_to_all | solution.py:317
  33.7 3.2 %collective-permute-start.4 = (bf16[2,2,128,256]{3,2,1,0:T(8,128)(2,1)S(1)}, bf16[2,2,128,256]{3,2,1,0:T(8,128)(2,1)}, u32[]{:S(2)}, u32[]{:S(2)}) collective-permute-start(bf16[2,2,128,256]{3,2,1,0:T(8,128)(2,1)S(1)} %pad_maximum_fusion.refs_0_), channel_id=1, source_target_pairs={{0,6},{1,7},{2,0},{3,1},{4,2},{5,3},{6,4},{7,5},{8,14},{9,15},{10,... | collective-permute-start | bytes 786440 | tf_op jit(solution)/shard_map/ppermute | solution.py:335
  36.9 1.2 %fusion = (bf16[4,384,256]{2,1,0:T(8,128)(2,1)}, bf16[4,384,256]{2,1,0:T(8,128)(2,1)}) fusion(bf16[8,384,256]{2,1,0:T(8,128)(2,1)S(1)} %all-to-all-done.1), kind=kLoop, calls=%fused_computation.9 | loop fusion | bytes 3145728 | tf_op jit(solution)/shard_map/slice | solution.py:360
  38.2 1.9 %collective-permute-start.3 = (bf16[4,384,256]{2,1,0:T(8,128)(2,1)}, bf16[4,384,256]{2,1,0:T(8,128)(2,1)}, u32[]{:S(2)}, u32[]{:S(2)}) collective-permute-start(bf16[4,384,256]{2,1,0:T(8,128)(2,1)} %get-tuple-element.30), channel_id=1, source_target_pairs={{0,2},{1,3},{2,4},{3,5},{4,6},{5,7},{8,10},{9,11},{10,12},{11,13},... | collective-permute-start | bytes 2359304 | tf_op jit(solution)/shard_map/ppermute | solution.py:360
  40.1 4.8 %collective-permute-start.6 = (bf16[4,384,256]{2,1,0:T(8,128)(2,1)}, bf16[4,384,256]{2,1,0:T(8,128)(2,1)}, u32[]{:S(2)}, u32[]{:S(2)}) collective-permute-start(bf16[4,384,256]{2,1,0:T(8,128)(2,1)} %get-tuple-element.29), channel_id=1, source_target_pairs={{2,0},{3,1},{4,2},{5,3},{6,4},{7,5},{10,8},{11,9},{12,10},{13,11},... | collective-permute-start | bytes 2359304 | tf_op jit(solution)/shard_map/ppermute | solution.py:360
  44.9 9.6 %all-to-all-done = bf16[8,400,256]{2,1,0:T(8,128)(2,1)S(1)} async-done(((bf16[8,400,256]{2,1,0:T(8,128)(2,1)}), bf16[8,400,256]{2,1,0:T(8,128)(2,1)S(1)}, u32[]{:S(2)}, u32[]{:S(2)}) %all-to-all-start) | async-done | bytes 1638432 | tf_op jit(solution)/shard_map/all_to_all | solution.py:317
  54.5 0.0 copy-start.1
  54.5 0.0 copy-start.3
  54.5 0.0 collective-permute-done.4.refs_3_
  54.6 3.5 %collective-permute-start.5 = (bf16[4,128,256]{2,1,0:T(8,128)(2,1)S(1)}, bf16[4,128,256]{2,1,0:T(8,128)(2,1)S(1)}, u32[]{:S(2)}, u32[]{:S(2)}) collective-permute-start(bf16[4,128,256]{2,1,0:T(8,128)(2,1)S(1)} %get-tuple-element.32), channel_id=1, source_target_pairs={{0,2},{1,3},{2,4},{3,5},{4,6},{5,7},{8,10},{9,11},{10,12},{11,13},... | collective-permute-start | bytes 786440 | tf_op jit(solution)/shard_map/ppermute | solution.py:363
  58.1 3.1 %collective-permute-start.7 = (bf16[4,128,256]{2,1,0:T(8,128)(2,1)S(1)}, bf16[4,128,256]{2,1,0:T(8,128)(2,1)S(1)}, u32[]{:S(2)}, u32[]{:S(2)}) collective-permute-start(bf16[4,128,256]{2,1,0:T(8,128)(2,1)S(1)} %get-tuple-element.31), channel_id=1, source_target_pairs={{2,0},{3,1},{4,2},{5,3},{6,4},{7,5},{10,8},{11,9},{12,10},{13,11},... | collective-permute-start | bytes 786440 | tf_op jit(solution)/shard_map/ppermute | solution.py:364
  61.2 0.0 copy-done.1
  61.2 0.0 copy-done.3
  61.2 11.0 %attend_near.1 = (f32[2,2,8,128,128]{4,3,2,1,0:T(8,128)S(1)}, f32[2,128,128]{2,1,0:T(8,128)S(1)}) custom-call(bf16[2,4,400,256]{3,2,1,0:T(8,128)(2,1)S(1)} %bitcast.25, bf16[2,4,384,256]{3,2,1,0:T(8,128)(2,1)S(1)} %bitcast.28, bf16[2,4,400,256]{3,2,1,0:T(8,128)(2,1)S(1)} %bitcast.26, bf16[2,2,128,256]{3,2,1,0:T(8,128)(2,1)S(1)} %pad_maximum_fusion.refs_0_, ...), custom_call_target="tpu_custom_call" | custom-call | flops 3758096384 | bytes 4194304 | tf_op jit(solution)/shard_map/attend_near/pallas_call | solution.py:210
  72.2 0.0 collective-permute-done.5.refs_1_
  72.3 0.0 collective-permute-done.7.refs_3_
  72.3 0.0 collective-permute-done.3.refs_0_
  72.3 0.0 collective-permute-done.6.refs_2_
  72.3 4.3 %attend_sides.1 = bf16[2,4,256,256]{3,2,1,0:T(8,128)(2,1)S(1)} custom-call(bf16[2,4,400,256]{3,2,1,0:T(8,128)(2,1)S(1)} %bitcast.27, bf16[4,384,256]{2,1,0:T(8,128)(2,1)} %collective-permute-done.3.refs_0_, bf16[4,128,256]{2,1,0:T(8,128)(2,1)S(1)} %collective-permute-done.5.refs_1_, bf16[4,384,256]{2,1,0:T(8,128)(2,1)} %collective-permute-done.6.refs_2_, ...), custom_call_target="tpu_custom_call" | custom-call | flops 805306368 | bytes 4194304 | tf_op jit(solution)/shard_map/attend_sides/pallas_call | solution.py:210
  76.6 17.1 %all_to_all.15.got_ref = bf16[8,256,256]{2,1,0:T(8,128)(2,1)S(1)} all-to-all(bf16[8,256,256]{2,1,0:T(8,128)(2,1)S(1)} %bitcast.29), channel_id=1, replica_groups={{0,8,16,24,1,9,17,25},{2,10,18,26,3,11,19,27},{4,12,20,28,5,13,21,29},{..., dimensions={0} | all-to-all | bytes 2097152 | tf_op jit(solution)/shard_map/all_to_all | solution.py:317
  93.7 1.1 %unpack.1 = bf16[256,2048]{1,0:T(8,128)(2,1)} custom-call(bf16[8,256,256]{2,1,0:T(8,128)(2,1)S(1)} %all_to_all.15.got_ref), custom_call_target="tpu_custom_call" | custom-call | bytes 4194304 | tf_op jit(solution)/shard_map/unpack/pallas_call | solution.py:210
  (5 shorter events, 0.1 us)
Async XLA Ops:
  1.0 5.3 %collective-permute-start = (bf16[2,128,256]{2,1,0:T(8,128)(2,1)S(1)}, bf16[2,128,256]{2,1,0:T(8,128)(2,1)S(1)}, u32[]{:S(2)}, u32[]{:S(2)}) collective-permute-start(bf16[2,128,256]{2,1,0:T(8,128)(2,1)S(1)} %pad_maximum_fusion.1), channel_id=1, source_target_pairs={{0,1},{1,0},{2,3},{3,2},{4,5},{5,4},{6,7},{7,6},{8,9},{9,8},{10,11... | collective-permute-start | bytes 393224 | tf_op jit(solution)/shard_map/ppermute | solution.py:326
  6.3 23.8 %all-to-all-start.1 = ((bf16[8,384,256]{2,1,0:T(8,128)(2,1)}), bf16[8,384,256]{2,1,0:T(8,128)(2,1)S(1)}, u32[]{:S(2)}, u32[]{:S(2)}) async-start(bf16[8,384,256]{2,1,0:T(8,128)(2,1)} %pack_first.1), calls=%async_computation.1 | async-start | bytes 3145728 | tf_op jit(solution)/shard_map/all_to_all | solution.py:317
  10.1 13.7 %collective-permute-start.1 = (bf16[2,2,128,256]{3,2,1,0:T(8,128)(2,1)S(1)}, bf16[2,2,128,256]{3,2,1,0:T(8,128)(2,1)S(1)}, u32[]{:S(2)}, u32[]{:S(2)}) collective-permute-start(bf16[2,2,128,256]{3,2,1,0:T(8,128)(2,1)S(1)} %pad_maximum_fusion.refs_0_), channel_id=1, source_target_pairs={{0,2},{1,3},{2,4},{3,5},{4,6},{5,7},{6,0},{7,1},{8,10},{9,11},{10,... | collective-permute-start | bytes 786440 | tf_op jit(solution)/shard_map/ppermute | solution.py:335
  11.7 17.5 %collective-permute-start.2 = (bf16[2,2,128,256]{3,2,1,0:T(8,128)(2,1)S(1)}, bf16[2,2,128,256]{3,2,1,0:T(8,128)(2,1)S(1)}, u32[]{:S(2)}, u32[]{:S(2)}) collective-permute-start(bf16[2,2,128,256]{3,2,1,0:T(8,128)(2,1)S(1)} %pad_maximum_fusion.refs_0_), channel_id=1, source_target_pairs={{0,4},{1,5},{2,6},{3,7},{4,0},{5,1},{6,2},{7,3},{8,12},{9,13},{10,... | collective-permute-start | bytes 786440 | tf_op jit(solution)/shard_map/ppermute | solution.py:335
  23.8 0.7 copy-start
  29.2 0.7 copy-start.2
  30.1 24.4 %all-to-all-start = ((bf16[8,400,256]{2,1,0:T(8,128)(2,1)}), bf16[8,400,256]{2,1,0:T(8,128)(2,1)S(1)}, u32[]{:S(2)}, u32[]{:S(2)}) async-start(bf16[8,400,256]{2,1,0:T(8,128)(2,1)} %pack_second.1), calls=%async_computation | async-start | bytes 3276800 | tf_op jit(solution)/shard_map/all_to_all | solution.py:317
  33.7 20.8 %collective-permute-start.4 = (bf16[2,2,128,256]{3,2,1,0:T(8,128)(2,1)S(1)}, bf16[2,2,128,256]{3,2,1,0:T(8,128)(2,1)}, u32[]{:S(2)}, u32[]{:S(2)}) collective-permute-start(bf16[2,2,128,256]{3,2,1,0:T(8,128)(2,1)S(1)} %pad_maximum_fusion.refs_0_), channel_id=1, source_target_pairs={{0,6},{1,7},{2,0},{3,1},{4,2},{5,3},{6,4},{7,5},{8,14},{9,15},{10,... | collective-permute-start | bytes 786440 | tf_op jit(solution)/shard_map/ppermute | solution.py:335
  38.2 34.1 %collective-permute-start.3 = (bf16[4,384,256]{2,1,0:T(8,128)(2,1)}, bf16[4,384,256]{2,1,0:T(8,128)(2,1)}, u32[]{:S(2)}, u32[]{:S(2)}) collective-permute-start(bf16[4,384,256]{2,1,0:T(8,128)(2,1)} %get-tuple-element.30), channel_id=1, source_target_pairs={{0,2},{1,3},{2,4},{3,5},{4,6},{5,7},{8,10},{9,11},{10,12},{11,13},... | collective-permute-start | bytes 2359304 | tf_op jit(solution)/shard_map/ppermute | solution.py:360
  40.1 32.2 %collective-permute-start.6 = (bf16[4,384,256]{2,1,0:T(8,128)(2,1)}, bf16[4,384,256]{2,1,0:T(8,128)(2,1)}, u32[]{:S(2)}, u32[]{:S(2)}) collective-permute-start(bf16[4,384,256]{2,1,0:T(8,128)(2,1)} %get-tuple-element.29), channel_id=1, source_target_pairs={{2,0},{3,1},{4,2},{5,3},{6,4},{7,5},{10,8},{11,9},{12,10},{13,11},... | collective-permute-start | bytes 2359304 | tf_op jit(solution)/shard_map/ppermute | solution.py:360
  54.5 6.7 %copy-start.1 = (bf16[2,2,128,256]{3,2,1,0:T(8,128)(2,1)S(1)}, bf16[2,2,128,256]{3,2,1,0:T(8,128)(2,1)}, u32[]{:S(2)}) copy-start(bf16[2,2,128,256]{3,2,1,0:T(8,128)(2,1)} %copy-done) | copy-start | bytes 786436
  54.5 6.7 %copy-start.3 = (bf16[2,2,128,256]{3,2,1,0:T(8,128)(2,1)S(1)}, bf16[2,2,128,256]{3,2,1,0:T(8,128)(2,1)}, u32[]{:S(2)}) copy-start(bf16[2,2,128,256]{3,2,1,0:T(8,128)(2,1)} %copy-done.2) | copy-start | bytes 786436
  54.6 17.7 %collective-permute-start.5 = (bf16[4,128,256]{2,1,0:T(8,128)(2,1)S(1)}, bf16[4,128,256]{2,1,0:T(8,128)(2,1)S(1)}, u32[]{:S(2)}, u32[]{:S(2)}) collective-permute-start(bf16[4,128,256]{2,1,0:T(8,128)(2,1)S(1)} %get-tuple-element.32), channel_id=1, source_target_pairs={{0,2},{1,3},{2,4},{3,5},{4,6},{5,7},{8,10},{9,11},{10,12},{11,13},... | collective-permute-start | bytes 786440 | tf_op jit(solution)/shard_map/ppermute | solution.py:363
  58.1 14.2 %collective-permute-start.7 = (bf16[4,128,256]{2,1,0:T(8,128)(2,1)S(1)}, bf16[4,128,256]{2,1,0:T(8,128)(2,1)S(1)}, u32[]{:S(2)}, u32[]{:S(2)}) collective-permute-start(bf16[4,128,256]{2,1,0:T(8,128)(2,1)S(1)} %get-tuple-element.31), channel_id=1, source_target_pairs={{2,0},{3,1},{4,2},{5,3},{6,4},{7,5},{10,8},{11,9},{12,10},{13,11},... | collective-permute-start | bytes 786440 | tf_op jit(solution)/shard_map/ppermute | solution.py:364

commit v6 on v5

--- a/solution.py
+++ b/solution.py
@@ -223,11 +223,12 @@
 
 def start_pack(pieces, out_ref, sem):
     part, copies, at = out_ref.shape[-1], [], 0
+    base = pl.program_id(0) * out_ref.shape[0]
     for n, (ref, first, end) in enumerate(pieces):
         for p in range(out_ref.shape[0]):
             copies.append(
                 pltpu.make_async_copy(
-                    ref.at[first:end, p * part : (p + 1) * part],
+                    ref.at[first:end, pl.ds(pl.multiple_of((base + p) * part, part), part)],
                     out_ref.at[p, at : at + end - first],
                     sem.at[n * out_ref.shape[0] + p],
                 )
@@ -274,7 +275,8 @@
         kernel,
         in_specs=[pl.BlockSpec(memory_space=pltpu.SMEM)] * len(small)
         + [pl.BlockSpec(memory_space=pltpu.HBM)] * len(arrays),
-        out_specs=VMEM,
+        grid=(2,),
+        out_specs=pl.BlockSpec((parts // 2, rows, width // parts), lambda s: (s, 0, 0)),
         out_shape=jax.ShapeDtypeStruct(
             (parts, rows, width // parts), arrays[0].dtype
         ),

time: 95.7 us -> 95.8 us (level)
  Pallas kernels: 22.6 us -> 24.6 us
  waiting for transfers between devices: 22.9 us -> 20.9 us
    pallas_call x2, Pallas kernels: 6.16 us -> 8.13 us  [packed(): pl.pallas_call(kernel, in_specs=[pl.BlockSpec(memory_space=pltpu.SMEM)] *...]
    ppermute x3, waiting for transfers between devices: 12 us -> 11 us  [body(): lax.ppermute(pair, 'col', [(c, (c + 2 * d) % ncol) for c in range(ncol)])]
  transfers between devices with their start and end apart: 10 -> 10, of which waited for: 5 -> 5; matrix products, arithmetic and copies ran while one was open for 1% -> 1% of each run, Pallas kernels for 18% -> 20%
where the time goes in v6:
time: 95.8 us; the launch traced here: 94.8 us
  starting transfers between devices  28.3 us (30%)
  Pallas kernels  24.6 us (26%)
  waiting for transfers between devices  20.9 us (22%)
  blocking collectives  17.1 us (18%)
  local copies, waits for them, and re-layouts  3.69 us (4%)
    all_to_all x1, blocking collectives, exchange(): return lax.all_to_all(a, axes, 0, 0, axis_index_groups=groups, tiled=True)  17.1 us
    pallas_call x3, Pallas kernels, call(): pl.pallas_call(kernel, in_specs=specs or [VMEM] * len(operands), out_spec...  16.4 us
    ppermute x3, waiting for transfers between devices, body(): lax.ppermute(pair, 'col', [(c, (c + 2 * d) % ncol) for c in range(ncol)])  11 us
    all_to_all x2, waiting for transfers between devices, exchange(): return lax.all_to_all(a, axes, 0, 0, axis_index_groups=groups, tiled=True)  9.82 us
    pallas_call x2, Pallas kernels, packed(): pl.pallas_call(kernel, in_specs=[pl.BlockSpec(memory_space=pltpu.SMEM)] *...  8.13 us
    all_to_all x2, starting transfers between devices, exchange(): return lax.all_to_all(a, axes, 0, 0, axis_index_groups=groups, tiled=True)  7.35 us
    ppermute x3, starting transfers between devices, body(): lax.ppermute(pair, 'col', [(c, (c + 2 * d) % ncol) for c in range(ncol)])  6.09 us
    ppermute x1, starting transfers between devices, body(): lax.ppermute(own[0], 'col', left_going)  4.8 us
  transfers between devices with their start and end apart: 10, of which 5 were waited for; matrix products, arithmetic and copies ran while one was open for 1% of the time, Pallas kernels for 20%

profile of v6, /device:TPU:8, one launch (start us, length us, event | category | flops | bytes accessed | tf_op | source)
XLA Modules:
  0.0 94.8 jit_solution(2276224080585242048)
XLA Ops:
  0.0 1.0 %dynamic-slice_bitcast_fusion.2 = (bf16[1,128,256]{2,1,0:T(8,128)(2,1)S(1)}, bf16[1,128,256]{2,1,0:T(8,128)(2,1)S(1)}, bf16[1,128,256]{2,1,0:T(8,128)(2,1)S(1)}, bf16[1,128,256]{2,1,0:T(8,128)(2,1)S(1)}) fusion(bf16[128,2048]{1,0:T(8,128)(2,1)} %param.11, s32[]{:T(128)S(6)} %select_n.21, s32[]{:T(128)S(6)} %select_n.22, bf16[128,2048]{1,0:T(8,128)(2,1)} %param.10), kind=kLoop, calls=%fused_computation.7 | loop fusion | bytes 524296 | tf_op jit(solution)/shard_map/stack | solution.py:323
  1.0 1.6 %collective-permute-start = (bf16[2,128,256]{2,1,0:T(8,128)(2,1)S(1)}, bf16[2,128,256]{2,1,0:T(8,128)(2,1)S(1)}, u32[]{:S(2)}, u32[]{:S(2)}) collective-permute-start(bf16[2,128,256]{2,1,0:T(8,128)(2,1)S(1)} %pad_maximum_fusion.1), channel_id=1, source_target_pairs={{0,1},{1,0},{2,3},{3,2},{4,5},{5,4},{6,7},{7,6},{8,9},{9,8},{10,11... | collective-permute-start | bytes 393224 | tf_op jit(solution)/shard_map/ppermute | solution.py:328
  2.5 3.6 %pack_first.1 = bf16[8,384,256]{2,1,0:T(8,128)(2,1)} custom-call(bf16[256,2048]{1,0:T(8,128)(2,1)} %bitcast.32, bf16[256,2048]{1,0:T(8,128)(2,1)} %bitcast.30), custom_call_target="tpu_custom_call" | custom-call | bytes 3145728 | tf_op jit(solution)/shard_map/pack_first/pallas_call | solution.py:274
  6.2 0.1 collective-permute-done
  6.3 3.7 %all-to-all-start.1 = ((bf16[8,384,256]{2,1,0:T(8,128)(2,1)}), bf16[8,384,256]{2,1,0:T(8,128)(2,1)S(1)}, u32[]{:S(2)}, u32[]{:S(2)}) async-start(bf16[8,384,256]{2,1,0:T(8,128)(2,1)} %pack_first.1), calls=%async_computation.1 | async-start | bytes 3145728 | tf_op jit(solution)/shard_map/all_to_all | solution.py:319
  10.1 1.6 %collective-permute-start.1 = (bf16[2,2,128,256]{3,2,1,0:T(8,128)(2,1)S(1)}, bf16[2,2,128,256]{3,2,1,0:T(8,128)(2,1)S(1)}, u32[]{:S(2)}, u32[]{:S(2)}) collective-permute-start(bf16[2,2,128,256]{3,2,1,0:T(8,128)(2,1)S(1)} %pad_maximum_fusion.refs_0_), channel_id=1, source_target_pairs={{0,2},{1,3},{2,4},{3,5},{4,6},{5,7},{6,0},{7,1},{8,10},{9,11},{10,... | collective-permute-start | bytes 786440 | tf_op jit(solution)/shard_map/ppermute | solution.py:337
  11.7 1.2 %collective-permute-start.2 = (bf16[2,2,128,256]{3,2,1,0:T(8,128)(2,1)S(1)}, bf16[2,2,128,256]{3,2,1,0:T(8,128)(2,1)S(1)}, u32[]{:S(2)}, u32[]{:S(2)}) collective-permute-start(bf16[2,2,128,256]{3,2,1,0:T(8,128)(2,1)S(1)} %pad_maximum_fusion.refs_0_), channel_id=1, source_target_pairs={{0,4},{1,5},{2,6},{3,7},{4,0},{5,1},{6,2},{7,3},{8,12},{9,13},{10,... | collective-permute-start | bytes 786440 | tf_op jit(solution)/shard_map/ppermute | solution.py:337
  12.9 4.5 %pack_second.1 = bf16[8,400,256]{2,1,0:T(8,128)(2,1)} custom-call(s32[2,1,9]{2,1,0:T(1,128)} %flags_ref.1, bf16[256,2048]{1,0:T(8,128)(2,1)} %bitcast.31, bf16[256,2048]{1,0:T(8,128)(2,1)} %bitcast.33), custom_call_target="tpu_custom_call" | custom-call | bytes 3145728 | tf_op jit(solution)/shard_map/pack_second/pallas_call | solution.py:274
  17.4 6.3 %collective-permute-done.1.refs_1_ = bf16[2,2,128,256]{3,2,1,0:T(8,128)(2,1)S(1)} collective-permute-done((bf16[2,2,128,256]{3,2,1,0:T(8,128)(2,1)S(1)}, bf16[2,2,128,256]{3,2,1,0:T(8,128)(2,1)S(1)}, u32[]{:S(2)}, u32[]{:S(2)}) %collective-permute-start.1) | collective-permute-done | bytes 262176 | tf_op jit(solution)/shard_map/ppermute | solution.py:337
  23.8 0.0 copy-start
  23.8 0.7 copy-done
  24.5 4.7 %collective-permute-done.2.refs_2_ = bf16[2,2,128,256]{3,2,1,0:T(8,128)(2,1)S(1)} collective-permute-done((bf16[2,2,128,256]{3,2,1,0:T(8,128)(2,1)S(1)}, bf16[2,2,128,256]{3,2,1,0:T(8,128)(2,1)S(1)}, u32[]{:S(2)}, u32[]{:S(2)}) %collective-permute-start.2) | collective-permute-done | bytes 262176 | tf_op jit(solution)/shard_map/ppermute | solution.py:337
  29.2 0.0 copy-start.2
  29.2 0.7 copy-done.2
  29.9 0.2 all-to-all-done.1
  30.1 3.6 %all-to-all-start = ((bf16[8,400,256]{2,1,0:T(8,128)(2,1)}), bf16[8,400,256]{2,1,0:T(8,128)(2,1)S(1)}, u32[]{:S(2)}, u32[]{:S(2)}) async-start(bf16[8,400,256]{2,1,0:T(8,128)(2,1)} %pack_second.1), calls=%async_computation | async-start | bytes 3276800 | tf_op jit(solution)/shard_map/all_to_all | solution.py:319
  33.7 3.2 %collective-permute-start.4 = (bf16[2,2,128,256]{3,2,1,0:T(8,128)(2,1)S(1)}, bf16[2,2,128,256]{3,2,1,0:T(8,128)(2,1)}, u32[]{:S(2)}, u32[]{:S(2)}) collective-permute-start(bf16[2,2,128,256]{3,2,1,0:T(8,128)(2,1)S(1)} %pad_maximum_fusion.refs_0_), channel_id=1, source_target_pairs={{0,6},{1,7},{2,0},{3,1},{4,2},{5,3},{6,4},{7,5},{8,14},{9,15},{10,... | collective-permute-start | bytes 786440 | tf_op jit(solution)/shard_map/ppermute | solution.py:337
  36.9 1.2 %fusion = (bf16[4,384,256]{2,1,0:T(8,128)(2,1)}, bf16[4,384,256]{2,1,0:T(8,128)(2,1)}) fusion(bf16[8,384,256]{2,1,0:T(8,128)(2,1)S(1)} %all-to-all-done.1), kind=kLoop, calls=%fused_computation.9 | loop fusion | bytes 3145728 | tf_op jit(solution)/shard_map/slice | solution.py:362
  38.2 1.9 %collective-permute-start.3 = (bf16[4,384,256]{2,1,0:T(8,128)(2,1)}, bf16[4,384,256]{2,1,0:T(8,128)(2,1)}, u32[]{:S(2)}, u32[]{:S(2)}) collective-permute-start(bf16[4,384,256]{2,1,0:T(8,128)(2,1)} %get-tuple-element.30), channel_id=1, source_target_pairs={{0,2},{1,3},{2,4},{3,5},{4,6},{5,7},{8,10},{9,11},{10,12},{11,13},... | collective-permute-start | bytes 2359304 | tf_op jit(solution)/shard_map/ppermute | solution.py:362
  40.1 4.8 %collective-permute-start.6 = (bf16[4,384,256]{2,1,0:T(8,128)(2,1)}, bf16[4,384,256]{2,1,0:T(8,128)(2,1)}, u32[]{:S(2)}, u32[]{:S(2)}) collective-permute-start(bf16[4,384,256]{2,1,0:T(8,128)(2,1)} %get-tuple-element.29), channel_id=1, source_target_pairs={{2,0},{3,1},{4,2},{5,3},{6,4},{7,5},{10,8},{11,9},{12,10},{13,11},... | collective-permute-start | bytes 2359304 | tf_op jit(solution)/shard_map/ppermute | solution.py:362
  44.9 9.6 %all-to-all-done = bf16[8,400,256]{2,1,0:T(8,128)(2,1)S(1)} async-done(((bf16[8,400,256]{2,1,0:T(8,128)(2,1)}), bf16[8,400,256]{2,1,0:T(8,128)(2,1)S(1)}, u32[]{:S(2)}, u32[]{:S(2)}) %all-to-all-start) | async-done | bytes 1638432 | tf_op jit(solution)/shard_map/all_to_all | solution.py:319
  54.5 0.0 copy-start.1
  54.5 0.0 copy-start.3
  54.5 0.0 collective-permute-done.4.refs_3_
  54.6 3.5 %collective-permute-start.5 = (bf16[4,128,256]{2,1,0:T(8,128)(2,1)S(1)}, bf16[4,128,256]{2,1,0:T(8,128)(2,1)S(1)}, u32[]{:S(2)}, u32[]{:S(2)}) collective-permute-start(bf16[4,128,256]{2,1,0:T(8,128)(2,1)S(1)} %get-tuple-element.32), channel_id=1, source_target_pairs={{0,2},{1,3},{2,4},{3,5},{4,6},{5,7},{8,10},{9,11},{10,12},{11,13},... | collective-permute-start | bytes 786440 | tf_op jit(solution)/shard_map/ppermute | solution.py:365
  58.1 3.1 %collective-permute-start.7 = (bf16[4,128,256]{2,1,0:T(8,128)(2,1)S(1)}, bf16[4,128,256]{2,1,0:T(8,128)(2,1)S(1)}, u32[]{:S(2)}, u32[]{:S(2)}) collective-permute-start(bf16[4,128,256]{2,1,0:T(8,128)(2,1)S(1)} %get-tuple-element.31), channel_id=1, source_target_pairs={{2,0},{3,1},{4,2},{5,3},{6,4},{7,5},{10,8},{11,9},{12,10},{13,11},... | collective-permute-start | bytes 786440 | tf_op jit(solution)/shard_map/ppermute | solution.py:366
  61.2 0.0 copy-done.1
  61.2 0.0 copy-done.3
  61.2 11.0 %attend_near.1 = (f32[2,2,8,128,128]{4,3,2,1,0:T(8,128)S(1)}, f32[2,128,128]{2,1,0:T(8,128)S(1)}) custom-call(bf16[2,4,400,256]{3,2,1,0:T(8,128)(2,1)S(1)} %bitcast.25, bf16[2,4,384,256]{3,2,1,0:T(8,128)(2,1)S(1)} %bitcast.28, bf16[2,4,400,256]{3,2,1,0:T(8,128)(2,1)S(1)} %bitcast.26, bf16[2,2,128,256]{3,2,1,0:T(8,128)(2,1)S(1)} %pad_maximum_fusion.refs_0_, ...), custom_call_target="tpu_custom_call" | custom-call | flops 3758096384 | bytes 4194304 | tf_op jit(solution)/shard_map/attend_near/pallas_call | solution.py:210
  72.2 0.0 collective-permute-done.5.refs_1_
  72.3 0.0 collective-permute-done.7.refs_3_
  72.3 0.0 collective-permute-done.3.refs_0_
  72.3 0.0 collective-permute-done.6.refs_2_
  72.3 4.3 %attend_sides.1 = bf16[2,4,256,256]{3,2,1,0:T(8,128)(2,1)S(1)} custom-call(bf16[2,4,400,256]{3,2,1,0:T(8,128)(2,1)S(1)} %bitcast.27, bf16[4,384,256]{2,1,0:T(8,128)(2,1)} %collective-permute-done.3.refs_0_, bf16[4,128,256]{2,1,0:T(8,128)(2,1)S(1)} %collective-permute-done.5.refs_1_, bf16[4,384,256]{2,1,0:T(8,128)(2,1)} %collective-permute-done.6.refs_2_, ...), custom_call_target="tpu_custom_call" | custom-call | flops 805306368 | bytes 4194304 | tf_op jit(solution)/shard_map/attend_sides/pallas_call | solution.py:210
  76.6 17.1 %all_to_all.15.got_ref = bf16[8,256,256]{2,1,0:T(8,128)(2,1)S(1)} all-to-all(bf16[8,256,256]{2,1,0:T(8,128)(2,1)S(1)} %bitcast.29), channel_id=1, replica_groups={{0,8,16,24,1,9,17,25},{2,10,18,26,3,11,19,27},{4,12,20,28,5,13,21,29},{..., dimensions={0} | all-to-all | bytes 2097152 | tf_op jit(solution)/shard_map/all_to_all | solution.py:319
  93.7 1.1 %unpack.1 = bf16[256,2048]{1,0:T(8,128)(2,1)} custom-call(bf16[8,256,256]{2,1,0:T(8,128)(2,1)S(1)} %all_to_all.15.got_ref), custom_call_target="tpu_custom_call" | custom-call | bytes 4194304 | tf_op jit(solution)/shard_map/unpack/pallas_call | solution.py:210
  (5 shorter events, 0.1 us)
Async XLA Ops:
  1.0 5.3 %collective-permute-start = (bf16[2,128,256]{2,1,0:T(8,128)(2,1)S(1)}, bf16[2,128,256]{2,1,0:T(8,128)(2,1)S(1)}, u32[]{:S(2)}, u32[]{:S(2)}) collective-permute-start(bf16[2,128,256]{2,1,0:T(8,128)(2,1)S(1)} %pad_maximum_fusion.1), channel_id=1, source_target_pairs={{0,1},{1,0},{2,3},{3,2},{4,5},{5,4},{6,7},{7,6},{8,9},{9,8},{10,11... | collective-permute-start | bytes 393224 | tf_op jit(solution)/shard_map/ppermute | solution.py:328
  6.3 23.8 %all-to-all-start.1 = ((bf16[8,384,256]{2,1,0:T(8,128)(2,1)}), bf16[8,384,256]{2,1,0:T(8,128)(2,1)S(1)}, u32[]{:S(2)}, u32[]{:S(2)}) async-start(bf16[8,384,256]{2,1,0:T(8,128)(2,1)} %pack_first.1), calls=%async_computation.1 | async-start | bytes 3145728 | tf_op jit(solution)/shard_map/all_to_all | solution.py:319
  10.1 13.7 %collective-permute-start.1 = (bf16[2,2,128,256]{3,2,1,0:T(8,128)(2,1)S(1)}, bf16[2,2,128,256]{3,2,1,0:T(8,128)(2,1)S(1)}, u32[]{:S(2)}, u32[]{:S(2)}) collective-permute-start(bf16[2,2,128,256]{3,2,1,0:T(8,128)(2,1)S(1)} %pad_maximum_fusion.refs_0_), channel_id=1, source_target_pairs={{0,2},{1,3},{2,4},{3,5},{4,6},{5,7},{6,0},{7,1},{8,10},{9,11},{10,... | collective-permute-start | bytes 786440 | tf_op jit(solution)/shard_map/ppermute | solution.py:337
  11.7 17.5 %collective-permute-start.2 = (bf16[2,2,128,256]{3,2,1,0:T(8,128)(2,1)S(1)}, bf16[2,2,128,256]{3,2,1,0:T(8,128)(2,1)S(1)}, u32[]{:S(2)}, u32[]{:S(2)}) collective-permute-start(bf16[2,2,128,256]{3,2,1,0:T(8,128)(2,1)S(1)} %pad_maximum_fusion.refs_0_), channel_id=1, source_target_pairs={{0,4},{1,5},{2,6},{3,7},{4,0},{5,1},{6,2},{7,3},{8,12},{9,13},{10,... | collective-permute-start | bytes 786440 | tf_op jit(solution)/shard_map/ppermute | solution.py:337
  23.8 0.7 copy-start
  29.2 0.7 copy-start.2
  30.1 24.4 %all-to-all-start = ((bf16[8,400,256]{2,1,0:T(8,128)(2,1)}), bf16[8,400,256]{2,1,0:T(8,128)(2,1)S(1)}, u32[]{:S(2)}, u32[]{:S(2)}) async-start(bf16[8,400,256]{2,1,0:T(8,128)(2,1)} %pack_second.1), calls=%async_computation | async-start | bytes 3276800 | tf_op jit(solution)/shard_map/all_to_all | solution.py:319
  33.7 20.8 %collective-permute-start.4 = (bf16[2,2,128,256]{3,2,1,0:T(8,128)(2,1)S(1)}, bf16[2,2,128,256]{3,2,1,0:T(8,128)(2,1)}, u32[]{:S(2)}, u32[]{:S(2)}) collective-permute-start(bf16[2,2,128,256]{3,2,1,0:T(8,128)(2,1)S(1)} %pad_maximum_fusion.refs_0_), channel_id=1, source_target_pairs={{0,6},{1,7},{2,0},{3,1},{4,2},{5,3},{6,4},{7,5},{8,14},{9,15},{10,... | collective-permute-start | bytes 786440 | tf_op jit(solution)/shard_map/ppermute | solution.py:337
  38.2 34.1 %collective-permute-start.3 = (bf16[4,384,256]{2,1,0:T(8,128)(2,1)}, bf16[4,384,256]{2,1,0:T(8,128)(2,1)}, u32[]{:S(2)}, u32[]{:S(2)}) collective-permute-start(bf16[4,384,256]{2,1,0:T(8,128)(2,1)} %get-tuple-element.30), channel_id=1, source_target_pairs={{0,2},{1,3},{2,4},{3,5},{4,6},{5,7},{8,10},{9,11},{10,12},{11,13},... | collective-permute-start | bytes 2359304 | tf_op jit(solution)/shard_map/ppermute | solution.py:362
  40.1 32.2 %collective-permute-start.6 = (bf16[4,384,256]{2,1,0:T(8,128)(2,1)}, bf16[4,384,256]{2,1,0:T(8,128)(2,1)}, u32[]{:S(2)}, u32[]{:S(2)}) collective-permute-start(bf16[4,384,256]{2,1,0:T(8,128)(2,1)} %get-tuple-element.29), channel_id=1, source_target_pairs={{2,0},{3,1},{4,2},{5,3},{6,4},{7,5},{10,8},{11,9},{12,10},{13,11},... | collective-permute-start | bytes 2359304 | tf_op jit(solution)/shard_map/ppermute | solution.py:362
  54.5 6.7 %copy-start.1 = (bf16[2,2,128,256]{3,2,1,0:T(8,128)(2,1)S(1)}, bf16[2,2,128,256]{3,2,1,0:T(8,128)(2,1)}, u32[]{:S(2)}) copy-start(bf16[2,2,128,256]{3,2,1,0:T(8,128)(2,1)} %copy-done) | copy-start | bytes 786436
  54.5 6.7 %copy-start.3 = (bf16[2,2,128,256]{3,2,1,0:T(8,128)(2,1)S(1)}, bf16[2,2,128,256]{3,2,1,0:T(8,128)(2,1)}, u32[]{:S(2)}) copy-start(bf16[2,2,128,256]{3,2,1,0:T(8,128)(2,1)} %copy-done.2) | copy-start | bytes 786436
  54.6 17.7 %collective-permute-start.5 = (bf16[4,128,256]{2,1,0:T(8,128)(2,1)S(1)}, bf16[4,128,256]{2,1,0:T(8,128)(2,1)S(1)}, u32[]{:S(2)}, u32[]{:S(2)}) collective-permute-start(bf16[4,128,256]{2,1,0:T(8,128)(2,1)S(1)} %get-tuple-element.32), channel_id=1, source_target_pairs={{0,2},{1,3},{2,4},{3,5},{4,6},{5,7},{8,10},{9,11},{10,12},{11,13},... | collective-permute-start | bytes 786440 | tf_op jit(solution)/shard_map/ppermute | solution.py:365
  58.1 14.2 %collective-permute-start.7 = (bf16[4,128,256]{2,1,0:T(8,128)(2,1)S(1)}, bf16[4,128,256]{2,1,0:T(8,128)(2,1)S(1)}, u32[]{:S(2)}, u32[]{:S(2)}) collective-permute-start(bf16[4,128,256]{2,1,0:T(8,128)(2,1)S(1)} %get-tuple-element.31), channel_id=1, source_target_pairs={{2,0},{3,1},{4,2},{5,3},{6,4},{7,5},{10,8},{11,9},{12,10},{13,11},... | collective-permute-start | bytes 786440 | tf_op jit(solution)/shard_map/ppermute | solution.py:366
